TPU v7x, 32 devices: a whole 2x2x4 slice. The times are simulated.
32 devices in a mesh: grp: 2 (over y), pair: 4 (over z), head: 4 (over x, core).
Axes of the slice: x: 2, y: 2, z: 4, core: 2. Of those that a mesh axis runs over, the one named last changes fastest.
Arguments:
- features: bfloat16 [8, 224, 768], P(('grp', 'pair'), None, 'head'), parts along dimension 0, may hold values from -6 to 6
- pair_list: int32 [8, 2], P('grp'), parts along dimension 0, may hold values from 0 to 3, as said below
- gain_self: float32 [768], replicated, may hold values from 0.1 to 1.9
- gain_memory: float32 [768], replicated, may hold values from 0.1 to 1.9
- gain_cross: float32 [768], replicated, may hold values from 0.1 to 1.9
- gain_mlp: float32 [768], replicated, may hold values from 0.1 to 1.9
- w_self_qkv: bfloat16 [3, 768, 512], P(None, None, 'head'), may hold values from -3 to 3, as said below
- w_self_out: bfloat16 [512, 768], P('head'), may hold values from -0.25 to 0.25
- w_cross_qkv: bfloat16 [3, 768, 512], P(None, None, 'head'), may hold values from -3 to 3, as said below
- w_cross_out: bfloat16 [512, 768], P('head'), may hold values from -1 to 1
- w_up: bfloat16 [768, 3072], P(None, 'head'), may hold values from -0.21875 to 0.21875
- w_down: bfloat16 [3072, 768], P('head'), may hold values from -0.109375 to 0.109375
Outputs:
- summed: float32 [8, 224, 768], P(('grp', 'pair'), None, 'head'), parts along dimension 0
There are 2 independent parts, one for each index of `grp`. A program takes and returns all parts, laid end to end along the dimension named above; an argument that names none is the same for every part. Nothing has to cross between parts.
Inputs may be any that keep to these rules, and one draw needn't show every extreme that they name: `pair_list`: the two images of a pair differ. Column 0 names one image at most 2 times, and some image exactly 2 times. At most 4 pairs name one image in either column, and some image is named by exactly 4 pairs. `w_self_qkv`: Queries, keys and values stacked along the first dimension. `w_cross_qkv`: Queries, keys and values stacked along the first dimension.
All inputs are finite; a program needn't handle non-finite values.
Results may differ from a plain program's by a relative error of at most 0.02.
Values may be sent and summed in bfloat16 or wider, within the bound.
No kernel may reach another device: no remote copies, remote signals or barrier semaphores. Data moves between devices by JAX's collectives and lax.ppermute only.
A program may use at most 64 MiB of HBM per device.

v0:
```python
import math

import jax
import jax.numpy as jnp
from jax import lax
from jax.sharding import PartitionSpec as P

HEAD_DIM = 64
PAIR_DEV = 1


def normalize(values_in, scale_gain):
    average = jnp.mean(values_in, axis=-1, keepdims=True)
    centred = values_in - average
    variance = jnp.mean(centred * centred, axis=-1, keepdims=True)
    return (centred * lax.rsqrt(variance + 1e-06) * scale_gain).astype(jnp.bfloat16)


def split_heads(matrix):
    return matrix.reshape(matrix.shape[:2] + (matrix.shape[2] // HEAD_DIM, HEAD_DIM))


def attend(query_in, key_in, w_qkv):
    queries = jnp.dot(query_in, w_qkv[0], preferred_element_type=jnp.float32).astype(jnp.bfloat16)
    keys_proj = jnp.dot(key_in, w_qkv[1], preferred_element_type=jnp.float32).astype(jnp.bfloat16)
    values_proj = jnp.dot(key_in, w_qkv[2], preferred_element_type=jnp.float32).astype(jnp.bfloat16)
    score_scale = 1.0 / math.sqrt(HEAD_DIM)
    scores = (
        jnp.einsum(
            "vqhd,vkhd->vhqk",
            split_heads(queries),
            split_heads(keys_proj),
            preferred_element_type=jnp.float32,
        )
        * score_scale
    )
    weights_attn = jax.nn.softmax(scores, axis=-1).astype(jnp.bfloat16)
    context = jnp.einsum(
        "vhqk,vkhd->vqhd",
        weights_attn,
        split_heads(values_proj),
        preferred_element_type=jnp.float32,
    ).astype(jnp.bfloat16)
    return context.reshape(queries.shape)


def project_heads(context, w_out):
    partial_sum = jnp.dot(context, w_out, preferred_element_type=jnp.float32)
    return lax.psum(partial_sum.astype(jnp.bfloat16), "head").astype(jnp.float32)


def pair_views(slot_pair, slot_valid, first_img, second_img, pair_ids):
    pair_pick = slot_pair[:, None] == pair_ids[None, :]
    fetch_img = jnp.concatenate(
        [
            jnp.sum(jnp.where(pair_pick, first_img[None, :], 0), axis=1),
            jnp.sum(jnp.where(pair_pick, second_img[None, :], 0), axis=1),
        ]
    )
    return (fetch_img, jnp.concatenate([slot_valid, slot_valid]))


def body(
    features,
    pair_list,
    gain_self,
    gain_memory,
    gain_cross,
    gain_mlp,
    w_self_qkv,
    w_self_out,
    w_cross_qkv,
    w_cross_out,
    w_up,
    w_down,
):
    worker = lax.axis_index("pair")
    first_img = pair_list[:, 0]
    second_img = pair_list[:, 1]
    pair_total = first_img.shape[0]
    pair_ids = jnp.arange(pair_total, dtype=jnp.int32)
    slot_count = 2 * PAIR_DEV
    owned = first_img == worker
    slot_rank = jnp.cumsum(owned.astype(jnp.int32)) - 1
    slot_hit = owned[None, :] & (
        slot_rank[None, :] == jnp.arange(slot_count, dtype=jnp.int32)[:, None]
    )
    slot_pair = jnp.sum(jnp.where(slot_hit, pair_ids[None, :], 0), axis=1)
    slot_valid = jnp.any(slot_hit, axis=1)
    fetch_img, view_valid = pair_views(slot_pair, slot_valid, first_img, second_img, pair_ids)
    gathered_rows = lax.all_gather(features, "pair", axis=0, tiled=True)
    image_ids = jnp.arange(gathered_rows.shape[0], dtype=jnp.int32)
    select = (fetch_img[:, None] == image_ids[None, :]).astype(jnp.bfloat16)
    picked = jnp.einsum("vk,ktd->vtd", select, gathered_rows, preferred_element_type=jnp.float32)
    to_gather = picked.astype(jnp.bfloat16)
    gathered = lax.all_gather(to_gather, "head", axis=2, tiled=True).astype(jnp.float32)
    memory_feats = jnp.concatenate([gathered[slot_count:], gathered[:slot_count]], axis=0)
    normed_self = normalize(gathered, gain_self)
    normed_memory = normalize(memory_feats, gain_memory)
    after_self = gathered + project_heads(attend(normed_self, normed_self, w_self_qkv), w_self_out)
    normed_cross = normalize(after_self, gain_cross)
    after_cross = after_self + project_heads(
        attend(normed_cross, normed_memory, w_cross_qkv), w_cross_out
    )
    normed_mlp = normalize(after_cross, gain_mlp)
    hidden = jax.nn.gelu(
        jnp.dot(normed_mlp, w_up, preferred_element_type=jnp.float32), approximate=False
    ).astype(jnp.bfloat16)
    mlp_partial = jnp.dot(hidden, w_down, preferred_element_type=jnp.float32)
    mlp_share = lax.psum_scatter(
        mlp_partial.astype(jnp.bfloat16), "head", scatter_dimension=2, tiled=True
    ).astype(jnp.float32)
    col_width = features.shape[2]
    col_start = lax.axis_index("head") * col_width
    decoded = lax.dynamic_slice_in_dim(after_cross, col_start, col_width, 2) + mlp_share
    image_ids = jnp.arange(features.shape[0] * lax.axis_size("pair"), dtype=jnp.int32)
    select = ((fetch_img[None, :] == image_ids[:, None]) & view_valid[None, :]).astype(jnp.float32)
    return lax.psum_scatter(
        jnp.einsum("iv,vtd->itd", select, decoded, precision=lax.Precision.HIGHEST).astype(
            jnp.bfloat16
        ),
        "pair",
        scatter_dimension=0,
        tiled=True,
    ).astype(jnp.float32)


def solution(mesh):
    in_specs = (
        P(("grp", "pair"), None, "head"),
        P("grp", None),
        P(),
        P(),
        P(),
        P(),
        P(None, None, "head"),
        P("head", None),
        P(None, None, "head"),
        P("head", None),
        P(None, "head"),
        P("head", None),
    )
    out_specs = P(("grp", "pair"), None, "head")
    return jax.shard_map(body, mesh=mesh, in_specs=in_specs, out_specs=out_specs, check_vma=False)
```

profile of v0, /device:TPU:0, one launch (start us, length us, event | category | flops | bytes accessed | tf_op | source)
XLA Modules:
  0.0 257.9 jit_solution(12181049153669514590)
XLA Ops:
  6.5 0.8 slice_bitcast_fusion
  7.3 0.7 broadcast_compare_fusion
  8.0 0.7 compare_convert_fusion
  8.7 16.4 %all_gather.6 = bf16[4,224,192]{1,2,0:T(8,128)(2,1)S(1)} all-gather(bf16[1,224,192]{1,2,0:T(8,128)(2,1)} %param.12), channel_id=1, replica_groups=mesh['grp'=2,'pair'=4,'head'=4] {'pair'}, dimensions={0}, use_global_device_ids=true | all-gather | bytes 430080 | tf_op jit(solution)/shard_map/all_gather | solution.py:91
  25.1 0.2 reduce-window.8
  25.3 0.1 select_reduce_fusion.2
  25.4 0.4 copy-done.15
  25.9 0.2 select_reduce_fusion.1
  26.0 0.1 pad_add_fusion.1
  26.1 1.2 convolution_convert_fusion.4
  27.3 0.0 all-reduce.5.cloned.1.call-start
  27.4 21.5 %all-gather.2.cloned.1.call-done = bf16[4,224,768]{1,0,2:T(4,128)(2,1)} async-done(((bf16[4,224,192]{1,0,2:T(4,128)(2,1)}), bf16[4,224,768]{1,0,2:T(4,128)(2,1)}) %all-gather.2.cloned.1.call-update) | async-done | bytes 1376272 | tf_op jit(solution)/shard_map/all_gather | solution.py:96
  48.9 1.7 copy_convert_fusion
  50.6 0.2 fusion.124
  50.8 0.3 fusion.12
  51.1 0.4 multiply_reduce_fusion.2
  51.5 0.5 copy-done.2
  52.0 0.5 copy-done.3
  52.4 0.9 copy-done.1
  53.3 0.2 convert_reduce_fusion
  53.6 0.5 multiply_reduce_fusion.3
  54.1 1.8 convolution_convert_fusion.11
  55.9 0.1 copy.92
  56.0 1.8 convolution_convert_fusion.10
  57.8 0.1 copy.94
  58.0 2.5 convolution_convert_fusion.9
  60.4 1.1 copy.96
  61.5 2.6 %fusion.125 = (f32[4,2,224]{2,1,0:T(2,128)}, f32[4,2,224,224]{2,3,1,0:T(8,128)}) fusion(bf16[4,224,2,64]{1,3,2,0:T(8,128)(2,1)S(1)} %bitcast.78, bf16[4,224,2,64]{1,3,2,0:T(8,128)(2,1)S(1)} %bitcast.79), kind=kOutput, calls=%fused_computation.188 | convolution fusion | flops 52584672 | bytes 2071552 | tf_op jit(solution)/shard_map/sub | solution.py:37
  64.1 1.8 convolution_convert_fusion.6
  66.0 1.8 convolution_convert_fusion.2
  67.8 0.2 all-reduce.7.cloned.1.call-start
  68.0 2.3 multiply_convert_fusion.2
  70.4 1.1 copy-done.6
  71.5 1.6 convolution_convert_fusion.8
  73.1 0.1 copy.101
  73.2 2.1 convolution_convert_fusion.7
  75.3 0.1 copy.105
  75.5 35.3 %all-reduce.5.cloned.1.call-done = bf16[4,224,768]{1,2,0:T(8,128)(2,1)} async-done(((bf16[4,224,768]{1,2,0:T(8,128)(2,1)}), bf16[4,224,768]{1,2,0:T(8,128)(2,1)}) %all-reduce.5.cloned.1.call-update) | async-done | bytes 1376272 | tf_op jit(solution)/shard_map/psum | solution.py:49
  110.8 1.9 fusion.11
  112.7 0.6 multiply_reduce_fusion.1
  113.3 2.0 fusion.51
  115.3 0.9 copy.103
  116.2 3.0 %fusion.126 = (f32[4,2,224]{2,1,0:T(2,128)S(1)}, f32[4,2,224,224]{2,3,1,0:T(8,128)}) fusion(bf16[4,224,2,64]{1,3,2,0:T(8,128)(2,1)} %bitcast.80, bf16[4,224,2,64]{1,3,2,0:T(8,128)(2,1)S(1)} %bitcast.76), kind=kOutput, calls=%fused_computation.189 | convolution fusion | flops 52584672 | bytes 2071552 | tf_op jit(solution)/shard_map/sub | solution.py:37
  119.1 1.8 convolution_convert_fusion.5
  121.0 1.8 convolution_convert_fusion.1
  122.8 0.3 all-reduce.9.cloned.1.call-start
  123.0 42.8 %all-reduce.7.cloned.1.call-done = bf16[4,224,768]{1,2,0:T(8,128)(2,1)} async-done(((bf16[4,224,768]{1,2,0:T(8,128)(2,1)}), bf16[4,224,768]{1,2,0:T(8,128)(2,1)}) %all-reduce.7.cloned.1.call-update) | async-done | bytes 1376272 | tf_op jit(solution)/shard_map/psum | solution.py:49
  165.8 2.5 fusion.123
  168.3 0.4 multiply_reduce_fusion
  168.7 0.3 copy-done.13
  169.0 2.1 fusion.58
  171.2 7.8 %convolution_convert_fusion = bf16[4,224,768]{1,2,0:T(8,128)(2,1)S(1)} fusion(f32[4,224,768]{2,1,0:T(8,128)S(1)} %get-tuple-element.19, bf16[768,768]{1,0:T(8,128)(2,1)S(1)} %copy-done.10, u8[224,768]{1,0:T(8,128)(4,1)S(1)} %get-tuple-element.6, u8[224,768]{1,0:T(8,128)(4,1)S(1)} %get-tuple-element.5), kind=kOutput, calls=%fused_computation.46 | convolution fusion | flops 1105821696 | bytes 5652480 | tf_op jit(solution)/shard_map/dot_general | solution.py:109
  179.0 2.4 copy.111
  181.4 0.0 reduce-scatter.2.cloned.1.call-start
  181.5 0.6 dynamic-slice
  182.7 0.1 fusion.88
  182.8 0.1 pad_add_fusion
  182.9 41.5 %all-reduce.9.cloned.1.call-done = bf16[4,224,768]{1,0,2:T(4,128)(2,1)} async-done(((bf16[4,224,768]{1,0,2:T(4,128)(2,1)}), bf16[4,224,768]{1,0,2:T(4,128)(2,1)}) %all-reduce.9.cloned.1.call-update) | async-done | bytes 1376272
  224.5 1.1 constant_dynamic-slice_fusion
  225.6 1.2 convert_add_fusion.2
  226.8 1.3 convolution_convert_fusion.3
  228.1 0.8 copy.114
  228.9 20.8 %reduce-scatter.2.cloned.1.call-done = bf16[1,224,192]{1,2,0:T(8,128)(2,1)} async-done(((bf16[4,224,192]{1,2,0:T(8,128)(2,1)}), bf16[1,224,192]{1,2,0:T(8,128)(2,1)}) %reduce-scatter.2.cloned.1.call-update) | async-done | bytes 86032 | tf_op jit(solution)/shard_map/reduce_scatter | solution.py:118
  249.8 1.6 convert_element_type.114
  (43 shorter events, 0.2 us)
Async XLA Ops:
  6.5 162.2 %copy-start = (bf16[768,768]{1,0:T(8,128)(2,1)S(1)}, bf16[768,768]{1,0:T(8,128)(2,1)}, u32[]{:S(2)}) copy-start(bf16[768,768]{1,0:T(8,128)(2,1)} %param.22) | copy-start | bytes 3538948
  6.5 42.4 %all-gather.2.cloned.1.call-start = ((), (), s32[]{:S(2)}) async-start(), calls=%async_computation.1 | async-start | bytes 1966080 | tf_op jit(solution)/shard_map/all_gather | solution.py:96
  25.3 0.5 copy-start.15
  27.3 83.5 %all-reduce.5.cloned.1.call-start = ((), (), s32[]{:S(2)}) async-start(), calls=%async_computation.2 | async-start | bytes 3145728 | tf_op jit(solution)/shard_map/psum | solution.py:49
  50.8 1.2 copy-start.2
  50.8 1.6 copy-start.3
  50.8 2.5 copy-start.1
  51.1 3.0 %copy-start.11 = (f32[768]{0:T(1024)S(1)}, f32[768]{0:T(1024)}, u32[]{:S(2)}) copy-start(f32[768]{0:T(1024)} %param.14) | copy-start | bytes 9220
  64.1 1.9 copy-start.7
  66.0 2.0 copy-start.9
  67.8 98.1 %all-reduce.7.cloned.1.call-start = ((), (), s32[]{:S(2)}) async-start(), calls=%async_computation.3 | async-start | bytes 3145728 | tf_op jit(solution)/shard_map/psum | solution.py:49
  70.3 1.1 copy-start.6
  75.4 37.9 %copy-start.12 = (f32[768]{0:T(1024)S(1)}, f32[768]{0:T(1024)}, u32[]{:S(2)}) copy-start(f32[768]{0:T(1024)} %param.16) | copy-start | bytes 9220
  110.8 1.9 copy-start.5
  119.1 1.8 copy-start.8
  122.8 101.7 %all-reduce.9.cloned.1.call-start = ((), (), s32[]{:S(2)}) async-start(), calls=%async_computation.5 | async-start | bytes 3145728
  168.3 2.9 %copy-start.4 = (f32[4,224,768]{1,2,0:T(8,128)}, f32[4,224,768]{1,2,0:T(8,128)S(1)}, u32[]{:S(2)}) copy-start(f32[4,224,768]{1,2,0:T(8,128)S(1)} %get-tuple-element.10) | copy-start | bytes 8257540
  168.3 0.7 copy-start.13
  169.0 2.2 copy-start.10
  179.0 2.5 copy-start.14
  179.0 3.7 %copy-start.16 = (s32[4]{0:T(128)S(1)}, s32[4]{0:T(128)}, u32[]{:S(2)}) copy-start(s32[4]{0:T(128)} %copy-done.15) | copy-start | bytes 52
  181.4 68.4 %reduce-scatter.2.cloned.1.call-start = ((), (), s32[]{:S(2)}) async-start(), calls=%async_computation.4 | async-start | bytes 491520 | tf_op jit(solution)/shard_map/reduce_scatter | solution.py:118
Sparse Core Ops, SparseCore 0:
  27.4 21.3 all-gather.1
  67.9 42.8 all-reduce.4
  122.9 42.9 all-reduce.6
  181.5 42.8 all-reduce.8
  229.1 20.6 reduce-scatter.1
where the time goes:
time: 259 us; the launch traced here: 258 us
  waiting for transfers between devices  162 us (63%)
  matrix products  36.8 us (14%)
  blocking collectives  16.4 us (6%)
  other arithmetic  15.7 us (6%)
  between operations  14.2 us (5%)
  local copies, waits for them, and re-layouts  12.1 us (5%)
    psum x2, waiting for transfers between devices, project_heads(): lax.psum(partial_sum.astype(jnp.bfloat16), 'head').astype(jnp.float32)  78.1 us
    unnamed x6, waiting for transfers between devices  41.6 us
    all_gather x1, waiting for transfers between devices, body(): lax.all_gather(to_gather, 'head', axis=2, tiled=True).astype(jnp.float32)  21.5 us
    reduce_scatter x1, waiting for transfers between devices, body(): lax.psum_scatter(jnp.einsum('iv,vtd->itd', select, decoded, precision=lax...  20.8 us
    all_gather x1, blocking collectives, body(): gathered_rows = lax.all_gather(features, 'pair', axis=0, tiled=True)  16.4 us
    dot_general x1, matrix products, body(): mlp_partial = jnp.dot(hidden, w_down, preferred_element_type=jnp.float32)  7.77 us
    sub x2, matrix products, attend(): weights_attn = jax.nn.softmax(scores, axis=-1).astype(jnp.bfloat16)  5.6 us
    unnamed x36, local copies, waits for them, and re-layouts  5.44 us
  transfers between devices with their start and end apart: 5, of which 5 were waited for; matrix products, arithmetic and copies ran while one was open for 3% of the time, Pallas kernels for 0%

commit v1 on v0

v1 whole, which is shorter than its diff:
```python
import math

import jax
import jax.numpy as jnp
from jax import lax
from jax.experimental import pallas as pl
from jax.experimental.pallas import tpu as pltpu
from jax.sharding import PartitionSpec as P

HEAD_DIM = 64
ROW_GROUPS = 2
DEGREE = 6
SCALE = 1.0 / math.sqrt(HEAD_DIM)
VMEM = pl.BlockSpec(memory_space=pltpu.VMEM)
SMEM = pl.BlockSpec(memory_space=pltpu.SMEM)
BF16 = jnp.bfloat16
F32 = jnp.float32


def mm(a, b):
    return jnp.dot(a, b, preferred_element_type=F32)


def standardize(x):
    centred = x - jnp.mean(x, axis=-1, keepdims=True)
    variance = jnp.mean(centred * centred, axis=-1, keepdims=True)
    return centred * lax.rsqrt(variance + 1e-06)


def head_attention(q, k, v):
    rows, width = q.shape
    heads = width // HEAD_DIM
    lane_head = lax.broadcasted_iota(jnp.int32, (rows, width), 1) // HEAD_DIM
    zero = jnp.zeros_like(q)
    stacked = jnp.concatenate([jnp.where(lane_head == i, q, zero) for i in range(heads)], axis=0)
    scores = lax.dot_general(stacked, k, (((1,), (1,)), ((), ())), preferred_element_type=F32)
    top = jnp.max(scores, axis=-1, keepdims=True)
    weights = jnp.exp((scores - top) * SCALE)
    total = jnp.sum(weights, axis=-1, keepdims=True)
    weights = (weights * (1.0 / total)).astype(BF16)
    mixed = mm(weights, v)
    context = jnp.zeros((rows, width), F32)
    for i in range(heads):
        context = context + jnp.where(lane_head == i, mixed[i * rows : (i + 1) * rows], 0.0)
    return context


def self_kernel(groups, place, *refs):
    blocks = refs[: 2 * groups]
    g_self, g_memory, w_own, w_other, w_kv = refs[2 * groups : 2 * groups + 5]
    x_rows, context, kv, x_full = refs[2 * groups + 5 :]
    group, member = place[0], place[1]
    width = blocks[0].shape[0]
    for step in range(groups):
        source = lax.rem(group - step + groups, groups)
        for other in range(2):
            index = source * 2 + (member if other == 0 else 1 - member)
            x_full[pl.ds(pl.multiple_of(index * width, width), width), :] = blocks[2 * step + other][...]
    x = x_full[...].astype(F32).T
    rows = x.shape[0] // ROW_GROUPS
    normed = standardize(x)
    memory = (normed * g_memory[...]).astype(BF16)
    kv[:, : kv.shape[1] // 2] = mm(memory, w_kv[1]).astype(BF16)
    kv[:, kv.shape[1] // 2 :] = mm(memory, w_kv[2]).astype(BF16)
    own = (normed * g_self[...]).astype(BF16)
    mine = jnp.where(member == 0, own[:rows], own[rows:])
    x_rows[...] = jnp.where(member == 0, x[:rows], x[rows:])
    q = jnp.concatenate([mm(mine, w_own[0]), mm(mine, w_other[0])], axis=1).astype(BF16)
    k = jnp.concatenate([mm(own, w_own[1]), mm(own, w_other[1])], axis=1).astype(BF16)
    v = jnp.concatenate([mm(own, w_own[2]), mm(own, w_other[2])], axis=1).astype(BF16)
    context[...] = head_attention(q, k, v).astype(BF16)


def query_kernel(groups, *refs):
    contexts = refs[:groups]
    w_out = refs[groups : 3 * groups]
    x_rows, gain, wq_own, wq_other, after, queries = refs[3 * groups :]
    total = x_rows[...]
    width = contexts[0].shape[1] // 2
    for step in range(groups):
        total = total + mm(contexts[step][:, :width], w_out[2 * step][...])
        total = total + mm(contexts[step][:, width:], w_out[2 * step + 1][...])
    after[...] = total
    normed = (standardize(total) * gain[...]).astype(BF16)
    queries[...] = jnp.concatenate([mm(normed, wq_own[...]), mm(normed, wq_other[...])], axis=1).astype(BF16)


def cross_kernel(views, queries, *refs):
    own, other, context = refs[:views], refs[views : 2 * views], refs[2 * views]
    q = queries[...]
    width = q.shape[1] // 2
    for view in range(views):
        k = jnp.concatenate([own[view][:, :width], other[view][:, :width]], axis=1)
        v = jnp.concatenate([own[view][:, width:], other[view][:, width:]], axis=1)
        context[view] = head_attention(q, k, v).astype(BF16)


def mlp_kernel(groups, place, counts, *refs):
    contexts = refs[:groups]
    w_out = refs[groups : 3 * groups]
    after, gain, up_own, up_other, down_own, down_other = refs[3 * groups : 3 * groups + 6]
    outs = refs[3 * groups + 6 : 5 * groups + 6]
    kept, partial = refs[5 * groups + 6 :]
    group, member = place[0], place[1]
    views, rows, width = contexts[0].shape
    width = width // 2
    column = after.shape[1] // (2 * groups)
    residual = after[...]
    total = jnp.concatenate([residual] * views, axis=0)
    for step in range(groups):
        held = contexts[step][...].reshape(views * rows, 2 * width)
        total = total + mm(held[:, :width], w_out[2 * step][...])
        total = total + mm(held[:, width:], w_out[2 * step + 1][...])
    share = [counts[view] for view in range(views)]
    keep = jnp.zeros_like(residual)
    for view in range(views):
        keep = keep + share[view] * total[view * rows : (view + 1) * rows]
    kept[...] = keep.T
    normed = (standardize(total) * gain[...]).astype(BF16)
    down = jnp.zeros_like(residual)
    for w_up, w_down in ((up_own, down_own), (up_other, down_other)):
        raw = mm(normed, w_up[...])
        hidden = (0.5 * raw * (1.0 + lax.erf(raw * math.sqrt(0.5)))).astype(BF16).astype(F32)
        added = jnp.zeros((rows, raw.shape[1]), F32)
        for view in range(views):
            added = added + share[view] * hidden[view * rows : (view + 1) * rows]
        down = down + mm(added.astype(BF16), w_down[...])
    partial[...] = down.T
    for step in range(groups):
        target = lax.rem(group + step, groups)
        for other in range(2):
            index = target * 2 + (member if other == 0 else 1 - member)
            here = pl.ds(pl.multiple_of(index * column, column), column)
            piece = partial[here, :]
            if step == 0:
                piece = piece + kept[here, :]
            outs[2 * step + other][...] = piece.astype(outs[2 * step + other].dtype)


def body(
    features,
    pair_list,
    gain_self,
    gain_memory,
    gain_cross,
    gain_mlp,
    w_self_qkv,
    w_self_out,
    w_cross_qkv,
    w_cross_out,
    w_up,
    w_down,
):
    head = lax.axis_size("head")
    groups = head // ROW_GROUPS
    images = lax.axis_size("pair")
    here = lax.axis_index("head")
    image = lax.axis_index("pair")
    group, member = here // ROW_GROUPS, here % ROW_GROUPS
    place = jnp.stack([group, member]).astype(jnp.int32)
    tokens, column = features.shape[1:]
    model = gain_self.shape[0]
    rows = tokens // ROW_GROUPS
    att = w_self_out.shape[0]

    def swap(value):
        return lax.ppermute(value, "head", [(i, i ^ 1) for i in range(head)])

    def turn(value, step, cross=0):
        return lax.ppermute(
            value,
            "head",
            [
                (i, ((i // 2 + step) % groups) * 2 + ((i % 2) ^ cross))
                for i in range(head)
            ],
        )

    def gather_blocks(value):
        blocks = [value, swap(value)]
        for step in range(1, groups):
            arrived = turn(value, step)
            blocks += [arrived, swap(arrived)]
        return blocks

    def call(kernel, out_shape, args, scratch=(), smem=0, flops=0):
        return pl.pallas_call(
            kernel,
            out_shape=out_shape,
            in_specs=[SMEM] * smem + [VMEM] * (len(args) - smem),
            out_specs=jax.tree.map(lambda _: VMEM, out_shape),
            scratch_shapes=list(scratch),
            compiler_params=pltpu.CompilerParams(vmem_limit_bytes=32 * 2**20),
            cost_estimate=pl.CostEstimate(flops=flops, bytes_accessed=2**20, transcendentals=0),
        )(*args)

    shape = jax.ShapeDtypeStruct
    gains = [g.reshape(1, model) for g in (gain_self, gain_memory, gain_cross, gain_mlp)]

    blocks = gather_blocks(features[0].T)
    self_other = swap(w_self_qkv)
    self_out = gather_blocks(w_self_out)
    query_own = w_cross_qkv[0]
    query_other = swap(query_own)
    cross_out = gather_blocks(w_cross_out)
    up_other, down_other = swap(w_up), swap(w_down)

    x_rows, context, kv = call(
        lambda *refs: self_kernel(groups, *refs),
        [
            shape((rows, model), F32),
            shape((rows, 2 * att), BF16),
            shape((tokens, 2 * att), BF16),
        ],
        [place, *blocks, gains[0], gains[1], w_self_qkv, self_other, w_cross_qkv],
        scratch=[pltpu.VMEM((model, tokens), BF16)],
        smem=1,
        flops=10**9,
    )
    contexts = [context] + [turn(context, step) for step in range(1, groups)]

    first, second = pair_list[:, 0], pair_list[:, 1]
    named = (first == image) | (second == image)
    partner = jnp.where(first == image, second, first)
    if images - 1 <= DEGREE:
        views = images - 1
        kv_own = [
            lax.ppermute(kv, "pair", [(i, (i - step) % images) for i in range(images)])
            for step in range(1, images)
        ]
        memories = jnp.stack([(image + step) % images for step in range(1, images)])
        counts = jnp.sum(named[None, :] & (partner[None, :] == memories[:, None]), axis=1)
    else:
        views = min(DEGREE, first.shape[0])
        rank = jnp.cumsum(named.astype(jnp.int32)) - 1
        hit = named[None, :] & (rank[None, :] == jnp.arange(views)[:, None])
        memories = jnp.sum(jnp.where(hit, partner[None, :], 0), axis=1)
        counts = jnp.any(hit, axis=1)
        gathered = lax.all_gather(kv, "pair", axis=0, tiled=False)
        kv_own = [lax.dynamic_index_in_dim(gathered, memories[view], 0, False) for view in range(views)]
    counts = counts.astype(F32)
    kv_other = [swap(value) for value in kv_own]

    after, queries = call(
        lambda *refs: query_kernel(groups, *refs),
        [shape((rows, model), F32), shape((rows, 2 * att), BF16)],
        [*contexts, *self_out, x_rows, gains[2], query_own, query_other],
        flops=10**9,
    )
    context = call(
        lambda *refs: cross_kernel(views, *refs),
        shape((views, rows, 2 * att), BF16),
        [queries, *kv_own, *kv_other],
        flops=10**9,
    )
    contexts = [context] + [turn(context, step) for step in range(1, groups)]
    pieces = call(
        lambda *refs: mlp_kernel(groups, *refs),
        [shape((column, rows), F32)] * 2 + [shape((column, rows), BF16)] * (2 * groups - 2),
        [place, counts, *contexts, *cross_out, after, gains[3], w_up, up_other, w_down, down_other],
        scratch=[pltpu.VMEM((model, rows), F32)] * 2,
        smem=2,
        flops=3 * 10**9,
    )
    mine, theirs = pieces[0], swap(pieces[1])
    for step in range(1, groups):
        mine = mine + turn(pieces[2 * step], step).astype(F32)
        theirs = theirs + turn(pieces[2 * step + 1], step, 1).astype(F32)
    low = jnp.where(member == 0, mine, theirs)
    high = jnp.where(member == 0, theirs, mine)
    return jnp.concatenate([low, high], axis=1).T[None]


def solution(mesh):
    in_specs = (
        P(("grp", "pair"), None, "head"),
        P("grp", None),
        P(),
        P(),
        P(),
        P(),
        P(None, None, "head"),
        P("head", None),
        P(None, None, "head"),
        P("head", None),
        P(None, "head"),
        P("head", None),
    )
    out_specs = P(("grp", "pair"), None, "head")
    return jax.shard_map(body, mesh=mesh, in_specs=in_specs, out_specs=out_specs, check_vma=False)
```

time: 259 us -> 63.2 us (0.24)
  waiting for transfers between devices: 162 us -> 16.8 us
  matrix products: 36.8 us -> 0 us
  starting transfers between devices: 0.57 us -> 17.9 us
  blocking collectives: 16.4 us -> 0 us
  other arithmetic: 15.7 us -> 1.17 us
  between operations: 14.2 us -> 0.2 us
  Pallas kernels: 0 us -> 11.1 us
  local copies, waits for them, and re-layouts: 12.1 us -> 15.4 us
    psum x2 -> x0, waiting for transfers between devices: 78.1 us -> none  [project_heads(): lax.psum(partial_sum.astype(jnp.bfloat16), 'head').astype(jnp.float32)]
    unnamed x6 -> x0, waiting for transfers between devices: 41.6 us -> none
    dot_general x14 -> x0, matrix products: 31.2 us -> none  [the longest x1 7.77 us: body(): mlp_partial = jnp.dot(hidden, w_down, preferred_element_type=jnp.float32)]
    all_gather x1 -> x0, waiting for transfers between devices: 21.5 us -> none  [body(): lax.all_gather(to_gather, 'head', axis=2, tiled=True).astype(jnp.float32)]
    reduce_scatter x1 -> x0, waiting for transfers between devices: 20.8 us -> none  [body(): lax.psum_scatter(jnp.einsum('iv,vtd->itd', select, decoded, precision=lax...]
    ppermute x0 -> x24, starting transfers between devices: none -> 17.9 us  [the longest x7 7.82 us: turn(): lax.ppermute(value, 'head', [(i, (i // 2 + step) % groups * 2 + (i % 2 ^...]
    ppermute x0 -> x24, waiting for transfers between devices: none -> 16.8 us  [the longest x7 12.1 us: turn(): lax.ppermute(value, 'head', [(i, (i // 2 + step) % groups * 2 + (i % 2 ^...]
    all_gather x1 -> x0, blocking collectives: 16.4 us -> none  [body(): gathered_rows = lax.all_gather(features, 'pair', axis=0, tiled=True)]
  transfers between devices with their start and end apart: 5 -> 24, of which waited for: 5 -> 8; matrix products, arithmetic and copies ran while one was open for 3% -> 4% of each run, Pallas kernels for 0% -> 11%
where the time goes in v1:
time: 63.2 us; the launch traced here: 62.5 us
  starting transfers between devices  17.9 us (28%)
  waiting for transfers between devices  16.8 us (27%)
  local copies, waits for them, and re-layouts  15.4 us (24%)
  Pallas kernels  11.1 us (18%)
  other arithmetic  1.17 us (2%)
    unnamed x46, local copies, waits for them, and re-layouts  13 us
    ppermute x7, waiting for transfers between devices, turn(): lax.ppermute(value, 'head', [(i, (i // 2 + step) % groups * 2 + (i % 2 ^...  12.1 us
    pallas_call x4, Pallas kernels, call(): pl.pallas_call(kernel, out_shape=out_shape, in_specs=[SMEM] * smem + [VME...  11.1 us
    ppermute x7, starting transfers between devices, turn(): lax.ppermute(value, 'head', [(i, (i // 2 + step) % groups * 2 + (i % 2 ^...  7.82 us
    ppermute x3, starting transfers between devices, body(): lax.ppermute(kv, 'pair', [(i, (i - step) % images) for i in range(images)])  7.2 us
    ppermute x3, waiting for transfers between devices, body(): lax.ppermute(kv, 'pair', [(i, (i - step) % images) for i in range(images)])  4.64 us
    ppermute x14, starting transfers between devices, swap(): return lax.ppermute(value, 'head', [(i, i ^ 1) for i in range(head)])  2.85 us
    reshape x4, local copies, waits for them, and re-layouts, body(): g.reshape(1, model)  1.39 us
  transfers between devices with their start and end apart: 24, of which 8 were waited for; matrix products, arithmetic and copies ran while one was open for 4% of the time, Pallas kernels for 11%

profile of v1, /device:TPU:0, one launch (start us, length us, event | category | flops | bytes accessed | tf_op | source)
XLA Modules:
  0.0 62.5 jit_solution(17889601266701263749)
XLA Ops:
  0.0 0.5 collective-permute-start.3
  0.5 2.5 %collective-permute-start.1 = (bf16[192,224]{1,0:T(8,128)(2,1)}, bf16[192,224]{1,0:T(8,128)(2,1)S(1)}, u32[]{:S(2)}, u32[]{:S(2)}) collective-permute-start(bf16[192,224]{1,0:T(8,128)(2,1)} %bitcast.20), channel_id=1, source_target_pairs={{0,2},{1,3},{2,0},{3,1},{4,6},{5,7},{6,4},{7,5},{8,10},{9,11},{10,... | collective-permute-start | bytes 258056 | tf_op jit(solution)/shard_map/ppermute | solution.py:170
  2.9 0.9 %slice_bitcast_fusion.refs_8_ = bf16[768,128]{1,0:T(8,128)(2,1)S(1)} fusion(bf16[3,768,128]{2,1,0:T(8,128)(2,1)} %refs_9_.1), kind=kLoop, calls=%fused_computation.1 | loop fusion | bytes 393216 | tf_op jit(solution)/shard_map/squeeze | solution.py:203
  3.9 0.3 collective-permute-start.8
  4.2 0.3 collective-permute-start.6
  4.5 0.0 collective-permute-start
  4.5 2.2 %collective-permute-done.1.refs_3_ = bf16[192,224]{1,0:T(8,128)(2,1)S(1)} collective-permute-done((bf16[192,224]{1,0:T(8,128)(2,1)}, bf16[192,224]{1,0:T(8,128)(2,1)S(1)}, u32[]{:S(2)}, u32[]{:S(2)}) %collective-permute-start.1) | collective-permute-done | bytes 86048 | tf_op jit(solution)/shard_map/ppermute | solution.py:170
  6.6 0.6 %copy-done.10 = bf16[192,224]{1,0:T(8,128)(2,1)} copy-done((bf16[192,224]{1,0:T(8,128)(2,1)}, bf16[192,224]{1,0:T(8,128)(2,1)S(1)}, u32[]{:S(2)}) %copy-start.10) | copy-done | bytes 86040
  7.3 0.0 collective-permute-done.refs_2_
  7.3 0.6 %copy-done.12 = bf16[192,224]{1,0:T(8,128)(2,1)} copy-done((bf16[192,224]{1,0:T(8,128)(2,1)}, bf16[192,224]{1,0:T(8,128)(2,1)S(1)}, u32[]{:S(2)}) %copy-start.12) | copy-done | bytes 86040
  7.9 0.5 collective-permute-start.19
  8.4 0.0 collective-permute-done.2.refs_4_
  8.4 0.6 %copy-done.14 = bf16[192,224]{1,0:T(8,128)(2,1)} copy-done((bf16[192,224]{1,0:T(8,128)(2,1)}, bf16[192,224]{1,0:T(8,128)(2,1)S(1)}, u32[]{:S(2)}) %copy-start.14) | copy-done | bytes 86040
  9.1 0.0 collective-permute-start.20
  9.1 0.5 collective-permute-start.5
  9.6 2.0 %collective-permute-done.6.refs_4_ = bf16[128,768]{1,0:T(8,128)(2,1)} collective-permute-done((bf16[128,768]{1,0:T(8,128)(2,1)}, bf16[128,768]{1,0:T(8,128)(2,1)}, u32[]{:S(2)}, u32[]{:S(2)}) %collective-permute-start.6) | collective-permute-done | bytes 196640 | tf_op jit(solution)/shard_map/ppermute | solution.py:170
  11.6 1.1 %collective-permute-start.17 = (bf16[128,768]{1,0:T(8,128)(2,1)}, bf16[128,768]{1,0:T(8,128)(2,1)}, u32[]{:S(2)}, u32[]{:S(2)}) collective-permute-start(bf16[128,768]{1,0:T(8,128)(2,1)} %refs_4_.1), channel_id=1, source_target_pairs={{0,2},{1,3},{2,0},{3,1},{4,6},{5,7},{6,4},{7,5},{8,10},{9,11},{10,... | collective-permute-start | bytes 589832 | tf_op jit(solution)/shard_map/ppermute | solution.py:170
  12.7 0.1 pad_add_fusion.refs_0_
  12.8 0.7 %reshape.35.refs_5_ = f32[1,768]{1,0:T(1,128)S(1)} reshape(f32[768]{0:T(1024)} %param.14) | data formatting | bytes 6144 | tf_op jit(solution)/shard_map/reshape | solution.py:198
  13.5 0.7 %reshape.36.refs_6_ = f32[1,768]{1,0:T(1,128)S(1)} reshape(f32[768]{0:T(1024)} %param.15) | data formatting | bytes 6144 | tf_op jit(solution)/shard_map/reshape | solution.py:198
  14.1 1.1 %copy-done = bf16[3,768,128]{2,1,0:T(8,128)(2,1)S(1)} copy-done((bf16[3,768,128]{2,1,0:T(8,128)(2,1)S(1)}, bf16[3,768,128]{2,1,0:T(8,128)(2,1)}, u32[]{:S(2)}) %copy-start) | copy-done | bytes 589848
  15.2 1.1 %copy-done.3 = bf16[3,768,128]{2,1,0:T(8,128)(2,1)S(1)} copy-done((bf16[3,768,128]{2,1,0:T(8,128)(2,1)S(1)}, bf16[3,768,128]{2,1,0:T(8,128)(2,1)}, u32[]{:S(2)}) %copy-start.3) | copy-done | bytes 589848
  16.3 0.9 %copy-done.9 = bf16[1,224,192]{1,2,0:T(8,128)(2,1)S(1)} copy-done((bf16[1,224,192]{1,2,0:T(8,128)(2,1)S(1)}, bf16[1,224,192]{1,2,0:T(8,128)(2,1)}, u32[]{:S(2)}) %copy-start.9) | copy-done | bytes 86040
  17.2 0.9 %copy-done.11 = bf16[192,224]{1,0:T(8,128)(2,1)S(1)} copy-done((bf16[192,224]{1,0:T(8,128)(2,1)S(1)}, bf16[192,224]{1,0:T(8,128)(2,1)}, u32[]{:S(2)}) %copy-start.11) | copy-done | bytes 86040
  18.1 0.9 %copy-done.13 = bf16[192,224]{1,0:T(8,128)(2,1)S(1)} copy-done((bf16[192,224]{1,0:T(8,128)(2,1)S(1)}, bf16[192,224]{1,0:T(8,128)(2,1)}, u32[]{:S(2)}) %copy-start.13) | copy-done | bytes 86040
  19.0 0.9 %copy-done.15 = bf16[192,224]{1,0:T(8,128)(2,1)S(1)} copy-done((bf16[192,224]{1,0:T(8,128)(2,1)S(1)}, bf16[192,224]{1,0:T(8,128)(2,1)}, u32[]{:S(2)}) %copy-start.15) | copy-done | bytes 86040
  19.9 2.8 %shard_map.118 = (f32[112,768]{1,0:T(8,128)S(1)}, bf16[112,256]{1,0:T(8,128)(2,1)}, bf16[224,256]{1,0:T(8,128)(2,1)S(1)}) custom-call(s32[2]{0:T(128)S(1)} %pad_add_fusion.refs_0_, bf16[192,224]{1,0:T(8,128)(2,1)S(1)} %bitcast.22, bf16[192,224]{1,0:T(8,128)(2,1)S(1)} %copy-done.13, bf16[192,224]{1,0:T(8,128)(2,1)S(1)} %copy-done.11, ...), custom_call_target="tpu_custom_call" | custom-call | flops 1000000000 | bytes 1048576 | tf_op jit(solution)/shard_map/pallas_call | solution.py:187
  22.7 0.7 %copy-done.8 = bf16[224,256]{1,0:T(8,128)(2,1)} copy-done((bf16[224,256]{1,0:T(8,128)(2,1)}, bf16[224,256]{1,0:T(8,128)(2,1)S(1)}, u32[]{:S(2)}) %copy-start.8) | copy-done | bytes 114712
  23.3 0.7 %copy-done.18 = f32[112,768]{1,0:T(8,128)} copy-done((f32[112,768]{1,0:T(8,128)}, f32[112,768]{1,0:T(8,128)S(1)}, u32[]{:S(2)}) %copy-start.18) | copy-done | bytes 344088
  24.1 0.0 collective-permute-done.5.refs_3_
  24.1 0.7 %copy-done.6 = bf16[128,768]{1,0:T(8,128)(2,1)} copy-done((bf16[128,768]{1,0:T(8,128)(2,1)}, bf16[128,768]{1,0:T(8,128)(2,1)S(1)}, u32[]{:S(2)}) %copy-start.6) | copy-done | bytes 196632
  24.7 0.9 %collective-permute-start.4 = (bf16[112,256]{1,0:T(8,128)(2,1)}, bf16[112,256]{1,0:T(8,128)(2,1)S(1)}, u32[]{:S(2)}, u32[]{:S(2)}) collective-permute-start(bf16[112,256]{1,0:T(8,128)(2,1)} %get-tuple-element.14.refs_0_), channel_id=1, source_target_pairs={{0,2},{1,3},{2,0},{3,1},{4,6},{5,7},{6,4},{7,5},{8,10},{9,11},{10,... | collective-permute-start | bytes 172040 | tf_op jit(solution)/shard_map/ppermute | solution.py:170
  25.7 0.0 collective-permute-done.17.refs_6_
  25.7 1.6 %collective-permute-start.11 = (bf16[224,256]{1,0:T(8,128)(2,1)}, bf16[224,256]{1,0:T(8,128)(2,1)S(1)}, u32[]{:S(2)}, u32[]{:S(2)}) collective-permute-start(bf16[224,256]{1,0:T(8,128)(2,1)} %copy-done.8), channel_id=1, source_target_pairs={{0,4},{4,8},{8,12},{12,0},{1,5},{5,9},{9,13},{13,1},{2,6},{6,10},{... | collective-permute-start | bytes 344072 | tf_op jit(solution)/shard_map/ppermute | solution.py:228
  27.3 0.0 collective-permute-done.7.refs_5_
  27.3 2.6 %collective-permute-start.10 = (bf16[224,256]{1,0:T(8,128)(2,1)}, bf16[224,256]{1,0:T(8,128)(2,1)S(1)}, u32[]{:S(2)}, u32[]{:S(2)}) collective-permute-start(bf16[224,256]{1,0:T(8,128)(2,1)} %copy-done.8), channel_id=1, source_target_pairs={{0,8},{4,12},{8,0},{12,4},{1,9},{5,13},{9,1},{13,5},{2,10},{6,14},... | collective-permute-start | bytes 344072 | tf_op jit(solution)/shard_map/ppermute | solution.py:228
  29.9 0.0 collective-permute-done.4.refs_1_
  29.9 0.6 copy-done.16
  30.5 3.0 %collective-permute-start.9 = (bf16[224,256]{1,0:T(8,128)(2,1)}, bf16[224,256]{1,0:T(8,128)(2,1)S(1)}, u32[]{:S(2)}, u32[]{:S(2)}) collective-permute-start(bf16[224,256]{1,0:T(8,128)(2,1)} %copy-done.8), channel_id=1, source_target_pairs={{0,12},{4,0},{8,4},{12,8},{1,13},{5,1},{9,5},{13,9},{2,14},{6,2},{... | collective-permute-start | bytes 344072 | tf_op jit(solution)/shard_map/ppermute | solution.py:228
  33.5 0.2 collective-permute-done.11.refs_3_
  33.8 0.0 collective-permute-start.14
  33.8 4.3 %collective-permute-done.10.refs_2_ = bf16[224,256]{1,0:T(8,128)(2,1)S(1)} collective-permute-done((bf16[224,256]{1,0:T(8,128)(2,1)}, bf16[224,256]{1,0:T(8,128)(2,1)S(1)}, u32[]{:S(2)}, u32[]{:S(2)}) %collective-permute-start.10) | collective-permute-done | bytes 114720 | tf_op jit(solution)/shard_map/ppermute | solution.py:228
  38.1 0.0 collective-permute-start.13
  38.1 0.1 collective-permute-done.9.refs_1_
  38.2 0.4 collective-permute-start.12
  38.7 0.0 copy-start.7
  38.7 0.9 %copy-done.7 = bf16[128,768]{1,0:T(8,128)(2,1)S(1)} copy-done((bf16[128,768]{1,0:T(8,128)(2,1)S(1)}, bf16[128,768]{1,0:T(8,128)(2,1)}, u32[]{:S(2)}) %copy-start.7) | copy-done | bytes 196632
  39.6 0.8 %copy-done.17 = bf16[112,256]{1,0:T(8,128)(2,1)S(1)} copy-done((bf16[112,256]{1,0:T(8,128)(2,1)S(1)}, bf16[112,256]{1,0:T(8,128)(2,1)}, u32[]{:S(2)}) %copy-start.17) | copy-done | bytes 57368
  40.4 1.0 %copy-done.19 = f32[112,768]{1,0:T(8,128)S(1)} copy-done((f32[112,768]{1,0:T(8,128)S(1)}, f32[112,768]{1,0:T(8,128)}, u32[]{:S(2)}) %copy-start.19) | copy-done | bytes 344088
  41.4 1.9 %shard_map.119 = (f32[112,768]{1,0:T(8,128)S(1)}, bf16[112,256]{1,0:T(8,128)(2,1)S(1)}) custom-call(bf16[112,256]{1,0:T(8,128)(2,1)} %get-tuple-element.14.refs_0_, bf16[112,256]{1,0:T(8,128)(2,1)S(1)} %copy-done.17, bf16[128,768]{1,0:T(8,128)(2,1)S(1)} %copy-done.4, bf16[128,768]{1,0:T(8,128)(2,1)S(1)} %copy-done.7, ...), custom_call_target="tpu_custom_call" | custom-call | flops 1000000000 | bytes 1048576 | tf_op jit(solution)/shard_map/pallas_call | solution.py:187
  43.3 0.2 collective-permute-start.16
  43.5 0.4 collective-permute-start.18
  43.9 2.4 %shard_map.120.refs_2_ = bf16[3,112,256]{2,1,0:T(8,128)(2,1)S(1)} custom-call(bf16[112,256]{1,0:T(8,128)(2,1)S(1)} %get-tuple-element.16.refs_0_, bf16[224,256]{1,0:T(8,128)(2,1)S(1)} %collective-permute-done.9.refs_1_, bf16[224,256]{1,0:T(8,128)(2,1)S(1)} %collective-permute-done.10.refs_2_, bf16[224,256]{1,0:T(8,128)(2,1)S(1)} %collective-permute-done.11.refs_3_, ...), custom_call_target="tpu_custom_call" | custom-call | flops 1000000000 | bytes 1048576 | tf_op jit(solution)/shard_map/pallas_call | solution.py:187
  46.4 1.2 %collective-permute-start.15 = (bf16[3,112,256]{2,1,0:T(8,128)(2,1)S(1)}, bf16[3,112,256]{2,1,0:T(8,128)(2,1)S(1)}, u32[]{:S(2)}, u32[]{:S(2)}) collective-permute-start(bf16[3,112,256]{2,1,0:T(8,128)(2,1)S(1)} %shard_map.120.refs_2_), channel_id=1, source_target_pairs={{0,2},{1,3},{2,0},{3,1},{4,6},{5,7},{6,4},{7,5},{8,10},{9,11},{10,... | collective-permute-start | bytes 516104 | tf_op jit(solution)/shard_map/ppermute | solution.py:170
  47.5 0.1 pad_add_fusion.1
  47.6 0.2 convert_reduce_fusion
  47.8 5.0 %collective-permute-done.15.refs_3_ = bf16[3,112,256]{2,1,0:T(8,128)(2,1)S(1)} collective-permute-done((bf16[3,112,256]{2,1,0:T(8,128)(2,1)S(1)}, bf16[3,112,256]{2,1,0:T(8,128)(2,1)S(1)}, u32[]{:S(2)}, u32[]{:S(2)}) %collective-permute-start.15) | collective-permute-done | bytes 172064 | tf_op jit(solution)/shard_map/ppermute | solution.py:170
  52.8 3.9 %shard_map.121 = (f32[192,112]{1,0:T(8,128)S(1)}, f32[192,112]{1,0:T(8,128)S(1)}, bf16[192,112]{1,0:T(8,128)(2,1)S(1)}, bf16[192,112]{1,0:T(8,128)(2,1)S(1)}) custom-call(s32[2]{0:T(128)S(1)} %pad_add_fusion.refs_0_, f32[3]{0:T(128)S(1)} %convert_element_type.13.refs_1_, bf16[3,112,256]{2,1,0:T(8,128)(2,1)S(1)} %shard_map.120.refs_2_, ...), custom_call_target="tpu_custom_call" | custom-call | flops 3000000000 | bytes 1048576 | tf_op jit(solution)/shard_map/pallas_call | solution.py:187
  56.7 0.1 collective-permute-start.22
  56.8 1.2 %collective-permute-start.21 = (bf16[192,112]{1,0:T(8,128)(2,1)S(1)}, bf16[192,112]{1,0:T(8,128)(2,1)S(1)}, u32[]{:S(2)}, u32[]{:S(2)}) collective-permute-start(bf16[192,112]{1,0:T(8,128)(2,1)S(1)} %get-tuple-element.20), channel_id=1, source_target_pairs={{0,2},{1,3},{2,0},{3,1},{4,6},{5,7},{6,4},{7,5},{8,10},{9,11},{10,... | collective-permute-start | bytes 129032 | tf_op jit(solution)/shard_map/ppermute | solution.py:170
  57.9 0.7 %collective-permute-start.23 = (bf16[192,112]{1,0:T(8,128)(2,1)S(1)}, bf16[192,112]{1,0:T(8,128)(2,1)S(1)}, u32[]{:S(2)}, u32[]{:S(2)}) collective-permute-start(bf16[192,112]{1,0:T(8,128)(2,1)S(1)} %get-tuple-element.22), channel_id=1, source_target_pairs={{0,3},{1,2},{2,1},{3,0},{4,7},{5,6},{6,5},{7,4},{8,11},{9,10},{10,... | collective-permute-start | bytes 129032 | tf_op jit(solution)/shard_map/ppermute | solution.py:170
  58.6 2.3 %collective-permute-done.21 = bf16[192,112]{1,0:T(8,128)(2,1)S(1)} collective-permute-done((bf16[192,112]{1,0:T(8,128)(2,1)S(1)}, bf16[192,112]{1,0:T(8,128)(2,1)S(1)}, u32[]{:S(2)}, u32[]{:S(2)}) %collective-permute-start.21) | collective-permute-done | bytes 43040 | tf_op jit(solution)/shard_map/ppermute | solution.py:170
  60.9 0.7 %collective-permute-done.23 = bf16[192,112]{1,0:T(8,128)(2,1)S(1)} collective-permute-done((bf16[192,112]{1,0:T(8,128)(2,1)S(1)}, bf16[192,112]{1,0:T(8,128)(2,1)S(1)}, u32[]{:S(2)}, u32[]{:S(2)}) %collective-permute-start.23) | collective-permute-done | bytes 43040 | tf_op jit(solution)/shard_map/ppermute | solution.py:170
  61.7 0.8 %maximum_bitcast_fusion = f32[1,224,192]{1,2,0:T(8,128)} fusion(f32[192,112]{1,0:T(8,128)S(1)} %get-tuple-element.24, f32[192,112]{1,0:T(8,128)S(1)} %get-tuple-element.23), kind=kLoop, calls=%fused_computation | loop fusion | flops 43008 | bytes 344064 | tf_op jit(solution)/shard_map/broadcast_in_dim | solution.py:271
  (47 shorter events, 0.1 us)
Async XLA Ops:
  0.0 12.7 %collective-permute-start.3 = (bf16[3,768,128]{2,1,0:T(8,128)(2,1)}, bf16[3,768,128]{2,1,0:T(8,128)(2,1)S(1)}, u32[]{:S(2)}, u32[]{:S(2)}) collective-permute-start(bf16[3,768,128]{2,1,0:T(8,128)(2,1)} %refs_7_.1), channel_id=1, source_target_pairs={{0,1},{1,0},{2,3},{3,2},{4,5},{5,4},{6,7},{7,6},{8,9},{9,8},{10,11... | collective-permute-start | bytes 1769480 | tf_op jit(solution)/shard_map/ppermute | solution.py:167
  0.5 6.2 %collective-permute-start.1 = (bf16[192,224]{1,0:T(8,128)(2,1)}, bf16[192,224]{1,0:T(8,128)(2,1)S(1)}, u32[]{:S(2)}, u32[]{:S(2)}) collective-permute-start(bf16[192,224]{1,0:T(8,128)(2,1)} %bitcast.20), channel_id=1, source_target_pairs={{0,2},{1,3},{2,0},{3,1},{4,6},{5,7},{6,4},{7,5},{8,10},{9,11},{10,... | collective-permute-start | bytes 258056 | tf_op jit(solution)/shard_map/ppermute | solution.py:170
  3.9 5.2 %collective-permute-start.8 = (bf16[768,128]{1,0:T(8,128)(2,1)S(1)}, bf16[768,128]{1,0:T(8,128)(2,1)S(1)}, u32[]{:S(2)}, u32[]{:S(2)}) collective-permute-start(bf16[768,128]{1,0:T(8,128)(2,1)S(1)} %slice_bitcast_fusion.refs_8_), channel_id=1, source_target_pairs={{0,1},{1,0},{2,3},{3,2},{4,5},{5,4},{6,7},{7,6},{8,9},{9,8},{10,11... | collective-permute-start | bytes 589832 | tf_op jit(solution)/shard_map/ppermute | solution.py:167
  4.2 7.4 %collective-permute-start.6 = (bf16[128,768]{1,0:T(8,128)(2,1)}, bf16[128,768]{1,0:T(8,128)(2,1)}, u32[]{:S(2)}, u32[]{:S(2)}) collective-permute-start(bf16[128,768]{1,0:T(8,128)(2,1)} %refs_2_.1), channel_id=1, source_target_pairs={{0,2},{1,3},{2,0},{3,1},{4,6},{5,7},{6,4},{7,5},{8,10},{9,11},{10,... | collective-permute-start | bytes 589832 | tf_op jit(solution)/shard_map/ppermute | solution.py:170
  4.5 2.8 %collective-permute-start = (bf16[192,224]{1,0:T(8,128)(2,1)}, bf16[192,224]{1,0:T(8,128)(2,1)S(1)}, u32[]{:S(2)}, u32[]{:S(2)}) collective-permute-start(bf16[192,224]{1,0:T(8,128)(2,1)} %bitcast.21), channel_id=1, source_target_pairs={{0,1},{1,0},{2,3},{3,2},{4,5},{5,4},{6,7},{7,6},{8,9},{9,8},{10,11... | collective-permute-start | bytes 258056 | tf_op jit(solution)/shard_map/ppermute | solution.py:167
  6.6 1.8 %collective-permute-start.2 = (bf16[192,224]{1,0:T(8,128)(2,1)S(1)}, bf16[192,224]{1,0:T(8,128)(2,1)S(1)}, u32[]{:S(2)}, u32[]{:S(2)}) collective-permute-start(bf16[192,224]{1,0:T(8,128)(2,1)S(1)} %collective-permute-done.1.refs_3_), channel_id=1, source_target_pairs={{0,1},{1,0},{2,3},{3,2},{4,5},{5,4},{6,7},{7,6},{8,9},{9,8},{10,11... | collective-permute-start | bytes 258056 | tf_op jit(solution)/shard_map/ppermute | solution.py:167
  6.6 0.6 %copy-start.10 = (bf16[192,224]{1,0:T(8,128)(2,1)}, bf16[192,224]{1,0:T(8,128)(2,1)S(1)}, u32[]{:S(2)}) copy-start(bf16[192,224]{1,0:T(8,128)(2,1)S(1)} %collective-permute-done.1.refs_3_) | copy-start | bytes 258052
  7.3 0.6 %copy-start.12 = (bf16[192,224]{1,0:T(8,128)(2,1)}, bf16[192,224]{1,0:T(8,128)(2,1)S(1)}, u32[]{:S(2)}) copy-start(bf16[192,224]{1,0:T(8,128)(2,1)S(1)} %collective-permute-done.refs_2_) | copy-start | bytes 258052
  7.9 44.9 %collective-permute-start.19 = (bf16[768,768]{1,0:T(8,128)(2,1)}, bf16[768,768]{1,0:T(8,128)(2,1)S(1)}, u32[]{:S(2)}, u32[]{:S(2)}) collective-permute-start(bf16[768,768]{1,0:T(8,128)(2,1)} %refs_10_.1), channel_id=1, source_target_pairs={{0,1},{1,0},{2,3},{3,2},{4,5},{5,4},{6,7},{7,6},{8,9},{9,8},{10,11... | collective-permute-start | bytes 3538952 | tf_op jit(solution)/shard_map/ppermute | solution.py:167
  8.4 0.6 %copy-start.14 = (bf16[192,224]{1,0:T(8,128)(2,1)}, bf16[192,224]{1,0:T(8,128)(2,1)S(1)}, u32[]{:S(2)}) copy-start(bf16[192,224]{1,0:T(8,128)(2,1)S(1)} %collective-permute-done.2.refs_4_) | copy-start | bytes 258052
  9.1 43.7 %collective-permute-start.20 = (bf16[768,768]{1,0:T(8,128)(2,1)}, bf16[768,768]{1,0:T(8,128)(2,1)S(1)}, u32[]{:S(2)}, u32[]{:S(2)}) collective-permute-start(bf16[768,768]{1,0:T(8,128)(2,1)} %refs_12_.1), channel_id=1, source_target_pairs={{0,1},{1,0},{2,3},{3,2},{4,5},{5,4},{6,7},{7,6},{8,9},{9,8},{10,11... | collective-permute-start | bytes 3538952 | tf_op jit(solution)/shard_map/ppermute | solution.py:167
  9.1 15.0 %collective-permute-start.5 = (bf16[128,768]{1,0:T(8,128)(2,1)}, bf16[128,768]{1,0:T(8,128)(2,1)S(1)}, u32[]{:S(2)}, u32[]{:S(2)}) collective-permute-start(bf16[128,768]{1,0:T(8,128)(2,1)} %refs_2_.1), channel_id=1, source_target_pairs={{0,1},{1,0},{2,3},{3,2},{4,5},{5,4},{6,7},{7,6},{8,9},{9,8},{10,11... | collective-permute-start | bytes 589832 | tf_op jit(solution)/shard_map/ppermute | solution.py:167
  11.6 14.1 %collective-permute-start.17 = (bf16[128,768]{1,0:T(8,128)(2,1)}, bf16[128,768]{1,0:T(8,128)(2,1)}, u32[]{:S(2)}, u32[]{:S(2)}) collective-permute-start(bf16[128,768]{1,0:T(8,128)(2,1)} %refs_4_.1), channel_id=1, source_target_pairs={{0,2},{1,3},{2,0},{3,1},{4,6},{5,7},{6,4},{7,5},{8,10},{9,11},{10,... | collective-permute-start | bytes 589832 | tf_op jit(solution)/shard_map/ppermute | solution.py:170
  12.7 14.6 %collective-permute-start.7 = (bf16[128,768]{1,0:T(8,128)(2,1)}, bf16[128,768]{1,0:T(8,128)(2,1)}, u32[]{:S(2)}, u32[]{:S(2)}) collective-permute-start(bf16[128,768]{1,0:T(8,128)(2,1)} %collective-permute-done.6.refs_4_), channel_id=1, source_target_pairs={{0,1},{1,0},{2,3},{3,2},{4,5},{5,4},{6,7},{7,6},{8,9},{9,8},{10,11... | collective-permute-start | bytes 589832 | tf_op jit(solution)/shard_map/ppermute | solution.py:167
  14.1 1.1 %copy-start = (bf16[3,768,128]{2,1,0:T(8,128)(2,1)S(1)}, bf16[3,768,128]{2,1,0:T(8,128)(2,1)}, u32[]{:S(2)}) copy-start(bf16[3,768,128]{2,1,0:T(8,128)(2,1)} %refs_9_.1) | copy-start | bytes 1769476
  15.2 1.1 %copy-start.3 = (bf16[3,768,128]{2,1,0:T(8,128)(2,1)S(1)}, bf16[3,768,128]{2,1,0:T(8,128)(2,1)}, u32[]{:S(2)}) copy-start(bf16[3,768,128]{2,1,0:T(8,128)(2,1)} %refs_7_.1) | copy-start | bytes 1769476
  16.3 0.9 %copy-start.9 = (bf16[1,224,192]{1,2,0:T(8,128)(2,1)S(1)}, bf16[1,224,192]{1,2,0:T(8,128)(2,1)}, u32[]{:S(2)}) copy-start(bf16[1,224,192]{1,2,0:T(8,128)(2,1)} %param.12) | copy-start | bytes 258052
  17.2 0.9 %copy-start.11 = (bf16[192,224]{1,0:T(8,128)(2,1)S(1)}, bf16[192,224]{1,0:T(8,128)(2,1)}, u32[]{:S(2)}) copy-start(bf16[192,224]{1,0:T(8,128)(2,1)} %copy-done.10) | copy-start | bytes 258052
  18.1 0.9 %copy-start.13 = (bf16[192,224]{1,0:T(8,128)(2,1)S(1)}, bf16[192,224]{1,0:T(8,128)(2,1)}, u32[]{:S(2)}) copy-start(bf16[192,224]{1,0:T(8,128)(2,1)} %copy-done.12) | copy-start | bytes 258052
  19.0 0.9 %copy-start.15 = (bf16[192,224]{1,0:T(8,128)(2,1)S(1)}, bf16[192,224]{1,0:T(8,128)(2,1)}, u32[]{:S(2)}) copy-start(bf16[192,224]{1,0:T(8,128)(2,1)} %copy-done.14) | copy-start | bytes 258052
  19.8 13.7 %copy-start.22 = (s32[4,2]{0,1:T(2,128)S(1)}, s32[4,2]{0,1:T(2,128)}, u32[]{:S(2)}) copy-start(s32[4,2]{0,1:T(2,128)} %param.13) | copy-start | bytes 100
  19.8 18.8 %copy-start.20 = (f32[768]{0:T(1024)S(1)}, f32[768]{0:T(1024)}, u32[]{:S(2)}) copy-start(f32[768]{0:T(1024)} %param.16) | copy-start | bytes 9220
  19.8 18.8 %copy-start.4 = (bf16[128,768]{1,0:T(8,128)(2,1)S(1)}, bf16[128,768]{1,0:T(8,128)(2,1)}, u32[]{:S(2)}) copy-start(bf16[128,768]{1,0:T(8,128)(2,1)} %refs_2_.1) | copy-start | bytes 589828
  22.7 0.7 %copy-start.8 = (bf16[224,256]{1,0:T(8,128)(2,1)}, bf16[224,256]{1,0:T(8,128)(2,1)S(1)}, u32[]{:S(2)}) copy-start(bf16[224,256]{1,0:T(8,128)(2,1)S(1)} %get-tuple-element.17) | copy-start | bytes 344068
  23.3 0.7 %copy-start.18 = (f32[112,768]{1,0:T(8,128)}, f32[112,768]{1,0:T(8,128)S(1)}, u32[]{:S(2)}) copy-start(f32[112,768]{1,0:T(8,128)S(1)} %get-tuple-element.15.refs_6_) | copy-start | bytes 1032196
  24.1 0.7 %copy-start.6 = (bf16[128,768]{1,0:T(8,128)(2,1)}, bf16[128,768]{1,0:T(8,128)(2,1)S(1)}, u32[]{:S(2)}) copy-start(bf16[128,768]{1,0:T(8,128)(2,1)S(1)} %collective-permute-done.5.refs_3_) | copy-start | bytes 589828
  24.7 5.1 %collective-permute-start.4 = (bf16[112,256]{1,0:T(8,128)(2,1)}, bf16[112,256]{1,0:T(8,128)(2,1)S(1)}, u32[]{:S(2)}, u32[]{:S(2)}) collective-permute-start(bf16[112,256]{1,0:T(8,128)(2,1)} %get-tuple-element.14.refs_0_), channel_id=1, source_target_pairs={{0,2},{1,3},{2,0},{3,1},{4,6},{5,7},{6,4},{7,5},{8,10},{9,11},{10,... | collective-permute-start | bytes 172040 | tf_op jit(solution)/shard_map/ppermute | solution.py:170
  25.7 8.1 %collective-permute-start.11 = (bf16[224,256]{1,0:T(8,128)(2,1)}, bf16[224,256]{1,0:T(8,128)(2,1)S(1)}, u32[]{:S(2)}, u32[]{:S(2)}) collective-permute-start(bf16[224,256]{1,0:T(8,128)(2,1)} %copy-done.8), channel_id=1, source_target_pairs={{0,4},{4,8},{8,12},{12,0},{1,5},{5,9},{9,13},{13,1},{2,6},{6,10},{... | collective-permute-start | bytes 344072 | tf_op jit(solution)/shard_map/ppermute | solution.py:228
  27.3 10.8 %collective-permute-start.10 = (bf16[224,256]{1,0:T(8,128)(2,1)}, bf16[224,256]{1,0:T(8,128)(2,1)S(1)}, u32[]{:S(2)}, u32[]{:S(2)}) collective-permute-start(bf16[224,256]{1,0:T(8,128)(2,1)} %copy-done.8), channel_id=1, source_target_pairs={{0,8},{4,12},{8,0},{12,4},{1,9},{5,13},{9,1},{13,5},{2,10},{6,14},... | collective-permute-start | bytes 344072 | tf_op jit(solution)/shard_map/ppermute | solution.py:228
  29.9 0.6 copy-start.16
  30.5 7.7 %collective-permute-start.9 = (bf16[224,256]{1,0:T(8,128)(2,1)}, bf16[224,256]{1,0:T(8,128)(2,1)S(1)}, u32[]{:S(2)}, u32[]{:S(2)}) collective-permute-start(bf16[224,256]{1,0:T(8,128)(2,1)} %copy-done.8), channel_id=1, source_target_pairs={{0,12},{4,0},{8,4},{12,8},{1,13},{5,1},{9,5},{13,9},{2,14},{6,2},{... | collective-permute-start | bytes 344072 | tf_op jit(solution)/shard_map/ppermute | solution.py:228
  33.8 9.5 %collective-permute-start.14 = (bf16[224,256]{1,0:T(8,128)(2,1)S(1)}, bf16[224,256]{1,0:T(8,128)(2,1)}, u32[]{:S(2)}, u32[]{:S(2)}) collective-permute-start(bf16[224,256]{1,0:T(8,128)(2,1)S(1)} %collective-permute-done.11.refs_3_), channel_id=1, source_target_pairs={{0,1},{1,0},{2,3},{3,2},{4,5},{5,4},{6,7},{7,6},{8,9},{9,8},{10,11... | collective-permute-start | bytes 344072 | tf_op jit(solution)/shard_map/ppermute | solution.py:167
  38.1 5.4 %collective-permute-start.13 = (bf16[224,256]{1,0:T(8,128)(2,1)S(1)}, bf16[224,256]{1,0:T(8,128)(2,1)}, u32[]{:S(2)}, u32[]{:S(2)}) collective-permute-start(bf16[224,256]{1,0:T(8,128)(2,1)S(1)} %collective-permute-done.10.refs_2_), channel_id=1, source_target_pairs={{0,1},{1,0},{2,3},{3,2},{4,5},{5,4},{6,7},{7,6},{8,9},{9,8},{10,11... | collective-permute-start | bytes 344072 | tf_op jit(solution)/shard_map/ppermute | solution.py:167
  38.2 5.7 %collective-permute-start.12 = (bf16[224,256]{1,0:T(8,128)(2,1)S(1)}, bf16[224,256]{1,0:T(8,128)(2,1)}, u32[]{:S(2)}, u32[]{:S(2)}) collective-permute-start(bf16[224,256]{1,0:T(8,128)(2,1)S(1)} %collective-permute-done.9.refs_1_), channel_id=1, source_target_pairs={{0,1},{1,0},{2,3},{3,2},{4,5},{5,4},{6,7},{7,6},{8,9},{9,8},{10,11... | collective-permute-start | bytes 344072 | tf_op jit(solution)/shard_map/ppermute | solution.py:167
  38.7 0.9 %copy-start.7 = (bf16[128,768]{1,0:T(8,128)(2,1)S(1)}, bf16[128,768]{1,0:T(8,128)(2,1)}, u32[]{:S(2)}) copy-start(bf16[128,768]{1,0:T(8,128)(2,1)} %copy-done.6) | copy-start | bytes 589828
  39.6 0.8 %copy-start.17 = (bf16[112,256]{1,0:T(8,128)(2,1)S(1)}, bf16[112,256]{1,0:T(8,128)(2,1)}, u32[]{:S(2)}) copy-start(bf16[112,256]{1,0:T(8,128)(2,1)} %copy-done.16) | copy-start | bytes 172036
  40.4 1.0 %copy-start.19 = (f32[112,768]{1,0:T(8,128)S(1)}, f32[112,768]{1,0:T(8,128)}, u32[]{:S(2)}) copy-start(f32[112,768]{1,0:T(8,128)} %copy-done.18) | copy-start | bytes 1032196
  41.4 1.9 %copy-start.5 = (bf16[128,768]{1,0:T(8,128)(2,1)S(1)}, bf16[128,768]{1,0:T(8,128)(2,1)}, u32[]{:S(2)}) copy-start(bf16[128,768]{1,0:T(8,128)(2,1)} %refs_4_.1) | copy-start | bytes 589828
  43.3 4.5 %collective-permute-start.16 = (bf16[128,768]{1,0:T(8,128)(2,1)S(1)}, bf16[128,768]{1,0:T(8,128)(2,1)S(1)}, u32[]{:S(2)}, u32[]{:S(2)}) collective-permute-start(bf16[128,768]{1,0:T(8,128)(2,1)S(1)} %copy-done.5), channel_id=1, source_target_pairs={{0,1},{1,0},{2,3},{3,2},{4,5},{5,4},{6,7},{7,6},{8,9},{9,8},{10,11... | collective-permute-start | bytes 589832 | tf_op jit(solution)/shard_map/ppermute | solution.py:167
  43.5 4.3 %collective-permute-start.18 = (bf16[128,768]{1,0:T(8,128)(2,1)}, bf16[128,768]{1,0:T(8,128)(2,1)S(1)}, u32[]{:S(2)}, u32[]{:S(2)}) collective-permute-start(bf16[128,768]{1,0:T(8,128)(2,1)} %collective-permute-done.17.refs_6_), channel_id=1, source_target_pairs={{0,1},{1,0},{2,3},{3,2},{4,5},{5,4},{6,7},{7,6},{8,9},{9,8},{10,11... | collective-permute-start | bytes 589832 | tf_op jit(solution)/shard_map/ppermute | solution.py:167
  43.9 3.9 %copy-start.21 = (f32[768]{0:T(1024)S(1)}, f32[768]{0:T(1024)}, u32[]{:S(2)}) copy-start(f32[768]{0:T(1024)} %param.17) | copy-start | bytes 9220
  43.9 8.9 %copy-start.1 = (bf16[768,768]{1,0:T(8,128)(2,1)S(1)}, bf16[768,768]{1,0:T(8,128)(2,1)}, u32[]{:S(2)}) copy-start(bf16[768,768]{1,0:T(8,128)(2,1)} %refs_10_.1) | copy-start | bytes 3538948
  43.9 8.9 %copy-start.2 = (bf16[768,768]{1,0:T(8,128)(2,1)S(1)}, bf16[768,768]{1,0:T(8,128)(2,1)}, u32[]{:S(2)}) copy-start(bf16[768,768]{1,0:T(8,128)(2,1)} %refs_12_.1) | copy-start | bytes 3538948
  46.4 6.4 %collective-permute-start.15 = (bf16[3,112,256]{2,1,0:T(8,128)(2,1)S(1)}, bf16[3,112,256]{2,1,0:T(8,128)(2,1)S(1)}, u32[]{:S(2)}, u32[]{:S(2)}) collective-permute-start(bf16[3,112,256]{2,1,0:T(8,128)(2,1)S(1)} %shard_map.120.refs_2_), channel_id=1, source_target_pairs={{0,2},{1,3},{2,0},{3,1},{4,6},{5,7},{6,4},{7,5},{8,10},{9,11},{10,... | collective-permute-start | bytes 516104 | tf_op jit(solution)/shard_map/ppermute | solution.py:170
  56.7 4.9 %collective-permute-start.22 = (f32[192,112]{1,0:T(8,128)S(1)}, f32[192,112]{1,0:T(8,128)S(1)}, u32[]{:S(2)}, u32[]{:S(2)}) collective-permute-start(f32[192,112]{1,0:T(8,128)S(1)} %get-tuple-element.21), channel_id=1, source_target_pairs={{0,1},{1,0},{2,3},{3,2},{4,5},{5,4},{6,7},{7,6},{8,9},{9,8},{10,11... | collective-permute-start | bytes 258056 | tf_op jit(solution)/shard_map/ppermute | solution.py:167
  56.8 4.2 %collective-permute-start.21 = (bf16[192,112]{1,0:T(8,128)(2,1)S(1)}, bf16[192,112]{1,0:T(8,128)(2,1)S(1)}, u32[]{:S(2)}, u32[]{:S(2)}) collective-permute-start(bf16[192,112]{1,0:T(8,128)(2,1)S(1)} %get-tuple-element.20), channel_id=1, source_target_pairs={{0,2},{1,3},{2,0},{3,1},{4,6},{5,7},{6,4},{7,5},{8,10},{9,11},{10,... | collective-permute-start | bytes 129032 | tf_op jit(solution)/shard_map/ppermute | solution.py:170
  57.9 3.7 %collective-permute-start.23 = (bf16[192,112]{1,0:T(8,128)(2,1)S(1)}, bf16[192,112]{1,0:T(8,128)(2,1)S(1)}, u32[]{:S(2)}, u32[]{:S(2)}) collective-permute-start(bf16[192,112]{1,0:T(8,128)(2,1)S(1)} %get-tuple-element.22), channel_id=1, source_target_pairs={{0,3},{1,2},{2,1},{3,0},{4,7},{5,6},{6,5},{7,4},{8,11},{9,10},{10,... | collective-permute-start | bytes 129032 | tf_op jit(solution)/shard_map/ppermute | solution.py:170

commit v2 on v1

v2 whole, which is shorter than its diff:
```python
import math

import jax
import jax.numpy as jnp
from jax import lax
from jax.experimental import pallas as pl
from jax.experimental.pallas import tpu as pltpu
from jax.sharding import PartitionSpec as P

HEAD_DIM = 64
ROW_GROUPS = 2
DEGREE = 6
SCALE = 1.0 / math.sqrt(HEAD_DIM)
VMEM = pl.BlockSpec(memory_space=pltpu.VMEM)
SMEM = pl.BlockSpec(memory_space=pltpu.SMEM)
BF16 = jnp.bfloat16
F32 = jnp.float32


def mm(a, b):
    return jnp.dot(a, b, preferred_element_type=F32)


def standardize(x):
    centred = x - jnp.mean(x, axis=-1, keepdims=True)
    variance = jnp.mean(centred * centred, axis=-1, keepdims=True)
    return centred * lax.rsqrt(variance + 1e-06)


def head_attention(q, k, v):
    rows, width = q.shape
    heads = width // HEAD_DIM
    lane_head = lax.broadcasted_iota(jnp.int32, (rows, width), 1) // HEAD_DIM
    zero = jnp.zeros_like(q)
    stacked = jnp.concatenate([jnp.where(lane_head == i, q, zero) for i in range(heads)], axis=0)
    scores = lax.dot_general(stacked, k, (((1,), (1,)), ((), ())), preferred_element_type=F32)
    top = jnp.max(scores, axis=-1, keepdims=True)
    weights = jnp.exp((scores - top) * SCALE)
    total = jnp.sum(weights, axis=-1, keepdims=True)
    weights = (weights * (1.0 / total)).astype(BF16)
    mixed = mm(weights, v)
    context = jnp.zeros((rows, width), F32)
    for i in range(heads):
        context = context + jnp.where(lane_head == i, mixed[i * rows : (i + 1) * rows], 0.0)
    return context


def position():
    here = lax.axis_index("head")
    return here // ROW_GROUPS, lax.rem(here, ROW_GROUPS)


def mark_kernel(block, out):
    out[...] = block[:8, :128].astype(F32)


def self_kernel(groups, *refs):
    blocks = refs[: 2 * groups]
    g_self, g_memory, w_cross, w_own, w_other, out_own, out_other = refs[2 * groups : 2 * groups + 7]
    x_rows, partial, kv, x_full = refs[-4:]
    group, member = position()
    width = blocks[0].shape[0]
    for index in range(2 * groups):
        source = lax.rem(group - index // 2 + groups, groups) * 2
        source = source + (member if index % 2 == 0 else 1 - member)
        x_full[pl.ds(pl.multiple_of(source * width, width), width), :] = blocks[index][...]
    x = x_full[...].astype(F32).T
    rows = x.shape[0] // ROW_GROUPS
    x_rows[...] = jnp.where(member == 0, x[:rows], x[rows:])
    normed = standardize(x)
    memory = (normed * g_memory[...].reshape(1, -1)).astype(BF16)
    kv[:, : kv.shape[1] // 2] = mm(memory, w_cross[1]).astype(BF16)
    kv[:, kv.shape[1] // 2 :] = mm(memory, w_cross[2]).astype(BF16)
    own = (normed * g_self[...].reshape(1, -1)).astype(BF16)
    mine = jnp.where(member == 0, own[:rows], own[rows:])
    q = jnp.concatenate([mm(mine, w_own[0]), mm(mine, w_other[0])], axis=1).astype(BF16)
    k = jnp.concatenate([mm(own, w_own[1]), mm(own, w_other[1])], axis=1).astype(BF16)
    v = jnp.concatenate([mm(own, w_own[2]), mm(own, w_other[2])], axis=1).astype(BF16)
    context = head_attention(q, k, v).astype(BF16)
    width = context.shape[1] // 2
    total = mm(context[:, :width], out_own[...]) + mm(context[:, width:], out_other[...])
    partial[...] = total.astype(BF16)


def query_kernel(x_rows, gain, w_own, w_other, *refs):
    after, kept, given = refs[-3:]
    total = x_rows[...]
    for partial in refs[:-3]:
        total = total + partial[...].astype(F32)
    after[...] = total
    normed = (standardize(total) * gain[...].reshape(1, -1)).astype(BF16)
    kept[...] = mm(normed, w_own[0]).astype(BF16)
    given[...] = mm(normed, w_other[0]).astype(BF16)


def hand_on(passed, handed, sems):
    copies = [pltpu.make_async_copy(passed[i], handed[i], sems.at[i]) for i in range(len(passed))]
    for copy in copies:
        copy.start()
    return copies


def cross_kernel(count, q_own, q_other, *refs):
    passed, refs = refs[:count], refs[count:]
    memories, kept, given = refs[: -3 - count], refs[-3 - count], refs[-2 - count]
    copies = hand_on(passed, refs[len(refs) - 1 - count : -1], refs[-1])
    rows, width = q_own.shape
    q = jnp.concatenate([q_own[...], q_other[...]], axis=0)
    for view, memory in enumerate(memories):
        context = head_attention(q, memory[:, :width], memory[:, width:]).astype(BF16)
        kept[view] = context[:rows]
        given[view] = context[rows:]
    for copy in copies:
        copy.wait()


def other_image(image, step, images):
    return image ^ step if images & (images - 1) == 0 else (image + step) % images


def view_counts(images, pairs):
    image = lax.axis_index("pair")
    counts = []
    for step in range(1, images):
        memory = other_image(image, step, images)
        count = jnp.int32(0)
        for pair in range(pairs.shape[1]):
            first, second = pairs[0, pair], pairs[1, pair]
            named = ((first == image) & (second == memory)) | ((first == memory) & (second == image))
            count = count + jnp.where(named, 1, 0)
        counts.append(count.astype(F32))
    return counts


def mlp_kernel(groups, images, listed, *refs):
    contexts, refs = refs[: 2 * groups], refs[2 * groups :]
    views = contexts[0].shape[0]
    w_out = refs[: 2 * groups]
    after, gain, up_own, up_other, down_own, down_other = refs[2 * groups : 2 * groups + 6]
    outs = refs[2 * groups + 6 : 4 * groups + 6]
    kept, partial = refs[4 * groups + 6 :]
    group, member = position()
    rows = after.shape[0]
    column = after.shape[1] // (2 * groups)
    residual = after[...]
    total = jnp.concatenate([residual] * views, axis=0)
    for source in range(2 * groups):
        held = contexts[source][...].reshape(views * rows, -1)
        total = total + mm(held, w_out[source][...])
    if images:
        share = view_counts(images, listed)
    else:
        share = [listed[view].astype(F32) for view in range(views)]
    keep = jnp.zeros_like(residual)
    for view in range(views):
        keep = keep + share[view] * total[view * rows : (view + 1) * rows]
    kept[...] = keep.T
    normed = (standardize(total) * gain[...].reshape(1, -1)).astype(BF16)
    down = jnp.zeros_like(residual)
    for w_up, w_down in ((up_own, down_own), (up_other, down_other)):
        raw = mm(normed, w_up[...])
        hidden = (0.5 * raw * (1.0 + lax.erf(raw * math.sqrt(0.5)))).astype(BF16).astype(F32)
        added = jnp.zeros((rows, raw.shape[1]), F32)
        for view in range(views):
            added = added + share[view] * hidden[view * rows : (view + 1) * rows]
        down = down + mm(added.astype(BF16), w_down[...])
    partial[...] = down.T
    for step in range(groups):
        target = lax.rem(group + step, groups)
        for other in range(2):
            index = target * 2 + (member if other == 0 else 1 - member)
            here = pl.ds(pl.multiple_of(index * column, column), column)
            piece = partial[here, :]
            if step == 0:
                piece = piece + kept[here, :]
            outs[2 * step + other][...] = piece.astype(outs[2 * step + other].dtype)


def sum_kernel(groups, *refs):
    member = position()[1]
    out = refs[2 * groups]
    rows = refs[0].shape[1]
    mine, theirs = refs[0][...], refs[1][...]
    for step in range(1, groups):
        mine = mine + refs[2 * step][...].astype(F32)
        theirs = theirs + refs[2 * step + 1][...].astype(F32)
    out[:, :rows] = jnp.where(member == 0, mine, theirs)
    out[:, rows:] = jnp.where(member == 0, theirs, mine)


def body(
    features,
    pair_list,
    gain_self,
    gain_memory,
    gain_cross,
    gain_mlp,
    w_self_qkv,
    w_self_out,
    w_cross_qkv,
    w_cross_out,
    w_up,
    w_down,
):
    head = lax.axis_size("head")
    groups = head // ROW_GROUPS
    images = lax.axis_size("pair")
    tokens, column = features.shape[1:]
    model = gain_self.shape[0]
    rows = tokens // ROW_GROUPS
    att = w_self_out.shape[0]

    def swap(value):
        return lax.ppermute(value, "head", [(i, i ^ 1) for i in range(head)])

    def turn(value, step, cross=0):
        return lax.ppermute(
            value,
            "head",
            [
                (i, ((i // 2 + step) % groups) * 2 + ((i % 2) ^ cross))
                for i in range(head)
            ],
        )

    def call(kernel, out_shape, args, scratch=(), smem=0, flops=0, moved=0):
        return pl.pallas_call(
            kernel,
            out_shape=out_shape,
            in_specs=[SMEM] * smem + [VMEM] * (len(args) - smem),
            out_specs=jax.tree.map(lambda _: VMEM, out_shape),
            scratch_shapes=list(scratch),
            compiler_params=pltpu.CompilerParams(vmem_limit_bytes=16 * 2**20),
            cost_estimate=pl.CostEstimate(flops=flops, bytes_accessed=moved, transcendentals=0),
        )(*args)

    def exchange(kept, given):
        blocks = [kept, swap(given)]
        for step in range(1, groups):
            blocks += [turn(kept, step), turn(given, step, 1)]
        return blocks

    shape = jax.ShapeDtypeStruct
    features = features[0].T
    blocks = [features, swap(features)]
    for step in range(1, groups):
        arrived = turn(features, step)
        blocks += [arrived, swap(arrived)]
    turned = [turn(w_cross_out, step) for step in range(1, groups)]
    self_other, self_out_other, cross_other = swap(w_self_qkv), swap(w_self_out), swap(w_cross_qkv)
    up_other, down_other, cross_out_other = swap(w_up), swap(w_down), swap(w_cross_out)

    mark = call(mark_kernel, shape((8, 128), F32), [blocks[1]], flops=3 * 10**9)
    x_rows, partial, kv = call(
        lambda *refs: self_kernel(groups, *refs),
        [shape((rows, model), F32), shape((rows, model), BF16), shape((tokens, 2 * att), BF16)],
        [
            *blocks,
            gain_self,
            gain_memory,
            w_cross_qkv,
            w_self_qkv,
            self_other,
            w_self_out,
            self_out_other,
            mark,
            cross_other,
            up_other,
            down_other,
        ],
        scratch=[pltpu.VMEM((model, tokens), BF16)],
        flops=10**8,
    )

    static = images - 1 <= DEGREE
    if static:
        views = images - 1
        listed = pair_list.T
        kv_own = [
            lax.ppermute(kv, "pair", [(other_image(i, step, images), i) for i in range(images)])
            for step in range(1, images)
        ]
    else:
        views = min(DEGREE, pair_list.shape[0])
        image = lax.axis_index("pair")
        first, second = pair_list[:, 0], pair_list[:, 1]
        named = (first == image) | (second == image)
        partner = jnp.where(first == image, second, first)
        rank = jnp.cumsum(named.astype(jnp.int32)) - 1
        hit = named[None, :] & (rank[None, :] == jnp.arange(views)[:, None])
        memories = jnp.sum(jnp.where(hit, partner[None, :], 0), axis=1)
        listed = jnp.any(hit, axis=1).astype(jnp.int32)
        gathered = lax.all_gather(kv, "pair", axis=0, tiled=False)
        kv_own = [lax.dynamic_index_in_dim(gathered, memories[view], 0, False) for view in range(views)]
    partials = [partial] + [turn(partial, step) for step in range(1, groups)]
    after, q_own, q_given = call(
        query_kernel,
        [shape((rows, model), F32)] + [shape((rows, att), BF16)] * 2,
        [x_rows, gain_cross, w_cross_qkv, cross_other, *partials],
        flops=10**8,
    )
    kept, given, *handed = call(
        lambda *refs: cross_kernel(groups - 1, *refs),
        [shape((views, rows, att), BF16)] * 2 + [shape(value.shape, BF16) for value in turned],
        [q_own, swap(q_given), *turned, *kv_own],
        scratch=[pltpu.SemaphoreType.DMA((max(groups - 1, 1),))],
        flops=10**8,
    )
    contexts = exchange(kept, given)
    cross_out = [w_cross_out, cross_out_other]
    for step in range(groups - 1):
        cross_out += [turned[step], swap(handed[step])]
    pieces = call(
        lambda *refs: mlp_kernel(groups, images if static else 0, *refs),
        [shape((column, rows), F32)] * 2 + [shape((column, rows), BF16)] * (2 * groups - 2),
        [listed, *contexts, *cross_out, after, gain_mlp, w_up, up_other, w_down, down_other],
        scratch=[pltpu.VMEM((model, rows), F32)] * 2,
        smem=1,
        flops=3 * 10**9,
    )
    arrived = [pieces[0], swap(pieces[1])]
    for step in range(1, groups):
        arrived += [turn(pieces[2 * step], step), turn(pieces[2 * step + 1], step, 1)]
    summed = call(lambda *refs: sum_kernel(groups, *refs), shape((column, tokens), F32), arrived)
    return summed.T[None]


def solution(mesh):
    in_specs = (
        P(("grp", "pair"), None, "head"),
        P("grp", None),
        P(),
        P(),
        P(),
        P(),
        P(None, None, "head"),
        P("head", None),
        P(None, None, "head"),
        P("head", None),
        P(None, "head"),
        P("head", None),
    )
    out_specs = P(("grp", "pair"), None, "head")
    return jax.shard_map(body, mesh=mesh, in_specs=in_specs, out_specs=out_specs, check_vma=False)
```

time: 63.2 us -> 47.4 us (0.75)
  local copies, waits for them, and re-layouts: 15.4 us -> 0.05 us
  waiting for transfers between devices: 16.8 us -> 24 us
  starting transfers between devices: 17.9 us -> 14.9 us
  Pallas kernels: 11.1 us -> 8.16 us
  other arithmetic: 1.17 us -> 0 us
    unnamed x46 -> x24, local copies, waits for them, and re-layouts: 13 us -> 0.05 us
    ppermute x14 -> x12, waiting for transfers between devices: 0.04 us -> 4.17 us  [swap(): return lax.ppermute(value, 'head', [(i, i ^ 1) for i in range(head)])]
    ppermute x7, waiting for transfers between devices: 12.1 us -> 15.1 us  [turn(): lax.ppermute(value, 'head', [(i, (i // 2 + step) % groups * 2 + (i % 2 ^...]
    pallas_call x4 -> x6, Pallas kernels: 11.1 us -> 8.16 us  [call(): pl.pallas_call(kernel, out_shape=out_shape, in_specs=[SMEM] * smem + [VME...]
    ppermute x3, starting transfers between devices: 7.2 us -> 4.43 us  [body(): lax.ppermute(kv, 'pair', [(other_image(i, step, images), i) for i in rang...]
    reshape x4 -> x0, local copies, waits for them, and re-layouts: 1.39 us -> none  [body(): g.reshape(1, model)]
    squeeze x1 -> x0, local copies, waits for them, and re-layouts: 0.94 us -> none  [body(): query_own = w_cross_qkv[0]]
    broadcast_in_dim x1 -> x0, other arithmetic: 0.8 us -> none  [body(): return jnp.concatenate([low, high], axis=1).T[None]]
  transfers between devices with their start and end apart: 24 -> 22, of which waited for: 8 -> 11; matrix products, arithmetic and copies ran while one was open for 4% -> 0% of each run, Pallas kernels for 11% -> 4%
where the time goes in v2:
time: 47.4 us; the launch traced here: 47.3 us
  waiting for transfers between devices  24 us (51%)
  starting transfers between devices  14.9 us (31%)
  Pallas kernels  8.16 us (17%)
    ppermute x7, waiting for transfers between devices, turn(): lax.ppermute(value, 'head', [(i, (i // 2 + step) % groups * 2 + (i % 2 ^...  15.1 us
    ppermute x7, starting transfers between devices, turn(): lax.ppermute(value, 'head', [(i, (i // 2 + step) % groups * 2 + (i % 2 ^...  8.36 us
    pallas_call x6, Pallas kernels, call(): pl.pallas_call(kernel, out_shape=out_shape, in_specs=[SMEM] * smem + [VME...  8.16 us
    ppermute x3, waiting for transfers between devices, body(): lax.ppermute(kv, 'pair', [(other_image(i, step, images), i) for i in rang...  4.67 us
    ppermute x3, starting transfers between devices, body(): lax.ppermute(kv, 'pair', [(other_image(i, step, images), i) for i in rang...  4.43 us
    ppermute x12, waiting for transfers between devices, swap(): return lax.ppermute(value, 'head', [(i, i ^ 1) for i in range(head)])  4.17 us
    ppermute x12, starting transfers between devices, swap(): return lax.ppermute(value, 'head', [(i, i ^ 1) for i in range(head)])  2.15 us
  transfers between devices with their start and end apart: 22, of which 11 were waited for; matrix products, arithmetic and copies ran while one was open for 0% of the time, Pallas kernels for 4%

profile of v2, /device:TPU:0, one launch (start us, length us, event | category | flops | bytes accessed | tf_op | source)
XLA Modules:
  0.0 47.3 jit_solution(1171645033392076252)
XLA Ops:
  0.0 0.5 collective-permute-start.6
  0.5 0.1 collective-permute-start.7
  0.5 0.5 collective-permute-start.5
  1.0 0.1 collective-permute-start.3
  1.0 0.0 copy-start.4
  1.0 0.0 copy-start.5
  1.1 3.0 %collective-permute-start.1 = (bf16[192,224]{1,0:T(8,128)(2,1)}, bf16[192,224]{1,0:T(8,128)(2,1)S(1)}, u32[]{:S(2)}, u32[]{:S(2)}) collective-permute-start(bf16[192,224]{1,0:T(8,128)(2,1)} %bitcast.7), channel_id=1, source_target_pairs={{0,2},{1,3},{2,0},{3,1},{4,6},{5,7},{6,4},{7,5},{8,10},{9,11},{10,... | collective-permute-start | bytes 258056 | tf_op jit(solution)/shard_map/ppermute | solution.py:217
  4.1 3.2 %collective-permute-done.1.refs_2_ = bf16[192,224]{1,0:T(8,128)(2,1)S(1)} collective-permute-done((bf16[192,224]{1,0:T(8,128)(2,1)}, bf16[192,224]{1,0:T(8,128)(2,1)S(1)}, u32[]{:S(2)}, u32[]{:S(2)}) %collective-permute-start.1) | collective-permute-done | bytes 86048 | tf_op jit(solution)/shard_map/ppermute | solution.py:217
  7.2 0.0 collective-permute-start
  7.2 1.5 %collective-permute-done.block.refs_1_ = bf16[192,224]{1,0:T(8,128)(2,1)S(1)} collective-permute-done((bf16[192,224]{1,0:T(8,128)(2,1)}, bf16[192,224]{1,0:T(8,128)(2,1)S(1)}, u32[]{:S(2)}, u32[]{:S(2)}) %collective-permute-start) | collective-permute-done | bytes 86048 | tf_op jit(solution)/shard_map/ppermute | solution.py:214
  8.8 0.2 collective-permute-start.2
  8.9 1.1 %collective-permute-done.2.refs_3_ = bf16[192,224]{1,0:T(8,128)(2,1)S(1)} collective-permute-done((bf16[192,224]{1,0:T(8,128)(2,1)S(1)}, bf16[192,224]{1,0:T(8,128)(2,1)S(1)}, u32[]{:S(2)}, u32[]{:S(2)}) %collective-permute-start.2) | collective-permute-done | bytes 86048 | tf_op jit(solution)/shard_map/ppermute | solution.py:214
  10.1 0.2 collective-permute-start.4
  10.2 1.5 %collective-permute-done.4.refs_10_ = bf16[128,768]{1,0:T(8,128)(2,1)S(1)} collective-permute-done((bf16[128,768]{1,0:T(8,128)(2,1)}, bf16[128,768]{1,0:T(8,128)(2,1)S(1)}, u32[]{:S(2)}, u32[]{:S(2)}) %collective-permute-start.4) | collective-permute-done | bytes 196640 | tf_op jit(solution)/shard_map/ppermute | solution.py:214
  11.7 0.0 collective-permute-done.5.refs_12_.w_other
  11.7 0.0 collective-permute-done.3.refs_8_
  11.7 0.0 collective-permute-done.6.refs_13_.refs_12_
  11.7 0.0 collective-permute-done.7.refs_14_
  11.7 0.0 copy-done
  11.7 0.0 copy-done.1
  11.8 0.0 copy-done.2
  11.8 0.0 copy-done.3
  11.8 0.0 copy-done.4
  11.8 0.0 copy-done.5
  11.8 1.9 %shard_map.119 = (f32[112,768]{1,0:T(8,128)S(1)}, bf16[112,768]{1,0:T(8,128)(2,1)S(1)}, bf16[224,256]{1,0:T(8,128)(2,1)S(1)}) custom-call(bf16[192,224]{1,0:T(8,128)(2,1)S(1)} %bitcast.9, bf16[192,224]{1,0:T(8,128)(2,1)S(1)} %collective-permute-done.block.refs_1_, bf16[192,224]{1,0:T(8,128)(2,1)S(1)} %collective-permute-done.1.refs_2_, ...), custom_call_target="tpu_custom_call" | custom-call | flops 100000000 | tf_op jit(solution)/shard_map/pallas_call | solution.py:227
  13.6 1.8 %collective-permute-start.8 = (bf16[112,768]{1,0:T(8,128)(2,1)S(1)}, bf16[112,768]{1,0:T(8,128)(2,1)S(1)}, u32[]{:S(2)}, u32[]{:S(2)}) collective-permute-start(bf16[112,768]{1,0:T(8,128)(2,1)S(1)} %get-tuple-element.19.refs_0_), channel_id=1, source_target_pairs={{0,2},{1,3},{2,0},{3,1},{4,6},{5,7},{6,4},{7,5},{8,10},{9,11},{10,... | collective-permute-start | bytes 516104 | tf_op jit(solution)/shard_map/ppermute | solution.py:217
  15.5 0.0 copy-done.9
  15.5 0.3 collective-permute-start.10
  15.7 1.8 %collective-permute-start.11 = (bf16[224,256]{1,0:T(8,128)(2,1)S(1)}, bf16[224,256]{1,0:T(8,128)(2,1)S(1)}, u32[]{:S(2)}, u32[]{:S(2)}) collective-permute-start(bf16[224,256]{1,0:T(8,128)(2,1)S(1)} %get-tuple-element.22), channel_id=1, source_target_pairs={{4,0},{0,4},{12,8},{8,12},{5,1},{1,5},{13,9},{9,13},{6,2},{2,6},{1... | collective-permute-start | bytes 344072 | tf_op jit(solution)/shard_map/ppermute | solution.py:280
  17.6 2.6 %collective-permute-start.12 = (bf16[224,256]{1,0:T(8,128)(2,1)S(1)}, bf16[224,256]{1,0:T(8,128)(2,1)S(1)}, u32[]{:S(2)}, u32[]{:S(2)}) collective-permute-start(bf16[224,256]{1,0:T(8,128)(2,1)S(1)} %get-tuple-element.22), channel_id=1, source_target_pairs={{8,0},{12,4},{0,8},{4,12},{9,1},{13,5},{1,9},{5,13},{10,2},{14,6},... | collective-permute-start | bytes 344072 | tf_op jit(solution)/shard_map/ppermute | solution.py:280
  20.2 0.0 collective-permute-start.13
  20.2 0.8 %collective-permute-done.8.refs_1_ = bf16[112,768]{1,0:T(8,128)(2,1)S(1)} collective-permute-done((bf16[112,768]{1,0:T(8,128)(2,1)S(1)}, bf16[112,768]{1,0:T(8,128)(2,1)S(1)}, u32[]{:S(2)}, u32[]{:S(2)}) %collective-permute-start.8) | collective-permute-done | bytes 172064 | tf_op jit(solution)/shard_map/ppermute | solution.py:217
  20.9 0.0 copy-done.6
  20.9 0.0 copy-start.11
  21.0 0.4 shard_map.120
  21.4 0.1 collective-permute-start.9
  21.5 2.9 %collective-permute-done.10.refs_2_.refs_7_ = bf16[128,768]{1,0:T(8,128)(2,1)S(1)} collective-permute-done((bf16[128,768]{1,0:T(8,128)(2,1)S(1)}, bf16[128,768]{1,0:T(8,128)(2,1)S(1)}, u32[]{:S(2)}, u32[]{:S(2)}) %collective-permute-start.10) | collective-permute-done | bytes 196640 | tf_op jit(solution)/shard_map/ppermute | solution.py:217
  24.4 0.0 collective-permute-start.17
  24.4 0.0 collective-permute-done.11.refs_3_
  24.4 4.7 %collective-permute-done.12.refs_4_ = bf16[224,256]{1,0:T(8,128)(2,1)S(1)} collective-permute-done((bf16[224,256]{1,0:T(8,128)(2,1)S(1)}, bf16[224,256]{1,0:T(8,128)(2,1)S(1)}, u32[]{:S(2)}, u32[]{:S(2)}) %collective-permute-start.12) | collective-permute-done | bytes 114720 | tf_op jit(solution)/shard_map/ppermute | solution.py:280
  29.0 0.0 collective-permute-done.13.refs_5_
  29.0 0.0 collective-permute-done.9.refs_1_
  29.1 1.5 %shard_map.121 = (bf16[3,112,128]{2,1,0:T(8,128)(2,1)S(1)}, bf16[3,112,128]{2,1,0:T(8,128)(2,1)S(1)}, bf16[128,768]{1,0:T(8,128)(2,1)S(1)}) custom-call(bf16[112,128]{1,0:T(8,128)(2,1)S(1)} %get-tuple-element.20.refs_0_, bf16[112,128]{1,0:T(8,128)(2,1)S(1)} %collective-permute-done.9.refs_1_, bf16[128,768]{1,0:T(8,128)(2,1)S(1)} %collective-permute-done.10.refs_2_.refs_7_, ...), custom_call_target="tpu_custom_call" | custom-call | flops 100000000 | tf_op jit(solution)/shard_map/pallas_call | solution.py:227
  30.6 0.1 collective-permute-start.18
  30.7 0.5 %collective-permute-start.14 = (bf16[3,112,128]{2,1,0:T(8,128)(2,1)S(1)}, bf16[3,112,128]{2,1,0:T(8,128)(2,1)S(1)}, u32[]{:S(2)}, u32[]{:S(2)}) collective-permute-start(bf16[3,112,128]{2,1,0:T(8,128)(2,1)S(1)} %get-tuple-element.24), channel_id=1, source_target_pairs={{0,1},{1,0},{2,3},{3,2},{4,5},{5,4},{6,7},{7,6},{8,9},{9,8},{10,11... | collective-permute-start | bytes 258056 | tf_op jit(solution)/shard_map/ppermute | solution.py:214
  31.2 1.5 %collective-permute-start.15 = (bf16[3,112,128]{2,1,0:T(8,128)(2,1)S(1)}, bf16[3,112,128]{2,1,0:T(8,128)(2,1)S(1)}, u32[]{:S(2)}, u32[]{:S(2)}) collective-permute-start(bf16[3,112,128]{2,1,0:T(8,128)(2,1)S(1)} %get-tuple-element.23.refs_1_), channel_id=1, source_target_pairs={{0,2},{1,3},{2,0},{3,1},{4,6},{5,7},{6,4},{7,5},{8,10},{9,11},{10,... | collective-permute-start | bytes 258056 | tf_op jit(solution)/shard_map/ppermute | solution.py:217
  32.7 0.0 collective-permute-start.16
  32.7 0.0 collective-permute-done.17.refs_6_
  32.7 0.0 collective-permute-done.14.refs_2_
  32.7 3.1 %collective-permute-done.15.refs_3_ = bf16[3,112,128]{2,1,0:T(8,128)(2,1)S(1)} collective-permute-done((bf16[3,112,128]{2,1,0:T(8,128)(2,1)S(1)}, bf16[3,112,128]{2,1,0:T(8,128)(2,1)S(1)}, u32[]{:S(2)}, u32[]{:S(2)}) %collective-permute-start.15) | collective-permute-done | bytes 86048 | tf_op jit(solution)/shard_map/ppermute | solution.py:217
  35.7 1.7 %collective-permute-done.16.refs_4_ = bf16[3,112,128]{2,1,0:T(8,128)(2,1)S(1)} collective-permute-done((bf16[3,112,128]{2,1,0:T(8,128)(2,1)S(1)}, bf16[3,112,128]{2,1,0:T(8,128)(2,1)S(1)}, u32[]{:S(2)}, u32[]{:S(2)}) %collective-permute-start.16) | collective-permute-done | bytes 86048 | tf_op jit(solution)/shard_map/ppermute | solution.py:217
  37.5 0.0 collective-permute-done.18.refs_8_
  37.5 0.0 copy-done.7
  37.5 0.0 copy-done.8
  37.5 0.0 copy-done.10
  37.5 0.0 copy-done.11
  37.5 3.6 %shard_map.122 = (f32[192,112]{1,0:T(8,128)S(1)}, f32[192,112]{1,0:T(8,128)S(1)}, bf16[192,112]{1,0:T(8,128)(2,1)S(1)}, bf16[192,112]{1,0:T(8,128)(2,1)S(1)}) custom-call(s32[2,4]{1,0:T(2,128)S(1)} %bitcast.10, bf16[3,112,128]{2,1,0:T(8,128)(2,1)S(1)} %get-tuple-element.23.refs_1_, bf16[3,112,128]{2,1,0:T(8,128)(2,1)S(1)} %collective-permute-done.14.refs_2_, ...), custom_call_target="tpu_custom_call" | custom-call | flops 3000000000 | tf_op jit(solution)/shard_map/pallas_call | solution.py:227
  41.1 0.2 collective-permute-start.19
  41.2 1.3 %collective-permute-start.20 = (bf16[192,112]{1,0:T(8,128)(2,1)S(1)}, bf16[192,112]{1,0:T(8,128)(2,1)S(1)}, u32[]{:S(2)}, u32[]{:S(2)}) collective-permute-start(bf16[192,112]{1,0:T(8,128)(2,1)S(1)} %get-tuple-element.29), channel_id=1, source_target_pairs={{0,2},{1,3},{2,0},{3,1},{4,6},{5,7},{6,4},{7,5},{8,10},{9,11},{10,... | collective-permute-start | bytes 129032 | tf_op jit(solution)/shard_map/ppermute | solution.py:217
  42.5 0.5 %collective-permute-start.21 = (bf16[192,112]{1,0:T(8,128)(2,1)S(1)}, bf16[192,112]{1,0:T(8,128)(2,1)S(1)}, u32[]{:S(2)}, u32[]{:S(2)}) collective-permute-start(bf16[192,112]{1,0:T(8,128)(2,1)S(1)} %get-tuple-element.30), channel_id=1, source_target_pairs={{0,3},{1,2},{2,1},{3,0},{4,7},{5,6},{6,5},{7,4},{8,11},{9,10},{10,... | collective-permute-start | bytes 129032 | tf_op jit(solution)/shard_map/ppermute | solution.py:217
  43.0 2.3 %collective-permute-done.20.refs_2_ = bf16[192,112]{1,0:T(8,128)(2,1)S(1)} collective-permute-done((bf16[192,112]{1,0:T(8,128)(2,1)S(1)}, bf16[192,112]{1,0:T(8,128)(2,1)S(1)}, u32[]{:S(2)}, u32[]{:S(2)}) %collective-permute-start.20) | collective-permute-done | bytes 43040 | tf_op jit(solution)/shard_map/ppermute | solution.py:217
  45.3 1.2 %collective-permute-done.21.refs_3_ = bf16[192,112]{1,0:T(8,128)(2,1)S(1)} collective-permute-done((bf16[192,112]{1,0:T(8,128)(2,1)S(1)}, bf16[192,112]{1,0:T(8,128)(2,1)S(1)}, u32[]{:S(2)}, u32[]{:S(2)}) %collective-permute-start.21) | collective-permute-done | bytes 43040 | tf_op jit(solution)/shard_map/ppermute | solution.py:217
  46.5 0.0 collective-permute-done.19.refs_1_
  46.5 0.8 %shard_map.123 = f32[192,224]{1,0:T(8,128)} custom-call(f32[192,112]{1,0:T(8,128)S(1)} %get-tuple-element.27.refs_0_, f32[192,112]{1,0:T(8,128)S(1)} %collective-permute-done.19.refs_1_, bf16[192,112]{1,0:T(8,128)(2,1)S(1)} %collective-permute-done.20.refs_2_, bf16[192,112]{1,0:T(8,128)(2,1)S(1)} %collective-permute-done.21.refs_3_), custom_call_target="tpu_custom_call" | custom-call | tf_op jit(solution)/shard_map/pallas_call | solution.py:227
  (10 shorter events, 0.0 us)
Async XLA Ops:
  0.0 11.7 %collective-permute-start.6 = (bf16[768,768]{1,0:T(8,128)(2,1)}, bf16[768,768]{1,0:T(8,128)(2,1)S(1)}, u32[]{:S(2)}, u32[]{:S(2)}) collective-permute-start(bf16[768,768]{1,0:T(8,128)(2,1)} %refs_11_.1), channel_id=1, source_target_pairs={{0,1},{1,0},{2,3},{3,2},{4,5},{5,4},{6,7},{7,6},{8,9},{9,8},{10,11... | collective-permute-start | bytes 3538952 | tf_op jit(solution)/shard_map/ppermute | solution.py:214
  0.5 11.3 %collective-permute-start.7 = (bf16[768,768]{1,0:T(8,128)(2,1)}, bf16[768,768]{1,0:T(8,128)(2,1)S(1)}, u32[]{:S(2)}, u32[]{:S(2)}) collective-permute-start(bf16[768,768]{1,0:T(8,128)(2,1)} %refs_13_.1), channel_id=1, source_target_pairs={{0,1},{1,0},{2,3},{3,2},{4,5},{5,4},{6,7},{7,6},{8,9},{9,8},{10,11... | collective-permute-start | bytes 3538952 | tf_op jit(solution)/shard_map/ppermute | solution.py:214
  0.5 11.2 %collective-permute-start.5 = (bf16[3,768,128]{2,1,0:T(8,128)(2,1)}, bf16[3,768,128]{2,1,0:T(8,128)(2,1)S(1)}, u32[]{:S(2)}, u32[]{:S(2)}) collective-permute-start(bf16[3,768,128]{2,1,0:T(8,128)(2,1)} %w_own.1), channel_id=1, source_target_pairs={{0,1},{1,0},{2,3},{3,2},{4,5},{5,4},{6,7},{7,6},{8,9},{9,8},{10,11... | collective-permute-start | bytes 1769480 | tf_op jit(solution)/shard_map/ppermute | solution.py:214
  1.0 10.7 %collective-permute-start.3 = (bf16[3,768,128]{2,1,0:T(8,128)(2,1)}, bf16[3,768,128]{2,1,0:T(8,128)(2,1)S(1)}, u32[]{:S(2)}, u32[]{:S(2)}) collective-permute-start(bf16[3,768,128]{2,1,0:T(8,128)(2,1)} %refs_7_.1), channel_id=1, source_target_pairs={{0,1},{1,0},{2,3},{3,2},{4,5},{5,4},{6,7},{7,6},{8,9},{9,8},{10,11... | collective-permute-start | bytes 1769480 | tf_op jit(solution)/shard_map/ppermute | solution.py:214
  1.0 10.7 %copy-start = (bf16[3,768,128]{2,1,0:T(8,128)(2,1)S(1)}, bf16[3,768,128]{2,1,0:T(8,128)(2,1)}, u32[]{:S(2)}) copy-start(bf16[3,768,128]{2,1,0:T(8,128)(2,1)} %w_own.1) | copy-start | bytes 1769476
  1.0 10.7 %copy-start.1 = (bf16[3,768,128]{2,1,0:T(8,128)(2,1)S(1)}, bf16[3,768,128]{2,1,0:T(8,128)(2,1)}, u32[]{:S(2)}) copy-start(bf16[3,768,128]{2,1,0:T(8,128)(2,1)} %refs_7_.1) | copy-start | bytes 1769476
  1.0 10.7 %copy-start.2 = (bf16[128,768]{1,0:T(8,128)(2,1)S(1)}, bf16[128,768]{1,0:T(8,128)(2,1)}, u32[]{:S(2)}) copy-start(bf16[128,768]{1,0:T(8,128)(2,1)} %refs_9_.1) | copy-start | bytes 589828
  1.0 10.7 %copy-start.3 = (bf16[1,224,192]{1,2,0:T(8,128)(2,1)S(1)}, bf16[1,224,192]{1,2,0:T(8,128)(2,1)}, u32[]{:S(2)}) copy-start(bf16[1,224,192]{1,2,0:T(8,128)(2,1)} %param.12) | copy-start | bytes 258052
  1.0 10.7 %copy-start.4 = (f32[768]{0:T(1024)S(1)}, f32[768]{0:T(1024)}, u32[]{:S(2)}) copy-start(f32[768]{0:T(1024)} %refs_4_.1) | copy-start | bytes 9220
  1.0 10.7 %copy-start.5 = (f32[768]{0:T(1024)S(1)}, f32[768]{0:T(1024)}, u32[]{:S(2)}) copy-start(f32[768]{0:T(1024)} %refs_5_.2) | copy-start | bytes 9220
  1.1 6.2 %collective-permute-start.1 = (bf16[192,224]{1,0:T(8,128)(2,1)}, bf16[192,224]{1,0:T(8,128)(2,1)S(1)}, u32[]{:S(2)}, u32[]{:S(2)}) collective-permute-start(bf16[192,224]{1,0:T(8,128)(2,1)} %bitcast.7), channel_id=1, source_target_pairs={{0,2},{1,3},{2,0},{3,1},{4,6},{5,7},{6,4},{7,5},{8,10},{9,11},{10,... | collective-permute-start | bytes 258056 | tf_op jit(solution)/shard_map/ppermute | solution.py:217
  7.2 1.5 %collective-permute-start = (bf16[192,224]{1,0:T(8,128)(2,1)}, bf16[192,224]{1,0:T(8,128)(2,1)S(1)}, u32[]{:S(2)}, u32[]{:S(2)}) collective-permute-start(bf16[192,224]{1,0:T(8,128)(2,1)} %bitcast.8), channel_id=1, source_target_pairs={{0,1},{1,0},{2,3},{3,2},{4,5},{5,4},{6,7},{7,6},{8,9},{9,8},{10,11... | collective-permute-start | bytes 258056 | tf_op jit(solution)/shard_map/ppermute | solution.py:214
  8.8 1.3 %collective-permute-start.2 = (bf16[192,224]{1,0:T(8,128)(2,1)S(1)}, bf16[192,224]{1,0:T(8,128)(2,1)S(1)}, u32[]{:S(2)}, u32[]{:S(2)}) collective-permute-start(bf16[192,224]{1,0:T(8,128)(2,1)S(1)} %collective-permute-done.1.refs_2_), channel_id=1, source_target_pairs={{0,1},{1,0},{2,3},{3,2},{4,5},{5,4},{6,7},{7,6},{8,9},{9,8},{10,11... | collective-permute-start | bytes 258056 | tf_op jit(solution)/shard_map/ppermute | solution.py:214
  10.1 1.7 %collective-permute-start.4 = (bf16[128,768]{1,0:T(8,128)(2,1)}, bf16[128,768]{1,0:T(8,128)(2,1)S(1)}, u32[]{:S(2)}, u32[]{:S(2)}) collective-permute-start(bf16[128,768]{1,0:T(8,128)(2,1)} %refs_9_.1), channel_id=1, source_target_pairs={{0,1},{1,0},{2,3},{3,2},{4,5},{5,4},{6,7},{7,6},{8,9},{9,8},{10,11... | collective-permute-start | bytes 589832 | tf_op jit(solution)/shard_map/ppermute | solution.py:214
  10.2 5.2 %copy-start.9 = (bf16[128,768]{1,0:T(8,128)(2,1)S(1)}, bf16[128,768]{1,0:T(8,128)(2,1)}, u32[]{:S(2)}) copy-start(bf16[128,768]{1,0:T(8,128)(2,1)} %refs_5_.3) | copy-start | bytes 589828
  10.2 10.7 %copy-start.6 = (f32[768]{0:T(1024)S(1)}, f32[768]{0:T(1024)}, u32[]{:S(2)}) copy-start(f32[768]{0:T(1024)} %gain.1) | copy-start | bytes 9220
  13.6 7.3 %collective-permute-start.8 = (bf16[112,768]{1,0:T(8,128)(2,1)S(1)}, bf16[112,768]{1,0:T(8,128)(2,1)S(1)}, u32[]{:S(2)}, u32[]{:S(2)}) collective-permute-start(bf16[112,768]{1,0:T(8,128)(2,1)S(1)} %get-tuple-element.19.refs_0_), channel_id=1, source_target_pairs={{0,2},{1,3},{2,0},{3,1},{4,6},{5,7},{6,4},{7,5},{8,10},{9,11},{10,... | collective-permute-start | bytes 516104 | tf_op jit(solution)/shard_map/ppermute | solution.py:217
  15.5 8.9 %collective-permute-start.10 = (bf16[128,768]{1,0:T(8,128)(2,1)S(1)}, bf16[128,768]{1,0:T(8,128)(2,1)S(1)}, u32[]{:S(2)}, u32[]{:S(2)}) collective-permute-start(bf16[128,768]{1,0:T(8,128)(2,1)S(1)} %copy-done.9), channel_id=1, source_target_pairs={{0,2},{1,3},{2,0},{3,1},{4,6},{5,7},{6,4},{7,5},{8,10},{9,11},{10,... | collective-permute-start | bytes 589832 | tf_op jit(solution)/shard_map/ppermute | solution.py:217
  15.7 8.6 %collective-permute-start.11 = (bf16[224,256]{1,0:T(8,128)(2,1)S(1)}, bf16[224,256]{1,0:T(8,128)(2,1)S(1)}, u32[]{:S(2)}, u32[]{:S(2)}) collective-permute-start(bf16[224,256]{1,0:T(8,128)(2,1)S(1)} %get-tuple-element.22), channel_id=1, source_target_pairs={{4,0},{0,4},{12,8},{8,12},{5,1},{1,5},{13,9},{9,13},{6,2},{2,6},{1... | collective-permute-start | bytes 344072 | tf_op jit(solution)/shard_map/ppermute | solution.py:280
  17.6 11.5 %collective-permute-start.12 = (bf16[224,256]{1,0:T(8,128)(2,1)S(1)}, bf16[224,256]{1,0:T(8,128)(2,1)S(1)}, u32[]{:S(2)}, u32[]{:S(2)}) collective-permute-start(bf16[224,256]{1,0:T(8,128)(2,1)S(1)} %get-tuple-element.22), channel_id=1, source_target_pairs={{8,0},{12,4},{0,8},{4,12},{9,1},{13,5},{1,9},{5,13},{10,2},{14,6},... | collective-permute-start | bytes 344072 | tf_op jit(solution)/shard_map/ppermute | solution.py:280
  20.2 8.9 %collective-permute-start.13 = (bf16[224,256]{1,0:T(8,128)(2,1)S(1)}, bf16[224,256]{1,0:T(8,128)(2,1)S(1)}, u32[]{:S(2)}, u32[]{:S(2)}) collective-permute-start(bf16[224,256]{1,0:T(8,128)(2,1)S(1)} %get-tuple-element.22), channel_id=1, source_target_pairs={{12,0},{8,4},{4,8},{0,12},{13,1},{9,5},{5,9},{1,13},{14,2},{10,6},... | collective-permute-start | bytes 344072 | tf_op jit(solution)/shard_map/ppermute | solution.py:280
  20.9 16.5 %copy-start.7 = (bf16[768,768]{1,0:T(8,128)(2,1)S(1)}, bf16[768,768]{1,0:T(8,128)(2,1)}, u32[]{:S(2)}) copy-start(bf16[768,768]{1,0:T(8,128)(2,1)} %refs_11_.1) | copy-start | bytes 3538948
  20.9 16.5 %copy-start.8 = (bf16[768,768]{1,0:T(8,128)(2,1)S(1)}, bf16[768,768]{1,0:T(8,128)(2,1)}, u32[]{:S(2)}) copy-start(bf16[768,768]{1,0:T(8,128)(2,1)} %refs_13_.1) | copy-start | bytes 3538948
  20.9 16.5 %copy-start.10 = (f32[768]{0:T(1024)S(1)}, f32[768]{0:T(1024)}, u32[]{:S(2)}) copy-start(f32[768]{0:T(1024)} %refs_10_.1) | copy-start | bytes 9220
  20.9 16.5 %copy-start.11 = (s32[4,2]{0,1:T(2,128)S(1)}, s32[4,2]{0,1:T(2,128)}, u32[]{:S(2)}) copy-start(s32[4,2]{0,1:T(2,128)} %param.13) | copy-start | bytes 100
  21.4 7.7 %collective-permute-start.9 = (bf16[112,128]{1,0:T(8,128)(2,1)S(1)}, bf16[112,128]{1,0:T(8,128)(2,1)S(1)}, u32[]{:S(2)}, u32[]{:S(2)}) collective-permute-start(bf16[112,128]{1,0:T(8,128)(2,1)S(1)} %get-tuple-element.21), channel_id=1, source_target_pairs={{0,1},{1,0},{2,3},{3,2},{4,5},{5,4},{6,7},{7,6},{8,9},{9,8},{10,11... | collective-permute-start | bytes 86024 | tf_op jit(solution)/shard_map/ppermute | solution.py:214
  24.4 8.3 %collective-permute-start.17 = (bf16[128,768]{1,0:T(8,128)(2,1)S(1)}, bf16[128,768]{1,0:T(8,128)(2,1)S(1)}, u32[]{:S(2)}, u32[]{:S(2)}) collective-permute-start(bf16[128,768]{1,0:T(8,128)(2,1)S(1)} %copy-done.9), channel_id=1, source_target_pairs={{0,1},{1,0},{2,3},{3,2},{4,5},{5,4},{6,7},{7,6},{8,9},{9,8},{10,11... | collective-permute-start | bytes 589832 | tf_op jit(solution)/shard_map/ppermute | solution.py:214
  30.6 6.9 %collective-permute-start.18 = (bf16[128,768]{1,0:T(8,128)(2,1)S(1)}, bf16[128,768]{1,0:T(8,128)(2,1)S(1)}, u32[]{:S(2)}, u32[]{:S(2)}) collective-permute-start(bf16[128,768]{1,0:T(8,128)(2,1)S(1)} %get-tuple-element.25), channel_id=1, source_target_pairs={{0,1},{1,0},{2,3},{3,2},{4,5},{5,4},{6,7},{7,6},{8,9},{9,8},{10,11... | collective-permute-start | bytes 589832 | tf_op jit(solution)/shard_map/ppermute | solution.py:214
  30.7 2.0 %collective-permute-start.14 = (bf16[3,112,128]{2,1,0:T(8,128)(2,1)S(1)}, bf16[3,112,128]{2,1,0:T(8,128)(2,1)S(1)}, u32[]{:S(2)}, u32[]{:S(2)}) collective-permute-start(bf16[3,112,128]{2,1,0:T(8,128)(2,1)S(1)} %get-tuple-element.24), channel_id=1, source_target_pairs={{0,1},{1,0},{2,3},{3,2},{4,5},{5,4},{6,7},{7,6},{8,9},{9,8},{10,11... | collective-permute-start | bytes 258056 | tf_op jit(solution)/shard_map/ppermute | solution.py:214
  31.2 4.6 %collective-permute-start.15 = (bf16[3,112,128]{2,1,0:T(8,128)(2,1)S(1)}, bf16[3,112,128]{2,1,0:T(8,128)(2,1)S(1)}, u32[]{:S(2)}, u32[]{:S(2)}) collective-permute-start(bf16[3,112,128]{2,1,0:T(8,128)(2,1)S(1)} %get-tuple-element.23.refs_1_), channel_id=1, source_target_pairs={{0,2},{1,3},{2,0},{3,1},{4,6},{5,7},{6,4},{7,5},{8,10},{9,11},{10,... | collective-permute-start | bytes 258056 | tf_op jit(solution)/shard_map/ppermute | solution.py:217
  32.7 4.8 %collective-permute-start.16 = (bf16[3,112,128]{2,1,0:T(8,128)(2,1)S(1)}, bf16[3,112,128]{2,1,0:T(8,128)(2,1)S(1)}, u32[]{:S(2)}, u32[]{:S(2)}) collective-permute-start(bf16[3,112,128]{2,1,0:T(8,128)(2,1)S(1)} %get-tuple-element.24), channel_id=1, source_target_pairs={{0,3},{1,2},{2,1},{3,0},{4,7},{5,6},{6,5},{7,4},{8,11},{9,10},{10,... | collective-permute-start | bytes 258056 | tf_op jit(solution)/shard_map/ppermute | solution.py:217
  41.1 5.5 %collective-permute-start.19 = (f32[192,112]{1,0:T(8,128)S(1)}, f32[192,112]{1,0:T(8,128)S(1)}, u32[]{:S(2)}, u32[]{:S(2)}) collective-permute-start(f32[192,112]{1,0:T(8,128)S(1)} %get-tuple-element.28), channel_id=1, source_target_pairs={{0,1},{1,0},{2,3},{3,2},{4,5},{5,4},{6,7},{7,6},{8,9},{9,8},{10,11... | collective-permute-start | bytes 258056 | tf_op jit(solution)/shard_map/ppermute | solution.py:214
  41.2 4.1 %collective-permute-start.20 = (bf16[192,112]{1,0:T(8,128)(2,1)S(1)}, bf16[192,112]{1,0:T(8,128)(2,1)S(1)}, u32[]{:S(2)}, u32[]{:S(2)}) collective-permute-start(bf16[192,112]{1,0:T(8,128)(2,1)S(1)} %get-tuple-element.29), channel_id=1, source_target_pairs={{0,2},{1,3},{2,0},{3,1},{4,6},{5,7},{6,4},{7,5},{8,10},{9,11},{10,... | collective-permute-start | bytes 129032 | tf_op jit(solution)/shard_map/ppermute | solution.py:217
  42.5 4.0 %collective-permute-start.21 = (bf16[192,112]{1,0:T(8,128)(2,1)S(1)}, bf16[192,112]{1,0:T(8,128)(2,1)S(1)}, u32[]{:S(2)}, u32[]{:S(2)}) collective-permute-start(bf16[192,112]{1,0:T(8,128)(2,1)S(1)} %get-tuple-element.30), channel_id=1, source_target_pairs={{0,3},{1,2},{2,1},{3,0},{4,7},{5,6},{6,5},{7,4},{8,11},{9,10},{10,... | collective-permute-start | bytes 129032 | tf_op jit(solution)/shard_map/ppermute | solution.py:217

commit v3 on v2

--- a/solution.py
+++ b/solution.py
@@ -54,10 +54,10 @@
     out[...] = block[:8, :128].astype(F32)
 
 
-def self_kernel(groups, *refs):
+def memory_kernel(groups, *refs):
     blocks = refs[: 2 * groups]
-    g_self, g_memory, w_cross, w_own, w_other, out_own, out_other = refs[2 * groups : 2 * groups + 7]
-    x_rows, partial, kv, x_full = refs[-4:]
+    g_self, g_memory, w_qkv = refs[2 * groups : 2 * groups + 3]
+    x_rows, normed_self, kv, x_full = refs[-4:]
     group, member = position()
     width = blocks[0].shape[0]
     for index in range(2 * groups):
@@ -69,9 +69,15 @@
     x_rows[...] = jnp.where(member == 0, x[:rows], x[rows:])
     normed = standardize(x)
     memory = (normed * g_memory[...].reshape(1, -1)).astype(BF16)
-    kv[:, : kv.shape[1] // 2] = mm(memory, w_cross[1]).astype(BF16)
-    kv[:, kv.shape[1] // 2 :] = mm(memory, w_cross[2]).astype(BF16)
-    own = (normed * g_self[...].reshape(1, -1)).astype(BF16)
+    kv[:, : kv.shape[1] // 2] = mm(memory, w_qkv[1]).astype(BF16)
+    kv[:, kv.shape[1] // 2 :] = mm(memory, w_qkv[2]).astype(BF16)
+    normed_self[...] = (normed * g_self[...].reshape(1, -1)).astype(BF16)
+
+
+def self_kernel(normed, w_own, w_other, out_own, out_other, partial):
+    member = position()[1]
+    own = normed[...]
+    rows = own.shape[0] // ROW_GROUPS
     mine = jnp.where(member == 0, own[:rows], own[rows:])
     q = jnp.concatenate([mm(mine, w_own[0]), mm(mine, w_other[0])], axis=1).astype(BF16)
     k = jnp.concatenate([mm(own, w_own[1]), mm(own, w_other[1])], axis=1).astype(BF16)
@@ -82,17 +88,6 @@
     partial[...] = total.astype(BF16)
 
 
-def query_kernel(x_rows, gain, w_own, w_other, *refs):
-    after, kept, given = refs[-3:]
-    total = x_rows[...]
-    for partial in refs[:-3]:
-        total = total + partial[...].astype(F32)
-    after[...] = total
-    normed = (standardize(total) * gain[...].reshape(1, -1)).astype(BF16)
-    kept[...] = mm(normed, w_own[0]).astype(BF16)
-    given[...] = mm(normed, w_other[0]).astype(BF16)
-
-
 def hand_on(passed, handed, sems):
     copies = [pltpu.make_async_copy(passed[i], handed[i], sems.at[i]) for i in range(len(passed))]
     for copy in copies:
@@ -100,28 +95,41 @@
     return copies
 
 
-def cross_kernel(count, q_own, q_other, *refs):
+def cross_kernel(groups, views, count, x_rows, gain, w_own, w_other, *refs):
+    partials, refs = refs[:groups], refs[groups:]
+    kv_own, kv_other, refs = refs[:views], refs[views : 2 * views], refs[2 * views :]
     passed, refs = refs[:count], refs[count:]
-    memories, kept, given = refs[: -3 - count], refs[-3 - count], refs[-2 - count]
-    copies = hand_on(passed, refs[len(refs) - 1 - count : -1], refs[-1])
-    rows, width = q_own.shape
-    q = jnp.concatenate([q_own[...], q_other[...]], axis=0)
-    for view, memory in enumerate(memories):
-        context = head_attention(q, memory[:, :width], memory[:, width:]).astype(BF16)
-        kept[view] = context[:rows]
-        given[view] = context[rows:]
+    after, context, handed, sems = refs[0], refs[1], refs[2:-1], refs[-1]
+    if len(handed) < count:
+        handed = [handed[0].at[0], handed[0].at[1], *handed[1:]]
+    copies = hand_on(passed, handed, sems)
+    total = x_rows[...]
+    for partial in partials:
+        total = total + partial[...].astype(F32)
+    after[...] = total
+    normed = (standardize(total) * gain[...].reshape(1, -1)).astype(BF16)
+    q = jnp.concatenate([mm(normed, w_own[0]), mm(normed, w_other[0])], axis=1).astype(BF16)
+    width = q.shape[1] // 2
+    for view in range(views):
+        k = jnp.concatenate([kv_own[view][:, :width], kv_other[view][:, :width]], axis=1)
+        v = jnp.concatenate([kv_own[view][:, width:], kv_other[view][:, width:]], axis=1)
+        context[view] = head_attention(q, k, v).astype(BF16)
     for copy in copies:
         copy.wait()
 
 
 def other_image(image, step, images):
     return image ^ step if images & (images - 1) == 0 else (image + step) % images
+
+
+def pair_steps(images):
+    return [*range(2, images), 1]
 
 
 def view_counts(images, pairs):
     image = lax.axis_index("pair")
     counts = []
-    for step in range(1, images):
+    for step in pair_steps(images):
         memory = other_image(image, step, images)
         count = jnp.int32(0)
         for pair in range(pairs.shape[1]):
@@ -133,20 +141,23 @@
 
 
 def mlp_kernel(groups, images, listed, *refs):
-    contexts, refs = refs[: 2 * groups], refs[2 * groups :]
-    views = contexts[0].shape[0]
+    contexts, refs = refs[:groups], refs[groups:]
+    views, _, width = contexts[0].shape
+    width = width // 2
     w_out = refs[: 2 * groups]
-    after, gain, up_own, up_other, down_own, down_other = refs[2 * groups : 2 * groups + 6]
-    outs = refs[2 * groups + 6 : 4 * groups + 6]
-    kept, partial = refs[4 * groups + 6 :]
+    after, gain, up_own, down_own = refs[2 * groups : 2 * groups + 4]
+    others = refs[2 * groups + 4 : -2 * groups - 2]
+    up_other, down_other = others if len(others) == 2 else (others[0].at[0], others[0].at[1])
+    outs, (kept, partial) = refs[-2 * groups - 2 : -2], refs[-2:]
     group, member = position()
     rows = after.shape[0]
     column = after.shape[1] // (2 * groups)
     residual = after[...]
     total = jnp.concatenate([residual] * views, axis=0)
-    for source in range(2 * groups):
-        held = contexts[source][...].reshape(views * rows, -1)
-        total = total + mm(held, w_out[source][...])
+    for step in range(groups):
+        held = contexts[step][...].reshape(views * rows, 2 * width)
+        total = total + mm(held[:, :width], w_out[2 * step][...])
+        total = total + mm(held[:, width:], w_out[2 * step + 1][...])
     if images:
         share = view_counts(images, listed)
     else:
@@ -234,12 +245,6 @@
             cost_estimate=pl.CostEstimate(flops=flops, bytes_accessed=moved, transcendentals=0),
         )(*args)
 
-    def exchange(kept, given):
-        blocks = [kept, swap(given)]
-        for step in range(1, groups):
-            blocks += [turn(kept, step), turn(given, step, 1)]
-        return blocks
-
     shape = jax.ShapeDtypeStruct
     features = features[0].T
     blocks = [features, swap(features)]
@@ -248,27 +253,20 @@
         blocks += [arrived, swap(arrived)]
     turned = [turn(w_cross_out, step) for step in range(1, groups)]
     self_other, self_out_other, cross_other = swap(w_self_qkv), swap(w_self_out), swap(w_cross_qkv)
-    up_other, down_other, cross_out_other = swap(w_up), swap(w_down), swap(w_cross_out)
+    cross_out_other = swap(w_cross_out)
 
     mark = call(mark_kernel, shape((8, 128), F32), [blocks[1]], flops=3 * 10**9)
-    x_rows, partial, kv = call(
-        lambda *refs: self_kernel(groups, *refs),
-        [shape((rows, model), F32), shape((rows, model), BF16), shape((tokens, 2 * att), BF16)],
-        [
-            *blocks,
-            gain_self,
-            gain_memory,
-            w_cross_qkv,
-            w_self_qkv,
-            self_other,
-            w_self_out,
-            self_out_other,
-            mark,
-            cross_other,
-            up_other,
-            down_other,
-        ],
+    x_rows, normed_self, kv = call(
+        lambda *refs: memory_kernel(groups, *refs),
+        [shape((rows, model), F32), shape((tokens, model), BF16), shape((tokens, 2 * att), BF16)],
+        [*blocks, gain_self, gain_memory, w_cross_qkv, mark, cross_other, cross_out_other],
         scratch=[pltpu.VMEM((model, tokens), BF16)],
+        flops=10**8,
+    )
+    partial = call(
+        self_kernel,
+        shape((rows, model), BF16),
+        [normed_self, w_self_qkv, self_other, w_self_out, self_out_other],
         flops=10**8,
     )
 
@@ -278,7 +276,7 @@
         listed = pair_list.T
         kv_own = [
             lax.ppermute(kv, "pair", [(other_image(i, step, images), i) for i in range(images)])
-            for step in range(1, images)
+            for step in pair_steps(images)
         ]
     else:
         views = min(DEGREE, pair_list.shape[0])
@@ -293,27 +291,37 @@
         gathered = lax.all_gather(kv, "pair", axis=0, tiled=False)
         kv_own = [lax.dynamic_index_in_dim(gathered, memories[view], 0, False) for view in range(views)]
     partials = [partial] + [turn(partial, step) for step in range(1, groups)]
-    after, q_own, q_given = call(
-        query_kernel,
-        [shape((rows, model), F32)] + [shape((rows, att), BF16)] * 2,
-        [x_rows, gain_cross, w_cross_qkv, cross_other, *partials],
+    late = [w_up, w_down, *turned]
+    packed = w_up.shape == w_down.shape
+    late_shapes = [shape(value.shape, BF16) for value in late]
+    if packed:
+        late_shapes = [shape((2, *w_up.shape), BF16), *late_shapes[2:]]
+    after, context, *handed = call(
+        lambda *refs: cross_kernel(groups, views, len(late), *refs),
+        [shape((rows, model), F32), shape((views, rows, 2 * att), BF16)] + late_shapes,
+        [
+            x_rows,
+            gain_cross,
+            w_cross_qkv,
+            cross_other,
+            *partials,
+            *kv_own,
+            *[swap(value) for value in kv_own],
+            *late,
+        ],
+        scratch=[pltpu.SemaphoreType.DMA((len(late),))],
         flops=10**8,
     )
-    kept, given, *handed = call(
-        lambda *refs: cross_kernel(groups - 1, *refs),
-        [shape((views, rows, att), BF16)] * 2 + [shape(value.shape, BF16) for value in turned],
-        [q_own, swap(q_given), *turned, *kv_own],
-        scratch=[pltpu.SemaphoreType.DMA((max(groups - 1, 1),))],
-        flops=10**8,
-    )
-    contexts = exchange(kept, given)
+    handed = [swap(value) for value in handed]
+    mlp_other = handed[: 1 if packed else 2]
     cross_out = [w_cross_out, cross_out_other]
     for step in range(groups - 1):
-        cross_out += [turned[step], swap(handed[step])]
+        cross_out += [turned[step], handed[len(mlp_other) + step]]
+    contexts = [context] + [turn(context, step) for step in range(1, groups)]
     pieces = call(
         lambda *refs: mlp_kernel(groups, images if static else 0, *refs),
         [shape((column, rows), F32)] * 2 + [shape((column, rows), BF16)] * (2 * groups - 2),
-        [listed, *contexts, *cross_out, after, gain_mlp, w_up, up_other, w_down, down_other],
+        [listed, *contexts, *cross_out, after, gain_mlp, w_up, w_down, *mlp_other],
         scratch=[pltpu.VMEM((model, rows), F32)] * 2,
         smem=1,
         flops=3 * 10**9,

time: 47.4 us -> 43.1 us (0.909)
  waiting for transfers between devices: 24 us -> 18.3 us
  starting transfers between devices: 14.9 us -> 15.6 us
  Pallas kernels: 8.16 us -> 8.83 us
    ppermute x12, waiting for transfers between devices: 4.17 us -> 1.02 us  [swap(): return lax.ppermute(value, 'head', [(i, i ^ 1) for i in range(head)])]
    ppermute x7 -> x6, waiting for transfers between devices: 15.1 us -> 12.8 us  [turn(): lax.ppermute(value, 'head', [(i, (i // 2 + step) % groups * 2 + (i % 2 ^...]
    pallas_call x6, Pallas kernels: 8.16 us -> 8.83 us  [call(): pl.pallas_call(kernel, out_shape=out_shape, in_specs=[SMEM] * smem + [VME...]
    ppermute x12, starting transfers between devices: 2.15 us -> 2.68 us  [swap(): return lax.ppermute(value, 'head', [(i, i ^ 1) for i in range(head)])]
    ppermute x7 -> x6, starting transfers between devices: 8.36 us -> 8.45 us  [turn(): lax.ppermute(value, 'head', [(i, (i // 2 + step) % groups * 2 + (i % 2 ^...]
  transfers between devices with their start and end apart: 22 -> 21, of which waited for: 11 -> 8; matrix products, arithmetic and copies ran while one was open for 0% -> 0% of each run, Pallas kernels for 4% -> 5%
where the time goes in v3:
time: 43.1 us; the launch traced here: 43 us
  waiting for transfers between devices  18.3 us (42%)
  starting transfers between devices  15.6 us (36%)
  Pallas kernels  8.83 us (20%)
    ppermute x6, waiting for transfers between devices, turn(): lax.ppermute(value, 'head', [(i, (i // 2 + step) % groups * 2 + (i % 2 ^...  12.8 us
    pallas_call x6, Pallas kernels, call(): pl.pallas_call(kernel, out_shape=out_shape, in_specs=[SMEM] * smem + [VME...  8.83 us
    ppermute x6, starting transfers between devices, turn(): lax.ppermute(value, 'head', [(i, (i // 2 + step) % groups * 2 + (i % 2 ^...  8.45 us
    ppermute x3, starting transfers between devices, body(): lax.ppermute(kv, 'pair', [(other_image(i, step, images), i) for i in rang...  4.48 us
    ppermute x3, waiting for transfers between devices, body(): lax.ppermute(kv, 'pair', [(other_image(i, step, images), i) for i in rang...  4.41 us
    ppermute x12, starting transfers between devices, swap(): return lax.ppermute(value, 'head', [(i, i ^ 1) for i in range(head)])  2.68 us
    ppermute x12, waiting for transfers between devices, swap(): return lax.ppermute(value, 'head', [(i, i ^ 1) for i in range(head)])  1.02 us
  transfers between devices with their start and end apart: 21, of which 8 were waited for; matrix products, arithmetic and copies ran while one was open for 0% of the time, Pallas kernels for 5%

profile of v3, /device:TPU:0, one launch (start us, length us, event | category | flops | bytes accessed | tf_op | source)
XLA Modules:
  0.0 43.0 jit_solution(5432507077075649395)
XLA Ops:
  0.0 0.5 %collective-permute-start.3 = (bf16[3,768,128]{2,1,0:T(8,128)(2,1)}, bf16[3,768,128]{2,1,0:T(8,128)(2,1)S(1)}, u32[]{:S(2)}, u32[]{:S(2)}) collective-permute-start(bf16[3,768,128]{2,1,0:T(8,128)(2,1)} %refs_2_.1), channel_id=1, source_target_pairs={{0,1},{1,0},{2,3},{3,2},{4,5},{5,4},{6,7},{7,6},{8,9},{9,8},{10,11... | collective-permute-start | bytes 1769480 | tf_op jit(solution)/shard_map/ppermute | solution.py:225
  0.5 0.1 collective-permute-start.5
  0.5 0.0 copy-start.9
  0.5 0.0 copy-start.3
  0.5 0.0 copy-start.4
  0.6 3.0 %collective-permute-start.1 = (bf16[192,224]{1,0:T(8,128)(2,1)}, bf16[192,224]{1,0:T(8,128)(2,1)S(1)}, u32[]{:S(2)}, u32[]{:S(2)}) collective-permute-start(bf16[192,224]{1,0:T(8,128)(2,1)} %bitcast.7), channel_id=1, source_target_pairs={{0,2},{1,3},{2,0},{3,1},{4,6},{5,7},{6,4},{7,5},{8,10},{9,11},{10,... | collective-permute-start | bytes 258056 | tf_op jit(solution)/shard_map/ppermute | solution.py:228
  3.6 0.0 collective-permute-start
  3.6 0.5 %collective-permute-start.4 = (bf16[128,768]{1,0:T(8,128)(2,1)}, bf16[128,768]{1,0:T(8,128)(2,1)S(1)}, u32[]{:S(2)}, u32[]{:S(2)}) collective-permute-start(bf16[128,768]{1,0:T(8,128)(2,1)} %refs_3_.1), channel_id=1, source_target_pairs={{0,1},{1,0},{2,3},{3,2},{4,5},{5,4},{6,7},{7,6},{8,9},{9,8},{10,11... | collective-permute-start | bytes 589832 | tf_op jit(solution)/shard_map/ppermute | solution.py:225
  4.1 2.7 %collective-permute-done.1.refs_2_ = bf16[192,224]{1,0:T(8,128)(2,1)S(1)} collective-permute-done((bf16[192,224]{1,0:T(8,128)(2,1)}, bf16[192,224]{1,0:T(8,128)(2,1)S(1)}, u32[]{:S(2)}, u32[]{:S(2)}) %collective-permute-start.1) | collective-permute-done | bytes 86048 | tf_op jit(solution)/shard_map/ppermute | solution.py:228
  6.7 0.0 collective-permute-start.6
  6.7 0.0 collective-permute-done.block.refs_1_
  6.7 0.5 %collective-permute-start.2 = (bf16[192,224]{1,0:T(8,128)(2,1)S(1)}, bf16[192,224]{1,0:T(8,128)(2,1)S(1)}, u32[]{:S(2)}, u32[]{:S(2)}) collective-permute-start(bf16[192,224]{1,0:T(8,128)(2,1)S(1)} %collective-permute-done.1.refs_2_), channel_id=1, source_target_pairs={{0,1},{1,0},{2,3},{3,2},{4,5},{5,4},{6,7},{7,6},{8,9},{9,8},{10,11... | collective-permute-start | bytes 258056 | tf_op jit(solution)/shard_map/ppermute | solution.py:225
  7.3 1.0 %collective-permute-done.2.refs_3_ = bf16[192,224]{1,0:T(8,128)(2,1)S(1)} collective-permute-done((bf16[192,224]{1,0:T(8,128)(2,1)S(1)}, bf16[192,224]{1,0:T(8,128)(2,1)S(1)}, u32[]{:S(2)}, u32[]{:S(2)}) %collective-permute-start.2) | collective-permute-done | bytes 86048 | tf_op jit(solution)/shard_map/ppermute | solution.py:225
  8.3 0.0 collective-permute-done.4.refs_9_.refs_4_
  8.3 0.0 collective-permute-done.3.refs_8_.refs_3_
  8.3 0.0 copy-done
  8.3 0.0 copy-done.5
  8.3 0.0 copy-done.6
  8.3 0.0 copy-done.7
  8.3 0.7 %shard_map.119 = (f32[112,768]{1,0:T(8,128)S(1)}, bf16[224,768]{1,0:T(8,128)(2,1)S(1)}, bf16[224,256]{1,0:T(8,128)(2,1)S(1)}) custom-call(bf16[192,224]{1,0:T(8,128)(2,1)S(1)} %bitcast.9, bf16[192,224]{1,0:T(8,128)(2,1)S(1)} %collective-permute-done.block.refs_1_, bf16[192,224]{1,0:T(8,128)(2,1)S(1)} %collective-permute-done.1.refs_2_, ...), custom_call_target="tpu_custom_call" | custom-call | flops 100000000 | tf_op jit(solution)/shard_map/pallas_call | solution.py:238
  9.0 2.9 %collective-permute-start.8 = (bf16[224,256]{1,0:T(8,128)(2,1)S(1)}, bf16[224,256]{1,0:T(8,128)(2,1)S(1)}, u32[]{:S(2)}, u32[]{:S(2)}) collective-permute-start(bf16[224,256]{1,0:T(8,128)(2,1)S(1)} %get-tuple-element.18), channel_id=1, source_target_pairs={{8,0},{12,4},{0,8},{4,12},{9,1},{13,5},{1,9},{5,13},{10,2},{14,6},... | collective-permute-start | bytes 344072 | tf_op jit(solution)/shard_map/ppermute | solution.py:278
  11.9 1.4 %collective-permute-start.9 = (bf16[224,256]{1,0:T(8,128)(2,1)S(1)}, bf16[224,256]{1,0:T(8,128)(2,1)S(1)}, u32[]{:S(2)}, u32[]{:S(2)}) collective-permute-start(bf16[224,256]{1,0:T(8,128)(2,1)S(1)} %get-tuple-element.18), channel_id=1, source_target_pairs={{12,0},{8,4},{4,8},{0,12},{13,1},{9,5},{5,9},{1,13},{14,2},{10,6},... | collective-permute-start | bytes 344072 | tf_op jit(solution)/shard_map/ppermute | solution.py:278
  13.3 0.2 collective-permute-start.10
  13.5 0.0 collective-permute-done.6.out_other
  13.5 0.0 copy-done.9
  13.5 1.5 %collective-permute-start.14 = (bf16[128,768]{1,0:T(8,128)(2,1)S(1)}, bf16[128,768]{1,0:T(8,128)(2,1)S(1)}, u32[]{:S(2)}, u32[]{:S(2)}) collective-permute-start(bf16[128,768]{1,0:T(8,128)(2,1)S(1)} %copy-done.9), channel_id=1, source_target_pairs={{0,2},{1,3},{2,0},{3,1},{4,6},{5,7},{6,4},{7,5},{8,10},{9,11},{10,... | collective-permute-start | bytes 589832 | tf_op jit(solution)/shard_map/ppermute | solution.py:228
  15.0 0.0 collective-permute-done.5.w_other
  15.0 0.0 copy-done.3
  15.0 0.0 copy-done.4
  15.0 1.3 %shard_map.120.refs_4_ = bf16[112,768]{1,0:T(8,128)(2,1)S(1)} custom-call(bf16[224,768]{1,0:T(8,128)(2,1)S(1)} %get-tuple-element.17.normed, bf16[3,768,128]{2,1,0:T(8,128)(2,1)S(1)} %copy-done.3, bf16[3,768,128]{2,1,0:T(8,128)(2,1)S(1)} %collective-permute-done.5.w_other, bf16[128,768]{1,0:T(8,128)(2,1)S(1)} %copy-done.4, ...), custom_call_target="tpu_custom_call" | custom-call | flops 100000000 | tf_op jit(solution)/shard_map/pallas_call | solution.py:238
  16.3 0.6 %collective-permute-start.7 = (bf16[112,768]{1,0:T(8,128)(2,1)S(1)}, bf16[112,768]{1,0:T(8,128)(2,1)S(1)}, u32[]{:S(2)}, u32[]{:S(2)}) collective-permute-start(bf16[112,768]{1,0:T(8,128)(2,1)S(1)} %shard_map.120.refs_4_), channel_id=1, source_target_pairs={{0,2},{1,3},{2,0},{3,1},{4,6},{5,7},{6,4},{7,5},{8,10},{9,11},{10,... | collective-permute-start | bytes 516104 | tf_op jit(solution)/shard_map/ppermute | solution.py:228
  16.9 4.0 %collective-permute-done.8.refs_6_ = bf16[224,256]{1,0:T(8,128)(2,1)S(1)} collective-permute-done((bf16[224,256]{1,0:T(8,128)(2,1)S(1)}, bf16[224,256]{1,0:T(8,128)(2,1)S(1)}, u32[]{:S(2)}, u32[]{:S(2)}) %collective-permute-start.8) | collective-permute-done | bytes 114720 | tf_op jit(solution)/shard_map/ppermute | solution.py:278
  20.9 0.0 collective-permute-start.11
  20.9 0.0 collective-permute-done.9.refs_7_
  20.9 0.5 %collective-permute-start.12 = (bf16[224,256]{1,0:T(8,128)(2,1)S(1)}, bf16[224,256]{1,0:T(8,128)(2,1)S(1)}, u32[]{:S(2)}, u32[]{:S(2)}) collective-permute-start(bf16[224,256]{1,0:T(8,128)(2,1)S(1)} %collective-permute-done.9.refs_7_), channel_id=1, source_target_pairs={{0,1},{1,0},{2,3},{3,2},{4,5},{5,4},{6,7},{7,6},{8,9},{9,8},{10,11... | collective-permute-start | bytes 344072 | tf_op jit(solution)/shard_map/ppermute | solution.py:225
  21.4 0.4 %collective-permute-done.10.refs_8_ = bf16[224,256]{1,0:T(8,128)(2,1)S(1)} collective-permute-done((bf16[224,256]{1,0:T(8,128)(2,1)S(1)}, bf16[224,256]{1,0:T(8,128)(2,1)S(1)}, u32[]{:S(2)}, u32[]{:S(2)}) %collective-permute-start.10) | collective-permute-done | bytes 114720 | tf_op jit(solution)/shard_map/ppermute | solution.py:278
  21.9 0.0 collective-permute-start.13
  21.9 0.0 collective-permute-done.14.refs_14_.refs_5_
  21.9 1.9 %collective-permute-done.7.refs_5_ = bf16[112,768]{1,0:T(8,128)(2,1)S(1)} collective-permute-done((bf16[112,768]{1,0:T(8,128)(2,1)S(1)}, bf16[112,768]{1,0:T(8,128)(2,1)S(1)}, u32[]{:S(2)}, u32[]{:S(2)}) %collective-permute-start.7) | collective-permute-done | bytes 172064 | tf_op jit(solution)/shard_map/ppermute | solution.py:228
  23.8 0.0 collective-permute-done.11.refs_9_
  23.8 0.0 collective-permute-done.12.refs_10_
  23.8 0.0 collective-permute-done.13.refs_11_
  23.8 0.0 copy-done.1
  23.8 0.0 copy-done.2
  23.8 0.0 copy-done.8
  23.8 0.0 copy-start.10
  23.8 0.0 copy-start.11
  23.8 2.5 %shard_map.121 = (f32[112,768]{1,0:T(8,128)S(1)}, bf16[3,112,256]{2,1,0:T(8,128)(2,1)S(1)}, bf16[2,768,768]{2,1,0:T(8,128)(2,1)S(1)}, bf16[128,768]{1,0:T(8,128)(2,1)S(1)}) custom-call(f32[112,768]{1,0:T(8,128)S(1)} %get-tuple-element.16.refs_0_, f32[768]{0:T(1024)S(1)} %copy-done.8, bf16[3,768,128]{2,1,0:T(8,128)(2,1)S(1)} %copy-done, ...), custom_call_target="tpu_custom_call" | custom-call | flops 100000000 | tf_op jit(solution)/shard_map/pallas_call | solution.py:238
  26.3 0.1 collective-permute-start.17
  26.4 0.5 %collective-permute-start.16 = (bf16[128,768]{1,0:T(8,128)(2,1)S(1)}, bf16[128,768]{1,0:T(8,128)(2,1)S(1)}, u32[]{:S(2)}, u32[]{:S(2)}) collective-permute-start(bf16[128,768]{1,0:T(8,128)(2,1)S(1)} %get-tuple-element.20), channel_id=1, source_target_pairs={{0,1},{1,0},{2,3},{3,2},{4,5},{5,4},{6,7},{7,6},{8,9},{9,8},{10,11... | collective-permute-start | bytes 589832 | tf_op jit(solution)/shard_map/ppermute | solution.py:225
  26.9 1.5 %collective-permute-start.15 = (bf16[3,112,256]{2,1,0:T(8,128)(2,1)S(1)}, bf16[3,112,256]{2,1,0:T(8,128)(2,1)S(1)}, u32[]{:S(2)}, u32[]{:S(2)}) collective-permute-start(bf16[3,112,256]{2,1,0:T(8,128)(2,1)S(1)} %get-tuple-element.19.refs_1_), channel_id=1, source_target_pairs={{0,2},{1,3},{2,0},{3,1},{4,6},{5,7},{6,4},{7,5},{8,10},{9,11},{10,... | collective-permute-start | bytes 516104 | tf_op jit(solution)/shard_map/ppermute | solution.py:228
  28.4 4.9 %collective-permute-done.15.refs_2_ = bf16[3,112,256]{2,1,0:T(8,128)(2,1)S(1)} collective-permute-done((bf16[3,112,256]{2,1,0:T(8,128)(2,1)S(1)}, bf16[3,112,256]{2,1,0:T(8,128)(2,1)S(1)}, u32[]{:S(2)}, u32[]{:S(2)}) %collective-permute-start.15) | collective-permute-done | bytes 172064 | tf_op jit(solution)/shard_map/ppermute | solution.py:228
  33.3 0.0 collective-permute-done.16.refs_6_
  33.3 0.0 collective-permute-done.17.refs_11_
  33.3 0.0 copy-done.10
  33.3 0.0 copy-done.11
  33.3 3.5 %shard_map.122 = (f32[192,112]{1,0:T(8,128)S(1)}, f32[192,112]{1,0:T(8,128)S(1)}, bf16[192,112]{1,0:T(8,128)(2,1)S(1)}, bf16[192,112]{1,0:T(8,128)(2,1)S(1)}) custom-call(s32[2,4]{1,0:T(2,128)S(1)} %bitcast.10, bf16[3,112,256]{2,1,0:T(8,128)(2,1)S(1)} %get-tuple-element.19.refs_1_, bf16[3,112,256]{2,1,0:T(8,128)(2,1)S(1)} %collective-permute-done.15.refs_2_, ...), custom_call_target="tpu_custom_call" | custom-call | flops 3000000000 | tf_op jit(solution)/shard_map/pallas_call | solution.py:238
  36.8 0.1 collective-permute-start.18
  36.9 1.6 %collective-permute-start.19 = (bf16[192,112]{1,0:T(8,128)(2,1)S(1)}, bf16[192,112]{1,0:T(8,128)(2,1)S(1)}, u32[]{:S(2)}, u32[]{:S(2)}) collective-permute-start(bf16[192,112]{1,0:T(8,128)(2,1)S(1)} %get-tuple-element.25), channel_id=1, source_target_pairs={{0,2},{1,3},{2,0},{3,1},{4,6},{5,7},{6,4},{7,5},{8,10},{9,11},{10,... | collective-permute-start | bytes 129032 | tf_op jit(solution)/shard_map/ppermute | solution.py:228
  38.5 0.3 collective-permute-start.20
  38.8 2.3 %collective-permute-done.19.refs_2_ = bf16[192,112]{1,0:T(8,128)(2,1)S(1)} collective-permute-done((bf16[192,112]{1,0:T(8,128)(2,1)S(1)}, bf16[192,112]{1,0:T(8,128)(2,1)S(1)}, u32[]{:S(2)}, u32[]{:S(2)}) %collective-permute-start.19) | collective-permute-done | bytes 43040 | tf_op jit(solution)/shard_map/ppermute | solution.py:228
  41.1 1.1 %collective-permute-done.20.refs_3_ = bf16[192,112]{1,0:T(8,128)(2,1)S(1)} collective-permute-done((bf16[192,112]{1,0:T(8,128)(2,1)S(1)}, bf16[192,112]{1,0:T(8,128)(2,1)S(1)}, u32[]{:S(2)}, u32[]{:S(2)}) %collective-permute-start.20) | collective-permute-done | bytes 43040 | tf_op jit(solution)/shard_map/ppermute | solution.py:228
  42.2 0.0 collective-permute-done.18.refs_1_
  42.2 0.8 %shard_map.123 = f32[192,224]{1,0:T(8,128)} custom-call(f32[192,112]{1,0:T(8,128)S(1)} %get-tuple-element.23.refs_0_, f32[192,112]{1,0:T(8,128)S(1)} %collective-permute-done.18.refs_1_, bf16[192,112]{1,0:T(8,128)(2,1)S(1)} %collective-permute-done.19.refs_2_, bf16[192,112]{1,0:T(8,128)(2,1)S(1)} %collective-permute-done.20.refs_3_), custom_call_target="tpu_custom_call" | custom-call | tf_op jit(solution)/shard_map/pallas_call | solution.py:238
  (8 shorter events, 0.0 us)
Async XLA Ops:
  0.0 8.3 %collective-permute-start.3 = (bf16[3,768,128]{2,1,0:T(8,128)(2,1)}, bf16[3,768,128]{2,1,0:T(8,128)(2,1)S(1)}, u32[]{:S(2)}, u32[]{:S(2)}) collective-permute-start(bf16[3,768,128]{2,1,0:T(8,128)(2,1)} %refs_2_.1), channel_id=1, source_target_pairs={{0,1},{1,0},{2,3},{3,2},{4,5},{5,4},{6,7},{7,6},{8,9},{9,8},{10,11... | collective-permute-start | bytes 1769480 | tf_op jit(solution)/shard_map/ppermute | solution.py:225
  0.5 14.6 %collective-permute-start.5 = (bf16[3,768,128]{2,1,0:T(8,128)(2,1)}, bf16[3,768,128]{2,1,0:T(8,128)(2,1)S(1)}, u32[]{:S(2)}, u32[]{:S(2)}) collective-permute-start(bf16[3,768,128]{2,1,0:T(8,128)(2,1)} %w_own.1), channel_id=1, source_target_pairs={{0,1},{1,0},{2,3},{3,2},{4,5},{5,4},{6,7},{7,6},{8,9},{9,8},{10,11... | collective-permute-start | bytes 1769480 | tf_op jit(solution)/shard_map/ppermute | solution.py:225
  0.5 7.8 %copy-start = (bf16[3,768,128]{2,1,0:T(8,128)(2,1)S(1)}, bf16[3,768,128]{2,1,0:T(8,128)(2,1)}, u32[]{:S(2)}) copy-start(bf16[3,768,128]{2,1,0:T(8,128)(2,1)} %refs_2_.1) | copy-start | bytes 1769476
  0.5 7.8 %copy-start.5 = (bf16[1,224,192]{1,2,0:T(8,128)(2,1)S(1)}, bf16[1,224,192]{1,2,0:T(8,128)(2,1)}, u32[]{:S(2)}) copy-start(bf16[1,224,192]{1,2,0:T(8,128)(2,1)} %param.12) | copy-start | bytes 258052
  0.5 7.8 %copy-start.6 = (f32[768]{0:T(1024)S(1)}, f32[768]{0:T(1024)}, u32[]{:S(2)}) copy-start(f32[768]{0:T(1024)} %refs_4_.1) | copy-start | bytes 9220
  0.5 7.8 %copy-start.7 = (f32[768]{0:T(1024)S(1)}, f32[768]{0:T(1024)}, u32[]{:S(2)}) copy-start(f32[768]{0:T(1024)} %refs_5_.1) | copy-start | bytes 9220
  0.5 13.0 %copy-start.9 = (bf16[128,768]{1,0:T(8,128)(2,1)S(1)}, bf16[128,768]{1,0:T(8,128)(2,1)}, u32[]{:S(2)}) copy-start(bf16[128,768]{1,0:T(8,128)(2,1)} %refs_3_.1) | copy-start | bytes 589828
  0.5 14.5 %copy-start.3 = (bf16[3,768,128]{2,1,0:T(8,128)(2,1)S(1)}, bf16[3,768,128]{2,1,0:T(8,128)(2,1)}, u32[]{:S(2)}) copy-start(bf16[3,768,128]{2,1,0:T(8,128)(2,1)} %w_own.1) | copy-start | bytes 1769476
  0.5 14.5 %copy-start.4 = (bf16[128,768]{1,0:T(8,128)(2,1)S(1)}, bf16[128,768]{1,0:T(8,128)(2,1)}, u32[]{:S(2)}) copy-start(bf16[128,768]{1,0:T(8,128)(2,1)} %out_own.1) | copy-start | bytes 589828
  0.6 6.2 %collective-permute-start.1 = (bf16[192,224]{1,0:T(8,128)(2,1)}, bf16[192,224]{1,0:T(8,128)(2,1)S(1)}, u32[]{:S(2)}, u32[]{:S(2)}) collective-permute-start(bf16[192,224]{1,0:T(8,128)(2,1)} %bitcast.7), channel_id=1, source_target_pairs={{0,2},{1,3},{2,0},{3,1},{4,6},{5,7},{6,4},{7,5},{8,10},{9,11},{10,... | collective-permute-start | bytes 258056 | tf_op jit(solution)/shard_map/ppermute | solution.py:228
  3.6 3.2 %collective-permute-start = (bf16[192,224]{1,0:T(8,128)(2,1)}, bf16[192,224]{1,0:T(8,128)(2,1)S(1)}, u32[]{:S(2)}, u32[]{:S(2)}) collective-permute-start(bf16[192,224]{1,0:T(8,128)(2,1)} %bitcast.8), channel_id=1, source_target_pairs={{0,1},{1,0},{2,3},{3,2},{4,5},{5,4},{6,7},{7,6},{8,9},{9,8},{10,11... | collective-permute-start | bytes 258056 | tf_op jit(solution)/shard_map/ppermute | solution.py:225
  3.6 4.7 %collective-permute-start.4 = (bf16[128,768]{1,0:T(8,128)(2,1)}, bf16[128,768]{1,0:T(8,128)(2,1)S(1)}, u32[]{:S(2)}, u32[]{:S(2)}) collective-permute-start(bf16[128,768]{1,0:T(8,128)(2,1)} %refs_3_.1), channel_id=1, source_target_pairs={{0,1},{1,0},{2,3},{3,2},{4,5},{5,4},{6,7},{7,6},{8,9},{9,8},{10,11... | collective-permute-start | bytes 589832 | tf_op jit(solution)/shard_map/ppermute | solution.py:225
  6.7 6.8 %collective-permute-start.6 = (bf16[128,768]{1,0:T(8,128)(2,1)}, bf16[128,768]{1,0:T(8,128)(2,1)S(1)}, u32[]{:S(2)}, u32[]{:S(2)}) collective-permute-start(bf16[128,768]{1,0:T(8,128)(2,1)} %out_own.1), channel_id=1, source_target_pairs={{0,1},{1,0},{2,3},{3,2},{4,5},{5,4},{6,7},{7,6},{8,9},{9,8},{10,11... | collective-permute-start | bytes 589832 | tf_op jit(solution)/shard_map/ppermute | solution.py:225
  6.7 1.5 %collective-permute-start.2 = (bf16[192,224]{1,0:T(8,128)(2,1)S(1)}, bf16[192,224]{1,0:T(8,128)(2,1)S(1)}, u32[]{:S(2)}, u32[]{:S(2)}) collective-permute-start(bf16[192,224]{1,0:T(8,128)(2,1)S(1)} %collective-permute-done.1.refs_2_), channel_id=1, source_target_pairs={{0,1},{1,0},{2,3},{3,2},{4,5},{5,4},{6,7},{7,6},{8,9},{9,8},{10,11... | collective-permute-start | bytes 258056 | tf_op jit(solution)/shard_map/ppermute | solution.py:225
  7.3 16.5 %copy-start.1 = (bf16[768,768]{1,0:T(8,128)(2,1)S(1)}, bf16[768,768]{1,0:T(8,128)(2,1)}, u32[]{:S(2)}) copy-start(bf16[768,768]{1,0:T(8,128)(2,1)} %refs_9_.1) | copy-start | bytes 3538948
  7.3 16.5 %copy-start.2 = (bf16[768,768]{1,0:T(8,128)(2,1)S(1)}, bf16[768,768]{1,0:T(8,128)(2,1)}, u32[]{:S(2)}) copy-start(bf16[768,768]{1,0:T(8,128)(2,1)} %refs_10_.1) | copy-start | bytes 3538948
  7.3 16.5 %copy-start.8 = (f32[768]{0:T(1024)S(1)}, f32[768]{0:T(1024)}, u32[]{:S(2)}) copy-start(f32[768]{0:T(1024)} %refs_1_.1) | copy-start | bytes 9220
  9.0 11.9 %collective-permute-start.8 = (bf16[224,256]{1,0:T(8,128)(2,1)S(1)}, bf16[224,256]{1,0:T(8,128)(2,1)S(1)}, u32[]{:S(2)}, u32[]{:S(2)}) collective-permute-start(bf16[224,256]{1,0:T(8,128)(2,1)S(1)} %get-tuple-element.18), channel_id=1, source_target_pairs={{8,0},{12,4},{0,8},{4,12},{9,1},{13,5},{1,9},{5,13},{10,2},{14,6},... | collective-permute-start | bytes 344072 | tf_op jit(solution)/shard_map/ppermute | solution.py:278
  11.9 9.0 %collective-permute-start.9 = (bf16[224,256]{1,0:T(8,128)(2,1)S(1)}, bf16[224,256]{1,0:T(8,128)(2,1)S(1)}, u32[]{:S(2)}, u32[]{:S(2)}) collective-permute-start(bf16[224,256]{1,0:T(8,128)(2,1)S(1)} %get-tuple-element.18), channel_id=1, source_target_pairs={{12,0},{8,4},{4,8},{0,12},{13,1},{9,5},{5,9},{1,13},{14,2},{10,6},... | collective-permute-start | bytes 344072 | tf_op jit(solution)/shard_map/ppermute | solution.py:278
  13.3 8.6 %collective-permute-start.10 = (bf16[224,256]{1,0:T(8,128)(2,1)S(1)}, bf16[224,256]{1,0:T(8,128)(2,1)S(1)}, u32[]{:S(2)}, u32[]{:S(2)}) collective-permute-start(bf16[224,256]{1,0:T(8,128)(2,1)S(1)} %get-tuple-element.18), channel_id=1, source_target_pairs={{4,0},{0,4},{12,8},{8,12},{5,1},{1,5},{13,9},{9,13},{6,2},{2,6},{1... | collective-permute-start | bytes 344072 | tf_op jit(solution)/shard_map/ppermute | solution.py:278
  13.5 8.3 %collective-permute-start.14 = (bf16[128,768]{1,0:T(8,128)(2,1)S(1)}, bf16[128,768]{1,0:T(8,128)(2,1)S(1)}, u32[]{:S(2)}, u32[]{:S(2)}) collective-permute-start(bf16[128,768]{1,0:T(8,128)(2,1)S(1)} %copy-done.9), channel_id=1, source_target_pairs={{0,2},{1,3},{2,0},{3,1},{4,6},{5,7},{6,4},{7,5},{8,10},{9,11},{10,... | collective-permute-start | bytes 589832 | tf_op jit(solution)/shard_map/ppermute | solution.py:228
  16.3 7.4 %collective-permute-start.7 = (bf16[112,768]{1,0:T(8,128)(2,1)S(1)}, bf16[112,768]{1,0:T(8,128)(2,1)S(1)}, u32[]{:S(2)}, u32[]{:S(2)}) collective-permute-start(bf16[112,768]{1,0:T(8,128)(2,1)S(1)} %shard_map.120.refs_4_), channel_id=1, source_target_pairs={{0,2},{1,3},{2,0},{3,1},{4,6},{5,7},{6,4},{7,5},{8,10},{9,11},{10,... | collective-permute-start | bytes 516104 | tf_op jit(solution)/shard_map/ppermute | solution.py:228
  20.9 2.9 %collective-permute-start.11 = (bf16[224,256]{1,0:T(8,128)(2,1)S(1)}, bf16[224,256]{1,0:T(8,128)(2,1)S(1)}, u32[]{:S(2)}, u32[]{:S(2)}) collective-permute-start(bf16[224,256]{1,0:T(8,128)(2,1)S(1)} %collective-permute-done.8.refs_6_), channel_id=1, source_target_pairs={{0,1},{1,0},{2,3},{3,2},{4,5},{5,4},{6,7},{7,6},{8,9},{9,8},{10,11... | collective-permute-start | bytes 344072 | tf_op jit(solution)/shard_map/ppermute | solution.py:225
  20.9 2.9 %collective-permute-start.12 = (bf16[224,256]{1,0:T(8,128)(2,1)S(1)}, bf16[224,256]{1,0:T(8,128)(2,1)S(1)}, u32[]{:S(2)}, u32[]{:S(2)}) collective-permute-start(bf16[224,256]{1,0:T(8,128)(2,1)S(1)} %collective-permute-done.9.refs_7_), channel_id=1, source_target_pairs={{0,1},{1,0},{2,3},{3,2},{4,5},{5,4},{6,7},{7,6},{8,9},{9,8},{10,11... | collective-permute-start | bytes 344072 | tf_op jit(solution)/shard_map/ppermute | solution.py:225
  21.9 1.9 %collective-permute-start.13 = (bf16[224,256]{1,0:T(8,128)(2,1)S(1)}, bf16[224,256]{1,0:T(8,128)(2,1)S(1)}, u32[]{:S(2)}, u32[]{:S(2)}) collective-permute-start(bf16[224,256]{1,0:T(8,128)(2,1)S(1)} %collective-permute-done.10.refs_8_), channel_id=1, source_target_pairs={{0,1},{1,0},{2,3},{3,2},{4,5},{5,4},{6,7},{7,6},{8,9},{9,8},{10,11... | collective-permute-start | bytes 344072 | tf_op jit(solution)/shard_map/ppermute | solution.py:225
  23.8 9.5 %copy-start.10 = (f32[768]{0:T(1024)S(1)}, f32[768]{0:T(1024)}, u32[]{:S(2)}) copy-start(f32[768]{0:T(1024)} %refs_8_.1) | copy-start | bytes 9220
  23.8 9.5 %copy-start.11 = (s32[4,2]{0,1:T(2,128)S(1)}, s32[4,2]{0,1:T(2,128)}, u32[]{:S(2)}) copy-start(s32[4,2]{0,1:T(2,128)} %param.13) | copy-start | bytes 100
  26.3 6.9 %collective-permute-start.17 = (bf16[2,768,768]{2,1,0:T(8,128)(2,1)S(1)}, bf16[2,768,768]{2,1,0:T(8,128)(2,1)S(1)}, u32[]{:S(2)}, u32[]{:S(2)}) collective-permute-start(bf16[2,768,768]{2,1,0:T(8,128)(2,1)S(1)} %get-tuple-element.22), channel_id=1, source_target_pairs={{0,1},{1,0},{2,3},{3,2},{4,5},{5,4},{6,7},{7,6},{8,9},{9,8},{10,11... | collective-permute-start | bytes 7077896 | tf_op jit(solution)/shard_map/ppermute | solution.py:225
  26.4 6.9 %collective-permute-start.16 = (bf16[128,768]{1,0:T(8,128)(2,1)S(1)}, bf16[128,768]{1,0:T(8,128)(2,1)S(1)}, u32[]{:S(2)}, u32[]{:S(2)}) collective-permute-start(bf16[128,768]{1,0:T(8,128)(2,1)S(1)} %get-tuple-element.20), channel_id=1, source_target_pairs={{0,1},{1,0},{2,3},{3,2},{4,5},{5,4},{6,7},{7,6},{8,9},{9,8},{10,11... | collective-permute-start | bytes 589832 | tf_op jit(solution)/shard_map/ppermute | solution.py:225
  26.9 6.4 %collective-permute-start.15 = (bf16[3,112,256]{2,1,0:T(8,128)(2,1)S(1)}, bf16[3,112,256]{2,1,0:T(8,128)(2,1)S(1)}, u32[]{:S(2)}, u32[]{:S(2)}) collective-permute-start(bf16[3,112,256]{2,1,0:T(8,128)(2,1)S(1)} %get-tuple-element.19.refs_1_), channel_id=1, source_target_pairs={{0,2},{1,3},{2,0},{3,1},{4,6},{5,7},{6,4},{7,5},{8,10},{9,11},{10,... | collective-permute-start | bytes 516104 | tf_op jit(solution)/shard_map/ppermute | solution.py:228
  36.8 5.3 %collective-permute-start.18 = (f32[192,112]{1,0:T(8,128)S(1)}, f32[192,112]{1,0:T(8,128)S(1)}, u32[]{:S(2)}, u32[]{:S(2)}) collective-permute-start(f32[192,112]{1,0:T(8,128)S(1)} %get-tuple-element.24), channel_id=1, source_target_pairs={{0,1},{1,0},{2,3},{3,2},{4,5},{5,4},{6,7},{7,6},{8,9},{9,8},{10,11... | collective-permute-start | bytes 258056 | tf_op jit(solution)/shard_map/ppermute | solution.py:225
  36.9 4.2 %collective-permute-start.19 = (bf16[192,112]{1,0:T(8,128)(2,1)S(1)}, bf16[192,112]{1,0:T(8,128)(2,1)S(1)}, u32[]{:S(2)}, u32[]{:S(2)}) collective-permute-start(bf16[192,112]{1,0:T(8,128)(2,1)S(1)} %get-tuple-element.25), channel_id=1, source_target_pairs={{0,2},{1,3},{2,0},{3,1},{4,6},{5,7},{6,4},{7,5},{8,10},{9,11},{10,... | collective-permute-start | bytes 129032 | tf_op jit(solution)/shard_map/ppermute | solution.py:228
  38.5 3.7 %collective-permute-start.20 = (bf16[192,112]{1,0:T(8,128)(2,1)S(1)}, bf16[192,112]{1,0:T(8,128)(2,1)S(1)}, u32[]{:S(2)}, u32[]{:S(2)}) collective-permute-start(bf16[192,112]{1,0:T(8,128)(2,1)S(1)} %get-tuple-element.26), channel_id=1, source_target_pairs={{0,3},{1,2},{2,1},{3,0},{4,7},{5,6},{6,5},{7,4},{8,11},{9,10},{10,... | collective-permute-start | bytes 129032 | tf_op jit(solution)/shard_map/ppermute | solution.py:228

commit v4 on v3

--- a/solution.py
+++ b/solution.py
@@ -12,6 +12,7 @@
 DEGREE = 6
 SCALE = 1.0 / math.sqrt(HEAD_DIM)
 VMEM = pl.BlockSpec(memory_space=pltpu.VMEM)
+ANY = pl.BlockSpec(memory_space=pl.ANY)
 SMEM = pl.BlockSpec(memory_space=pltpu.SMEM)
 BF16 = jnp.bfloat16
 F32 = jnp.float32
@@ -51,7 +52,7 @@
 
 
 def mark_kernel(block, out):
-    out[...] = block[:8, :128].astype(F32)
+    out[...] = block[:8, :128].astype(out.dtype)
 
 
 def memory_kernel(groups, *refs):
@@ -74,7 +75,8 @@
     normed_self[...] = (normed * g_self[...].reshape(1, -1)).astype(BF16)
 
 
-def self_kernel(normed, w_own, w_other, out_own, out_other, partial):
+def self_kernel(normed, w_own, w_other, out_own, out_other, *refs):
+    partial = refs[-1]
     member = position()[1]
     own = normed[...]
     rows = own.shape[0] // ROW_GROUPS
@@ -88,34 +90,30 @@
     partial[...] = total.astype(BF16)
 
 
-def hand_on(passed, handed, sems):
-    copies = [pltpu.make_async_copy(passed[i], handed[i], sems.at[i]) for i in range(len(passed))]
+def query_kernel(groups, x_rows, gain, w_own, w_other, *refs):
+    partials, packing, refs = refs[:groups], refs[groups : groups + 2], refs[groups + 2 :]
+    after, queries, packed, sems = refs
+    copies = [pltpu.make_async_copy(packing[i], packed.at[i], sems.at[i]) for i in range(2)]
     for copy in copies:
         copy.start()
-    return copies
-
-
-def cross_kernel(groups, views, count, x_rows, gain, w_own, w_other, *refs):
-    partials, refs = refs[:groups], refs[groups:]
-    kv_own, kv_other, refs = refs[:views], refs[views : 2 * views], refs[2 * views :]
-    passed, refs = refs[:count], refs[count:]
-    after, context, handed, sems = refs[0], refs[1], refs[2:-1], refs[-1]
-    if len(handed) < count:
-        handed = [handed[0].at[0], handed[0].at[1], *handed[1:]]
-    copies = hand_on(passed, handed, sems)
     total = x_rows[...]
     for partial in partials:
         total = total + partial[...].astype(F32)
     after[...] = total
     normed = (standardize(total) * gain[...].reshape(1, -1)).astype(BF16)
-    q = jnp.concatenate([mm(normed, w_own[0]), mm(normed, w_other[0])], axis=1).astype(BF16)
+    queries[...] = jnp.concatenate([mm(normed, w_own[0]), mm(normed, w_other[0])], axis=1).astype(BF16)
+    for copy in copies:
+        copy.wait()
+
+
+def cross_kernel(first, views, total, queries, *refs):
+    kv_own, kv_other, context = refs[first:], refs[total + first :], refs[-1]
+    q = queries[...]
     width = q.shape[1] // 2
     for view in range(views):
         k = jnp.concatenate([kv_own[view][:, :width], kv_other[view][:, :width]], axis=1)
         v = jnp.concatenate([kv_own[view][:, width:], kv_other[view][:, width:]], axis=1)
         context[view] = head_attention(q, k, v).astype(BF16)
-    for copy in copies:
-        copy.wait()
 
 
 def other_image(image, step, images):
@@ -140,22 +138,19 @@
     return counts
 
 
-def mlp_kernel(groups, images, listed, *refs):
-    contexts, refs = refs[:groups], refs[groups:]
-    views, _, width = contexts[0].shape
-    width = width // 2
-    w_out = refs[: 2 * groups]
-    after, gain, up_own, down_own = refs[2 * groups : 2 * groups + 4]
-    others = refs[2 * groups + 4 : -2 * groups - 2]
-    up_other, down_other = others if len(others) == 2 else (others[0].at[0], others[0].at[1])
-    outs, (kept, partial) = refs[-2 * groups - 2 : -2], refs[-2:]
+def mlp_kernel(groups, batches, shared, images, listed, *refs):
+    count = groups * len(batches)
+    contexts, w_out, refs = refs[:count], refs[count : count + 2 * groups], refs[count + 2 * groups :]
+    after, gain, mlp_own, mlp_other = refs[:4]
+    outs, (kept, partial) = refs[4:-2], refs[-2:]
+    views, width = sum(batches), contexts[0].shape[2] // 2
     group, member = position()
     rows = after.shape[0]
     column = after.shape[1] // (2 * groups)
     residual = after[...]
     total = jnp.concatenate([residual] * views, axis=0)
     for step in range(groups):
-        held = contexts[step][...].reshape(views * rows, 2 * width)
+        held = jnp.concatenate([block[...].reshape(-1, 2 * width) for block in contexts[step::groups]], axis=0)
         total = total + mm(held[:, :width], w_out[2 * step][...])
         total = total + mm(held[:, width:], w_out[2 * step + 1][...])
     if images:
@@ -168,13 +163,14 @@
     kept[...] = keep.T
     normed = (standardize(total) * gain[...].reshape(1, -1)).astype(BF16)
     down = jnp.zeros_like(residual)
-    for w_up, w_down in ((up_own, down_own), (up_other, down_other)):
-        raw = mm(normed, w_up[...])
+    for weights in (mlp_own, mlp_other):
+        raw = mm(normed, weights[0])
         hidden = (0.5 * raw * (1.0 + lax.erf(raw * math.sqrt(0.5)))).astype(BF16).astype(F32)
         added = jnp.zeros((rows, raw.shape[1]), F32)
         for view in range(views):
             added = added + share[view] * hidden[view * rows : (view + 1) * rows]
-        down = down + mm(added.astype(BF16), w_down[...])
+        w_down = weights[1] if shared else weights[1].T
+        down = down + mm(added.astype(BF16), w_down)
     partial[...] = down.T
     for step in range(groups):
         target = lax.rem(group + step, groups)
@@ -234,13 +230,14 @@
             ],
         )
 
-    def call(kernel, out_shape, args, scratch=(), smem=0, flops=0, moved=0):
+    def call(kernel, out_shape, args, scratch=(), smem=0, flops=0, moved=0, aliases={}):
         return pl.pallas_call(
             kernel,
             out_shape=out_shape,
-            in_specs=[SMEM] * smem + [VMEM] * (len(args) - smem),
-            out_specs=jax.tree.map(lambda _: VMEM, out_shape),
+            in_specs=[SMEM] * smem + [VMEM] * (len(args) - smem - len(aliases)) + [ANY] * len(aliases),
+            out_specs=[ANY if i in aliases.values() else VMEM for i in range(len(out_shape))],
             scratch_shapes=list(scratch),
+            input_output_aliases=aliases,
             compiler_params=pltpu.CompilerParams(vmem_limit_bytes=16 * 2**20),
             cost_estimate=pl.CostEstimate(flops=flops, bytes_accessed=moved, transcendentals=0),
         )(*args)
@@ -255,7 +252,8 @@
     self_other, self_out_other, cross_other = swap(w_self_qkv), swap(w_self_out), swap(w_cross_qkv)
     cross_out_other = swap(w_cross_out)
 
-    mark = call(mark_kernel, shape((8, 128), F32), [blocks[1]], flops=3 * 10**9)
+    (mark,) = call(mark_kernel, [shape((8, 128), F32)], [blocks[1]], flops=3 * 10**9)
+    (mark,) = call(mark_kernel, [shape((8, 128), F32)], [mark], flops=3 * 10**9)
     x_rows, normed_self, kv = call(
         lambda *refs: memory_kernel(groups, *refs),
         [shape((rows, model), F32), shape((tokens, model), BF16), shape((tokens, 2 * att), BF16)],
@@ -263,10 +261,10 @@
         scratch=[pltpu.VMEM((model, tokens), BF16)],
         flops=10**8,
     )
-    partial = call(
+    (partial,) = call(
         self_kernel,
-        shape((rows, model), BF16),
-        [normed_self, w_self_qkv, self_other, w_self_out, self_out_other],
+        [shape((rows, model), BF16)],
+        [normed_self, w_self_qkv, self_other, w_self_out, self_out_other, *turned],
         flops=10**8,
     )
 
@@ -291,37 +289,47 @@
         gathered = lax.all_gather(kv, "pair", axis=0, tiled=False)
         kv_own = [lax.dynamic_index_in_dim(gathered, memories[view], 0, False) for view in range(views)]
     partials = [partial] + [turn(partial, step) for step in range(1, groups)]
-    late = [w_up, w_down, *turned]
-    packed = w_up.shape == w_down.shape
-    late_shapes = [shape(value.shape, BF16) for value in late]
-    if packed:
-        late_shapes = [shape((2, *w_up.shape), BF16), *late_shapes[2:]]
-    after, context, *handed = call(
-        lambda *refs: cross_kernel(groups, views, len(late), *refs),
-        [shape((rows, model), F32), shape((views, rows, 2 * att), BF16)] + late_shapes,
-        [
-            x_rows,
-            gain_cross,
-            w_cross_qkv,
-            cross_other,
-            *partials,
-            *kv_own,
-            *[swap(value) for value in kv_own],
-            *late,
-        ],
-        scratch=[pltpu.SemaphoreType.DMA((len(late),))],
+    shared = w_up.shape == w_down.shape
+    w_down_as_up = w_down if shared else w_down.T
+    after, queries, packed = call(
+        lambda *refs: query_kernel(groups, *refs),
+        [shape((rows, model), F32), shape((rows, 2 * att), BF16), shape((2, *w_up.shape), BF16)],
+        [x_rows, gain_cross, w_cross_qkv, cross_other, *partials, w_up, w_down_as_up],
+        scratch=[pltpu.SemaphoreType.DMA((2,))],
         flops=10**8,
     )
-    handed = [swap(value) for value in handed]
-    mlp_other = handed[: 1 if packed else 2]
+    kv_other = [swap(value) for value in kv_own]
+    passing = [packed, *turned]
+    batches = [views - views // 3, views // 3] if views >= 3 else [views]
+    contexts, done = [], 0
+    for index, batch in enumerate(batches):
+        args = [queries, *kv_own, *kv_other]
+        out_shape = [shape((batch, rows, 2 * att), BF16)]
+        aliases = {}
+        if index == 0:
+            aliases = {len(args) + i: i for i in range(len(passing))}
+            args += passing
+            out_shape = [shape(value.shape, BF16) for value in passing] + out_shape
+        *passed, context = call(
+            lambda *refs, done=done, batch=batch: cross_kernel(done, batch, views, *refs),
+            out_shape,
+            args,
+            flops=10**8,
+            aliases=aliases,
+        )
+        if index == 0:
+            packed, turned = passed[0], passed[1:]
+        contexts.append([context] + [turn(context, step) for step in range(1, groups)])
+        done += batch
+    packed_other = swap(packed)
     cross_out = [w_cross_out, cross_out_other]
-    for step in range(groups - 1):
-        cross_out += [turned[step], handed[len(mlp_other) + step]]
-    contexts = [context] + [turn(context, step) for step in range(1, groups)]
+    for value in turned:
+        cross_out += [value, swap(value)]
+    contexts = [context for batch in contexts for context in batch]
     pieces = call(
-        lambda *refs: mlp_kernel(groups, images if static else 0, *refs),
+        lambda *refs: mlp_kernel(groups, batches, shared, images if static else 0, *refs),
         [shape((column, rows), F32)] * 2 + [shape((column, rows), BF16)] * (2 * groups - 2),
-        [listed, *contexts, *cross_out, after, gain_mlp, w_up, w_down, *mlp_other],
+        [listed, *contexts, *cross_out, after, gain_mlp, packed, packed_other],
         scratch=[pltpu.VMEM((model, rows), F32)] * 2,
         smem=1,
         flops=3 * 10**9,
@@ -329,7 +337,7 @@
     arrived = [pieces[0], swap(pieces[1])]
     for step in range(1, groups):
         arrived += [turn(pieces[2 * step], step), turn(pieces[2 * step + 1], step, 1)]
-    summed = call(lambda *refs: sum_kernel(groups, *refs), shape((column, tokens), F32), arrived)
+    (summed,) = call(lambda *refs: sum_kernel(groups, *refs), [shape((column, tokens), F32)], arrived)
     return summed.T[None]
 
 

time: 43.1 us -> 41.9 us (0.972)
  waiting for transfers between devices: 18.3 us -> 16 us
  starting transfers between devices: 15.6 us -> 16.3 us
    ppermute x6 -> x7, waiting for transfers between devices: 12.8 us -> 10.2 us  [turn(): lax.ppermute(value, 'head', [(i, (i // 2 + step) % groups * 2 + (i % 2 ^...]
    ppermute x6 -> x7, starting transfers between devices: 8.45 us -> 9.36 us  [turn(): lax.ppermute(value, 'head', [(i, (i // 2 + step) % groups * 2 + (i % 2 ^...]
    ppermute x12, waiting for transfers between devices: 1.02 us -> 1.54 us  [swap(): return lax.ppermute(value, 'head', [(i, i ^ 1) for i in range(head)])]
    pallas_call x6 -> x9, Pallas kernels: 8.83 us -> 9.04 us  [call(): pl.pallas_call(kernel, out_shape=out_shape, in_specs=[SMEM] * smem + [VME...]
  transfers between devices with their start and end apart: 21 -> 22, of which waited for: 8 -> 8; matrix products, arithmetic and copies ran while one was open for 0% -> 0% of each run, Pallas kernels for 5% -> 9%
where the time goes in v4:
time: 41.9 us; the launch traced here: 41.6 us
  starting transfers between devices  16.3 us (39%)
  waiting for transfers between devices  16 us (38%)
  Pallas kernels  9.04 us (22%)
    ppermute x7, waiting for transfers between devices, turn(): lax.ppermute(value, 'head', [(i, (i // 2 + step) % groups * 2 + (i % 2 ^...  10.2 us
    ppermute x7, starting transfers between devices, turn(): lax.ppermute(value, 'head', [(i, (i // 2 + step) % groups * 2 + (i % 2 ^...  9.36 us
    pallas_call x9, Pallas kernels, call(): pl.pallas_call(kernel, out_shape=out_shape, in_specs=[SMEM] * smem + [VME...  9.04 us
    ppermute x3, starting transfers between devices, body(): lax.ppermute(kv, 'pair', [(other_image(i, step, images), i) for i in rang...  4.4 us
    ppermute x3, waiting for transfers between devices, body(): lax.ppermute(kv, 'pair', [(other_image(i, step, images), i) for i in rang...  4.27 us
    ppermute x12, starting transfers between devices, swap(): return lax.ppermute(value, 'head', [(i, i ^ 1) for i in range(head)])  2.56 us
    ppermute x12, waiting for transfers between devices, swap(): return lax.ppermute(value, 'head', [(i, i ^ 1) for i in range(head)])  1.54 us
  transfers between devices with their start and end apart: 22, of which 8 were waited for; matrix products, arithmetic and copies ran while one was open for 0% of the time, Pallas kernels for 9%

profile of v4, /device:TPU:0, one launch (start us, length us, event | category | flops | bytes accessed | tf_op | source)
XLA Modules:
  0.0 41.6 jit_solution(3114149705058671219)
XLA Ops:
  0.0 2.9 %collective-permute-start.1 = (bf16[192,224]{1,0:T(8,128)(2,1)}, bf16[192,224]{1,0:T(8,128)(2,1)S(1)}, u32[]{:S(2)}, u32[]{:S(2)}) collective-permute-start(bf16[192,224]{1,0:T(8,128)(2,1)} %bitcast.7), channel_id=1, source_target_pairs={{0,2},{1,3},{2,0},{3,1},{4,6},{5,7},{6,4},{7,5},{8,10},{9,11},{10,... | collective-permute-start | bytes 258056 | tf_op jit(solution)/shard_map/ppermute | solution.py:224
  2.9 0.0 collective-permute-start
  2.9 0.5 %collective-permute-start.3 = (bf16[3,768,128]{2,1,0:T(8,128)(2,1)}, bf16[3,768,128]{2,1,0:T(8,128)(2,1)S(1)}, u32[]{:S(2)}, u32[]{:S(2)}) collective-permute-start(bf16[3,768,128]{2,1,0:T(8,128)(2,1)} %refs_2_.1), channel_id=1, source_target_pairs={{0,1},{1,0},{2,3},{3,2},{4,5},{5,4},{6,7},{7,6},{8,9},{9,8},{10,11... | collective-permute-start | bytes 1769480 | tf_op jit(solution)/shard_map/ppermute | solution.py:221
  3.5 0.0 collective-permute-start.4
  3.5 0.1 collective-permute-start.7
  3.6 2.5 %collective-permute-done.1.refs_2_ = bf16[192,224]{1,0:T(8,128)(2,1)S(1)} collective-permute-done((bf16[192,224]{1,0:T(8,128)(2,1)}, bf16[192,224]{1,0:T(8,128)(2,1)S(1)}, u32[]{:S(2)}, u32[]{:S(2)}) %collective-permute-start.1) | collective-permute-done | bytes 86048 | tf_op jit(solution)/shard_map/ppermute | solution.py:224
  6.1 0.0 collective-permute-start.5
  6.1 0.0 collective-permute-done.block.refs_1_
  6.1 0.5 %collective-permute-start.2 = (bf16[192,224]{1,0:T(8,128)(2,1)S(1)}, bf16[192,224]{1,0:T(8,128)(2,1)S(1)}, u32[]{:S(2)}, u32[]{:S(2)}) collective-permute-start(bf16[192,224]{1,0:T(8,128)(2,1)S(1)} %collective-permute-done.1.refs_2_), channel_id=1, source_target_pairs={{0,1},{1,0},{2,3},{3,2},{4,5},{5,4},{6,7},{7,6},{8,9},{9,8},{10,11... | collective-permute-start | bytes 258056 | tf_op jit(solution)/shard_map/ppermute | solution.py:221
  6.6 0.0 copy-start.7
  6.6 0.0 copy-start.3
  6.7 1.2 %collective-permute-done.2.refs_3_ = bf16[192,224]{1,0:T(8,128)(2,1)S(1)} collective-permute-done((bf16[192,224]{1,0:T(8,128)(2,1)S(1)}, bf16[192,224]{1,0:T(8,128)(2,1)S(1)}, u32[]{:S(2)}, u32[]{:S(2)}) %collective-permute-start.2) | collective-permute-done | bytes 86048 | tf_op jit(solution)/shard_map/ppermute | solution.py:221
  7.9 0.0 copy-done.4
  7.9 0.4 collective-permute-start.6
  8.3 0.0 collective-permute-done.4.refs_9_.refs_6_
  8.3 0.0 collective-permute-done.3.refs_8_.refs_3_
  8.3 0.0 copy-done
  8.3 0.0 copy-done.5
  8.3 0.0 copy-done.6
  8.3 0.0 copy-done.7
  8.3 0.7 %shard_map.120 = (f32[112,768]{1,0:T(8,128)S(1)}, bf16[224,768]{1,0:T(8,128)(2,1)S(1)}, bf16[224,256]{1,0:T(8,128)(2,1)S(1)}) custom-call(bf16[192,224]{1,0:T(8,128)(2,1)S(1)} %bitcast.9, bf16[192,224]{1,0:T(8,128)(2,1)S(1)} %collective-permute-done.block.refs_1_, bf16[192,224]{1,0:T(8,128)(2,1)S(1)} %collective-permute-done.1.refs_2_, ...), custom_call_target="tpu_custom_call" | custom-call | flops 100000000 | tf_op jit(solution)/shard_map/pallas_call | solution.py:234
  9.1 2.8 %collective-permute-start.9 = (bf16[224,256]{1,0:T(8,128)(2,1)S(1)}, bf16[224,256]{1,0:T(8,128)(2,1)S(1)}, u32[]{:S(2)}, u32[]{:S(2)}) collective-permute-start(bf16[224,256]{1,0:T(8,128)(2,1)S(1)} %get-tuple-element.21), channel_id=1, source_target_pairs={{8,0},{12,4},{0,8},{4,12},{9,1},{13,5},{1,9},{5,13},{10,2},{14,6},... | collective-permute-start | bytes 344072 | tf_op jit(solution)/shard_map/ppermute | solution.py:276
  11.9 1.3 %collective-permute-start.10 = (bf16[224,256]{1,0:T(8,128)(2,1)S(1)}, bf16[224,256]{1,0:T(8,128)(2,1)S(1)}, u32[]{:S(2)}, u32[]{:S(2)}) collective-permute-start(bf16[224,256]{1,0:T(8,128)(2,1)S(1)} %get-tuple-element.21), channel_id=1, source_target_pairs={{12,0},{8,4},{4,8},{0,12},{13,1},{9,5},{5,9},{1,13},{14,2},{10,6},... | collective-permute-start | bytes 344072 | tf_op jit(solution)/shard_map/ppermute | solution.py:276
  13.2 0.0 collective-permute-done.7.refs_0_.refs_8_
  13.3 0.2 collective-permute-start.11
  13.5 0.0 collective-permute-done.6.out_other
  13.5 0.0 collective-permute-done.5.w_other
  13.5 0.0 copy-done.3
  13.5 1.3 %shard_map.121.refs_4_ = bf16[112,768]{1,0:T(8,128)(2,1)S(1)} custom-call(bf16[224,768]{1,0:T(8,128)(2,1)S(1)} %get-tuple-element.19.normed, bf16[3,768,128]{2,1,0:T(8,128)(2,1)S(1)} %copy-done.3, bf16[3,768,128]{2,1,0:T(8,128)(2,1)S(1)} %collective-permute-done.5.w_other, bf16[128,768]{1,0:T(8,128)(2,1)S(1)} %copy-done.4, ...), custom_call_target="tpu_custom_call" | custom-call | flops 100000000 | tf_op jit(solution)/shard_map/pallas_call | solution.py:234
  14.8 2.1 %collective-permute-start.8 = (bf16[112,768]{1,0:T(8,128)(2,1)S(1)}, bf16[112,768]{1,0:T(8,128)(2,1)S(1)}, u32[]{:S(2)}, u32[]{:S(2)}) collective-permute-start(bf16[112,768]{1,0:T(8,128)(2,1)S(1)} %shard_map.121.refs_4_), channel_id=1, source_target_pairs={{0,2},{1,3},{2,0},{3,1},{4,6},{5,7},{6,4},{7,5},{8,10},{9,11},{10,... | collective-permute-start | bytes 516104 | tf_op jit(solution)/shard_map/ppermute | solution.py:224
  16.9 4.1 %collective-permute-done.9.refs_1_ = bf16[224,256]{1,0:T(8,128)(2,1)S(1)} collective-permute-done((bf16[224,256]{1,0:T(8,128)(2,1)S(1)}, bf16[224,256]{1,0:T(8,128)(2,1)S(1)}, u32[]{:S(2)}, u32[]{:S(2)}) %collective-permute-start.9) | collective-permute-done | bytes 114720 | tf_op jit(solution)/shard_map/ppermute | solution.py:276
  21.0 0.0 collective-permute-start.12
  21.0 0.0 collective-permute-done.10.refs_2_
  21.0 0.5 %collective-permute-start.13 = (bf16[224,256]{1,0:T(8,128)(2,1)S(1)}, bf16[224,256]{1,0:T(8,128)(2,1)S(1)}, u32[]{:S(2)}, u32[]{:S(2)}) collective-permute-start(bf16[224,256]{1,0:T(8,128)(2,1)S(1)} %collective-permute-done.10.refs_2_), channel_id=1, source_target_pairs={{0,1},{1,0},{2,3},{3,2},{4,5},{5,4},{6,7},{7,6},{8,9},{9,8},{10,11... | collective-permute-start | bytes 344072 | tf_op jit(solution)/shard_map/ppermute | solution.py:221
  21.5 0.2 collective-permute-done.11.refs_3_
  21.7 0.0 collective-permute-start.14
  21.7 0.0 collective-permute-done.8.refs_5_
  21.7 0.0 copy-done.1
  21.7 0.0 copy-done.2
  21.7 0.9 %shard_map.122 = (f32[112,768]{1,0:T(8,128)S(1)}, bf16[112,256]{1,0:T(8,128)(2,1)S(1)}, bf16[2,768,768]{2,1,0:T(8,128)(2,1)S(1)}) custom-call(f32[112,768]{1,0:T(8,128)S(1)} %get-tuple-element.18.refs_0_, f32[768]{0:T(1024)S(1)} %copy-done.8, bf16[3,768,128]{2,1,0:T(8,128)(2,1)S(1)} %copy-done, ...), custom_call_target="tpu_custom_call" | custom-call | flops 100000000 | tf_op jit(solution)/shard_map/pallas_call | solution.py:234
  22.6 0.0 copy-start.9
  22.7 0.0 copy-start.10
  22.7 0.0 copy-start.11
  22.7 0.0 collective-permute-done.12.refs_4_
  22.7 0.0 collective-permute-done.13.refs_5_
  22.7 0.3 collective-permute-done.14.refs_6_
  23.0 1.1 %shard_map.123 = (bf16[2,768,768]{2,1,0:T(8,128)(2,1)S(1)}, bf16[128,768]{1,0:T(8,128)(2,1)S(1)}, bf16[2,112,256]{2,1,0:T(8,128)(2,1)S(1)}) custom-call(bf16[112,256]{1,0:T(8,128)(2,1)S(1)} %get-tuple-element.20.refs_0_, bf16[224,256]{1,0:T(8,128)(2,1)S(1)} %collective-permute-done.9.refs_1_, ...), custom_call_target="tpu_custom_call", output_to_operand_aliasing={{0}: (7, {}), {1}: (8, {})} | custom-call | flops 100000000 | tf_op jit(solution)/shard_map/pallas_call | solution.py:234
  24.1 0.3 collective-permute-start.18
  24.4 0.3 collective-permute-start.17
  24.7 2.3 %collective-permute-start.15 = (bf16[2,112,256]{2,1,0:T(8,128)(2,1)S(1)}, bf16[2,112,256]{2,1,0:T(8,128)(2,1)S(1)}, u32[]{:S(2)}, u32[]{:S(2)}) collective-permute-start(bf16[2,112,256]{2,1,0:T(8,128)(2,1)S(1)} %get-tuple-element.23.refs_1_), channel_id=1, source_target_pairs={{0,2},{1,3},{2,0},{3,1},{4,6},{5,7},{6,4},{7,5},{8,10},{9,11},{10,... | collective-permute-start | bytes 344072 | tf_op jit(solution)/shard_map/ppermute | solution.py:224
  26.9 0.7 %shard_map.124.refs_3_ = bf16[1,112,256]{2,1,0:T(8,128)(2,1)S(1)} custom-call(bf16[112,256]{1,0:T(8,128)(2,1)S(1)} %get-tuple-element.20.refs_0_, bf16[224,256]{1,0:T(8,128)(2,1)S(1)} %collective-permute-done.9.refs_1_, bf16[224,256]{1,0:T(8,128)(2,1)S(1)} %collective-permute-done.10.refs_2_, bf16[224,256]{1,0:T(8,128)(2,1)S(1)} %collective-permute-done.11.refs_3_, ...), custom_call_target="tpu_custom_call" | custom-call | flops 100000000 | tf_op jit(solution)/shard_map/pallas_call | solution.py:234
  27.6 0.1 collective-permute-start.16
  27.7 4.2 %collective-permute-done.16.refs_4_ = bf16[1,112,256]{2,1,0:T(8,128)(2,1)S(1)} collective-permute-done((bf16[1,112,256]{2,1,0:T(8,128)(2,1)S(1)}, bf16[1,112,256]{2,1,0:T(8,128)(2,1)S(1)}, u32[]{:S(2)}, u32[]{:S(2)}) %collective-permute-start.16) | collective-permute-done | bytes 57376 | tf_op jit(solution)/shard_map/ppermute | solution.py:224
  31.8 0.0 collective-permute-done.15.refs_2_
  31.8 0.0 collective-permute-done.17.refs_8_
  31.8 0.0 collective-permute-done.18.refs_12_
  31.9 3.5 %shard_map.125 = (f32[192,112]{1,0:T(8,128)S(1)}, f32[192,112]{1,0:T(8,128)S(1)}, bf16[192,112]{1,0:T(8,128)(2,1)S(1)}, bf16[192,112]{1,0:T(8,128)(2,1)S(1)}) custom-call(s32[2,4]{1,0:T(2,128)S(1)} %bitcast.10, bf16[2,112,256]{2,1,0:T(8,128)(2,1)S(1)} %get-tuple-element.23.refs_1_, bf16[2,112,256]{2,1,0:T(8,128)(2,1)S(1)} %collective-permute-done.15.refs_2_, ...), custom_call_target="tpu_custom_call" | custom-call | flops 3000000000 | tf_op jit(solution)/shard_map/pallas_call | solution.py:234
  35.4 0.1 collective-permute-start.19
  35.5 1.7 %collective-permute-start.20 = (bf16[192,112]{1,0:T(8,128)(2,1)S(1)}, bf16[192,112]{1,0:T(8,128)(2,1)S(1)}, u32[]{:S(2)}, u32[]{:S(2)}) collective-permute-start(bf16[192,112]{1,0:T(8,128)(2,1)S(1)} %get-tuple-element.29), channel_id=1, source_target_pairs={{0,2},{1,3},{2,0},{3,1},{4,6},{5,7},{6,4},{7,5},{8,10},{9,11},{10,... | collective-permute-start | bytes 129032 | tf_op jit(solution)/shard_map/ppermute | solution.py:224
  37.2 0.2 collective-permute-start.21
  37.4 2.3 %collective-permute-done.20.refs_2_ = bf16[192,112]{1,0:T(8,128)(2,1)S(1)} collective-permute-done((bf16[192,112]{1,0:T(8,128)(2,1)S(1)}, bf16[192,112]{1,0:T(8,128)(2,1)S(1)}, u32[]{:S(2)}, u32[]{:S(2)}) %collective-permute-start.20) | collective-permute-done | bytes 43040 | tf_op jit(solution)/shard_map/ppermute | solution.py:224
  39.6 1.2 %collective-permute-done.21.refs_3_ = bf16[192,112]{1,0:T(8,128)(2,1)S(1)} collective-permute-done((bf16[192,112]{1,0:T(8,128)(2,1)S(1)}, bf16[192,112]{1,0:T(8,128)(2,1)S(1)}, u32[]{:S(2)}, u32[]{:S(2)}) %collective-permute-start.21) | collective-permute-done | bytes 43040 | tf_op jit(solution)/shard_map/ppermute | solution.py:224
  40.8 0.0 collective-permute-done.19.refs_1_
  40.9 0.8 %shard_map.126 = f32[192,224]{1,0:T(8,128)} custom-call(f32[192,112]{1,0:T(8,128)S(1)} %get-tuple-element.27.refs_0_, f32[192,112]{1,0:T(8,128)S(1)} %collective-permute-done.19.refs_1_, bf16[192,112]{1,0:T(8,128)(2,1)S(1)} %collective-permute-done.20.refs_2_, bf16[192,112]{1,0:T(8,128)(2,1)S(1)} %collective-permute-done.21.refs_3_), custom_call_target="tpu_custom_call" | custom-call | tf_op jit(solution)/shard_map/pallas_call | solution.py:234
  (13 shorter events, 0.0 us)
Async XLA Ops:
  0.0 7.9 %copy-start.4 = (bf16[128,768]{1,0:T(8,128)(2,1)S(1)}, bf16[128,768]{1,0:T(8,128)(2,1)}, u32[]{:S(2)}) copy-start(bf16[128,768]{1,0:T(8,128)(2,1)} %out_own.1) | copy-start | bytes 589828
  0.0 6.1 %collective-permute-start.1 = (bf16[192,224]{1,0:T(8,128)(2,1)}, bf16[192,224]{1,0:T(8,128)(2,1)S(1)}, u32[]{:S(2)}, u32[]{:S(2)}) collective-permute-start(bf16[192,224]{1,0:T(8,128)(2,1)} %bitcast.7), channel_id=1, source_target_pairs={{0,2},{1,3},{2,0},{3,1},{4,6},{5,7},{6,4},{7,5},{8,10},{9,11},{10,... | collective-permute-start | bytes 258056 | tf_op jit(solution)/shard_map/ppermute | solution.py:224
  2.9 3.2 %collective-permute-start = (bf16[192,224]{1,0:T(8,128)(2,1)}, bf16[192,224]{1,0:T(8,128)(2,1)S(1)}, u32[]{:S(2)}, u32[]{:S(2)}) collective-permute-start(bf16[192,224]{1,0:T(8,128)(2,1)} %bitcast.8), channel_id=1, source_target_pairs={{0,1},{1,0},{2,3},{3,2},{4,5},{5,4},{6,7},{7,6},{8,9},{9,8},{10,11... | collective-permute-start | bytes 258056 | tf_op jit(solution)/shard_map/ppermute | solution.py:221
  2.9 5.3 %collective-permute-start.3 = (bf16[3,768,128]{2,1,0:T(8,128)(2,1)}, bf16[3,768,128]{2,1,0:T(8,128)(2,1)S(1)}, u32[]{:S(2)}, u32[]{:S(2)}) collective-permute-start(bf16[3,768,128]{2,1,0:T(8,128)(2,1)} %refs_2_.1), channel_id=1, source_target_pairs={{0,1},{1,0},{2,3},{3,2},{4,5},{5,4},{6,7},{7,6},{8,9},{9,8},{10,11... | collective-permute-start | bytes 1769480 | tf_op jit(solution)/shard_map/ppermute | solution.py:221
  3.5 4.8 %collective-permute-start.4 = (bf16[128,768]{1,0:T(8,128)(2,1)}, bf16[128,768]{1,0:T(8,128)(2,1)S(1)}, u32[]{:S(2)}, u32[]{:S(2)}) collective-permute-start(bf16[128,768]{1,0:T(8,128)(2,1)} %refs_5_.3), channel_id=1, source_target_pairs={{0,1},{1,0},{2,3},{3,2},{4,5},{5,4},{6,7},{7,6},{8,9},{9,8},{10,11... | collective-permute-start | bytes 589832 | tf_op jit(solution)/shard_map/ppermute | solution.py:221
  3.5 9.8 %collective-permute-start.7 = (bf16[128,768]{1,0:T(8,128)(2,1)}, bf16[128,768]{1,0:T(8,128)(2,1)S(1)}, u32[]{:S(2)}, u32[]{:S(2)}) collective-permute-start(bf16[128,768]{1,0:T(8,128)(2,1)} %refs_5_.3), channel_id=1, source_target_pairs={{0,2},{1,3},{2,0},{3,1},{4,6},{5,7},{6,4},{7,5},{8,10},{9,11},{10,... | collective-permute-start | bytes 589832 | tf_op jit(solution)/shard_map/ppermute | solution.py:224
  6.1 7.4 %collective-permute-start.5 = (bf16[3,768,128]{2,1,0:T(8,128)(2,1)}, bf16[3,768,128]{2,1,0:T(8,128)(2,1)S(1)}, u32[]{:S(2)}, u32[]{:S(2)}) collective-permute-start(bf16[3,768,128]{2,1,0:T(8,128)(2,1)} %w_own.1), channel_id=1, source_target_pairs={{0,1},{1,0},{2,3},{3,2},{4,5},{5,4},{6,7},{7,6},{8,9},{9,8},{10,11... | collective-permute-start | bytes 1769480 | tf_op jit(solution)/shard_map/ppermute | solution.py:221
  6.1 1.8 %collective-permute-start.2 = (bf16[192,224]{1,0:T(8,128)(2,1)S(1)}, bf16[192,224]{1,0:T(8,128)(2,1)S(1)}, u32[]{:S(2)}, u32[]{:S(2)}) collective-permute-start(bf16[192,224]{1,0:T(8,128)(2,1)S(1)} %collective-permute-done.1.refs_2_), channel_id=1, source_target_pairs={{0,1},{1,0},{2,3},{3,2},{4,5},{5,4},{6,7},{7,6},{8,9},{9,8},{10,11... | collective-permute-start | bytes 258056 | tf_op jit(solution)/shard_map/ppermute | solution.py:221
  6.6 1.7 %copy-start = (bf16[3,768,128]{2,1,0:T(8,128)(2,1)S(1)}, bf16[3,768,128]{2,1,0:T(8,128)(2,1)}, u32[]{:S(2)}) copy-start(bf16[3,768,128]{2,1,0:T(8,128)(2,1)} %refs_2_.1) | copy-start | bytes 1769476
  6.6 1.7 %copy-start.5 = (bf16[1,224,192]{1,2,0:T(8,128)(2,1)S(1)}, bf16[1,224,192]{1,2,0:T(8,128)(2,1)}, u32[]{:S(2)}) copy-start(bf16[1,224,192]{1,2,0:T(8,128)(2,1)} %param.12) | copy-start | bytes 258052
  6.6 1.7 %copy-start.6 = (f32[768]{0:T(1024)S(1)}, f32[768]{0:T(1024)}, u32[]{:S(2)}) copy-start(f32[768]{0:T(1024)} %refs_4_.1) | copy-start | bytes 9220
  6.6 1.7 %copy-start.7 = (f32[768]{0:T(1024)S(1)}, f32[768]{0:T(1024)}, u32[]{:S(2)}) copy-start(f32[768]{0:T(1024)} %refs_5_.2) | copy-start | bytes 9220
  6.6 6.8 %copy-start.3 = (bf16[3,768,128]{2,1,0:T(8,128)(2,1)S(1)}, bf16[3,768,128]{2,1,0:T(8,128)(2,1)}, u32[]{:S(2)}) copy-start(bf16[3,768,128]{2,1,0:T(8,128)(2,1)} %w_own.1) | copy-start | bytes 1769476
  7.9 5.6 %collective-permute-start.6 = (bf16[128,768]{1,0:T(8,128)(2,1)S(1)}, bf16[128,768]{1,0:T(8,128)(2,1)S(1)}, u32[]{:S(2)}, u32[]{:S(2)}) collective-permute-start(bf16[128,768]{1,0:T(8,128)(2,1)S(1)} %copy-done.4), channel_id=1, source_target_pairs={{0,1},{1,0},{2,3},{3,2},{4,5},{5,4},{6,7},{7,6},{8,9},{9,8},{10,11... | collective-permute-start | bytes 589832 | tf_op jit(solution)/shard_map/ppermute | solution.py:221
  8.3 13.4 %copy-start.1 = (bf16[768,768]{1,0:T(8,128)(2,1)S(1)}, bf16[768,768]{1,0:T(8,128)(2,1)}, u32[]{:S(2)}) copy-start(bf16[768,768]{1,0:T(8,128)(2,1)} %refs_6_.3) | copy-start | bytes 3538948
  8.3 13.4 %copy-start.2 = (bf16[768,768]{1,0:T(8,128)(2,1)S(1)}, bf16[768,768]{1,0:T(8,128)(2,1)}, u32[]{:S(2)}) copy-start(bf16[768,768]{1,0:T(8,128)(2,1)} %refs_7_.1) | copy-start | bytes 3538948
  8.3 13.4 %copy-start.8 = (f32[768]{0:T(1024)S(1)}, f32[768]{0:T(1024)}, u32[]{:S(2)}) copy-start(f32[768]{0:T(1024)} %refs_1_.1) | copy-start | bytes 9220
  9.1 11.9 %collective-permute-start.9 = (bf16[224,256]{1,0:T(8,128)(2,1)S(1)}, bf16[224,256]{1,0:T(8,128)(2,1)S(1)}, u32[]{:S(2)}, u32[]{:S(2)}) collective-permute-start(bf16[224,256]{1,0:T(8,128)(2,1)S(1)} %get-tuple-element.21), channel_id=1, source_target_pairs={{8,0},{12,4},{0,8},{4,12},{9,1},{13,5},{1,9},{5,13},{10,2},{14,6},... | collective-permute-start | bytes 344072 | tf_op jit(solution)/shard_map/ppermute | solution.py:276
  11.9 9.1 %collective-permute-start.10 = (bf16[224,256]{1,0:T(8,128)(2,1)S(1)}, bf16[224,256]{1,0:T(8,128)(2,1)S(1)}, u32[]{:S(2)}, u32[]{:S(2)}) collective-permute-start(bf16[224,256]{1,0:T(8,128)(2,1)S(1)} %get-tuple-element.21), channel_id=1, source_target_pairs={{12,0},{8,4},{4,8},{0,12},{13,1},{9,5},{5,9},{1,13},{14,2},{10,6},... | collective-permute-start | bytes 344072 | tf_op jit(solution)/shard_map/ppermute | solution.py:276
  13.3 8.4 %collective-permute-start.11 = (bf16[224,256]{1,0:T(8,128)(2,1)S(1)}, bf16[224,256]{1,0:T(8,128)(2,1)S(1)}, u32[]{:S(2)}, u32[]{:S(2)}) collective-permute-start(bf16[224,256]{1,0:T(8,128)(2,1)S(1)} %get-tuple-element.21), channel_id=1, source_target_pairs={{4,0},{0,4},{12,8},{8,12},{5,1},{1,5},{13,9},{9,13},{6,2},{2,6},{1... | collective-permute-start | bytes 344072 | tf_op jit(solution)/shard_map/ppermute | solution.py:276
  14.8 6.9 %collective-permute-start.8 = (bf16[112,768]{1,0:T(8,128)(2,1)S(1)}, bf16[112,768]{1,0:T(8,128)(2,1)S(1)}, u32[]{:S(2)}, u32[]{:S(2)}) collective-permute-start(bf16[112,768]{1,0:T(8,128)(2,1)S(1)} %shard_map.121.refs_4_), channel_id=1, source_target_pairs={{0,2},{1,3},{2,0},{3,1},{4,6},{5,7},{6,4},{7,5},{8,10},{9,11},{10,... | collective-permute-start | bytes 516104 | tf_op jit(solution)/shard_map/ppermute | solution.py:224
  21.0 1.7 %collective-permute-start.12 = (bf16[224,256]{1,0:T(8,128)(2,1)S(1)}, bf16[224,256]{1,0:T(8,128)(2,1)S(1)}, u32[]{:S(2)}, u32[]{:S(2)}) collective-permute-start(bf16[224,256]{1,0:T(8,128)(2,1)S(1)} %collective-permute-done.9.refs_1_), channel_id=1, source_target_pairs={{0,1},{1,0},{2,3},{3,2},{4,5},{5,4},{6,7},{7,6},{8,9},{9,8},{10,11... | collective-permute-start | bytes 344072 | tf_op jit(solution)/shard_map/ppermute | solution.py:221
  21.0 1.7 %collective-permute-start.13 = (bf16[224,256]{1,0:T(8,128)(2,1)S(1)}, bf16[224,256]{1,0:T(8,128)(2,1)S(1)}, u32[]{:S(2)}, u32[]{:S(2)}) collective-permute-start(bf16[224,256]{1,0:T(8,128)(2,1)S(1)} %collective-permute-done.10.refs_2_), channel_id=1, source_target_pairs={{0,1},{1,0},{2,3},{3,2},{4,5},{5,4},{6,7},{7,6},{8,9},{9,8},{10,11... | collective-permute-start | bytes 344072 | tf_op jit(solution)/shard_map/ppermute | solution.py:221
  21.7 1.3 %collective-permute-start.14 = (bf16[224,256]{1,0:T(8,128)(2,1)S(1)}, bf16[224,256]{1,0:T(8,128)(2,1)S(1)}, u32[]{:S(2)}, u32[]{:S(2)}) collective-permute-start(bf16[224,256]{1,0:T(8,128)(2,1)S(1)} %collective-permute-done.11.refs_3_), channel_id=1, source_target_pairs={{0,1},{1,0},{2,3},{3,2},{4,5},{5,4},{6,7},{7,6},{8,9},{9,8},{10,11... | collective-permute-start | bytes 344072 | tf_op jit(solution)/shard_map/ppermute | solution.py:221
  22.6 9.2 %copy-start.9 = (bf16[128,768]{1,0:T(8,128)(2,1)S(1)}, bf16[128,768]{1,0:T(8,128)(2,1)}, u32[]{:S(2)}) copy-start(bf16[128,768]{1,0:T(8,128)(2,1)} %refs_5_.3) | copy-start | bytes 589828
  22.7 9.2 %copy-start.10 = (f32[768]{0:T(1024)S(1)}, f32[768]{0:T(1024)}, u32[]{:S(2)}) copy-start(f32[768]{0:T(1024)} %refs_10_.1) | copy-start | bytes 9220
  22.7 9.2 %copy-start.11 = (s32[4,2]{0,1:T(2,128)S(1)}, s32[4,2]{0,1:T(2,128)}, u32[]{:S(2)}) copy-start(s32[4,2]{0,1:T(2,128)} %param.13) | copy-start | bytes 100
  24.1 7.7 %collective-permute-start.18 = (bf16[2,768,768]{2,1,0:T(8,128)(2,1)S(1)}, bf16[2,768,768]{2,1,0:T(8,128)(2,1)S(1)}, u32[]{:S(2)}, u32[]{:S(2)}) collective-permute-start(bf16[2,768,768]{2,1,0:T(8,128)(2,1)S(1)} %get-tuple-element.26.refs_11_), channel_id=1, source_target_pairs={{0,1},{1,0},{2,3},{3,2},{4,5},{5,4},{6,7},{7,6},{8,9},{9,8},{10,11... | collective-permute-start | bytes 7077896 | tf_op jit(solution)/shard_map/ppermute | solution.py:221
  24.4 7.4 %collective-permute-start.17 = (bf16[128,768]{1,0:T(8,128)(2,1)S(1)}, bf16[128,768]{1,0:T(8,128)(2,1)S(1)}, u32[]{:S(2)}, u32[]{:S(2)}) collective-permute-start(bf16[128,768]{1,0:T(8,128)(2,1)S(1)} %get-tuple-element.24.refs_7_), channel_id=1, source_target_pairs={{0,1},{1,0},{2,3},{3,2},{4,5},{5,4},{6,7},{7,6},{8,9},{9,8},{10,11... | collective-permute-start | bytes 589832 | tf_op jit(solution)/shard_map/ppermute | solution.py:221
  24.7 7.2 %collective-permute-start.15 = (bf16[2,112,256]{2,1,0:T(8,128)(2,1)S(1)}, bf16[2,112,256]{2,1,0:T(8,128)(2,1)S(1)}, u32[]{:S(2)}, u32[]{:S(2)}) collective-permute-start(bf16[2,112,256]{2,1,0:T(8,128)(2,1)S(1)} %get-tuple-element.23.refs_1_), channel_id=1, source_target_pairs={{0,2},{1,3},{2,0},{3,1},{4,6},{5,7},{6,4},{7,5},{8,10},{9,11},{10,... | collective-permute-start | bytes 344072 | tf_op jit(solution)/shard_map/ppermute | solution.py:224
  27.6 4.2 %collective-permute-start.16 = (bf16[1,112,256]{2,1,0:T(8,128)(2,1)S(1)}, bf16[1,112,256]{2,1,0:T(8,128)(2,1)S(1)}, u32[]{:S(2)}, u32[]{:S(2)}) collective-permute-start(bf16[1,112,256]{2,1,0:T(8,128)(2,1)S(1)} %shard_map.124.refs_3_), channel_id=1, source_target_pairs={{0,2},{1,3},{2,0},{3,1},{4,6},{5,7},{6,4},{7,5},{8,10},{9,11},{10,... | collective-permute-start | bytes 172040 | tf_op jit(solution)/shard_map/ppermute | solution.py:224
  35.4 5.4 %collective-permute-start.19 = (f32[192,112]{1,0:T(8,128)S(1)}, f32[192,112]{1,0:T(8,128)S(1)}, u32[]{:S(2)}, u32[]{:S(2)}) collective-permute-start(f32[192,112]{1,0:T(8,128)S(1)} %get-tuple-element.28), channel_id=1, source_target_pairs={{0,1},{1,0},{2,3},{3,2},{4,5},{5,4},{6,7},{7,6},{8,9},{9,8},{10,11... | collective-permute-start | bytes 258056 | tf_op jit(solution)/shard_map/ppermute | solution.py:221
  35.5 4.2 %collective-permute-start.20 = (bf16[192,112]{1,0:T(8,128)(2,1)S(1)}, bf16[192,112]{1,0:T(8,128)(2,1)S(1)}, u32[]{:S(2)}, u32[]{:S(2)}) collective-permute-start(bf16[192,112]{1,0:T(8,128)(2,1)S(1)} %get-tuple-element.29), channel_id=1, source_target_pairs={{0,2},{1,3},{2,0},{3,1},{4,6},{5,7},{6,4},{7,5},{8,10},{9,11},{10,... | collective-permute-start | bytes 129032 | tf_op jit(solution)/shard_map/ppermute | solution.py:224
  37.2 3.7 %collective-permute-start.21 = (bf16[192,112]{1,0:T(8,128)(2,1)S(1)}, bf16[192,112]{1,0:T(8,128)(2,1)S(1)}, u32[]{:S(2)}, u32[]{:S(2)}) collective-permute-start(bf16[192,112]{1,0:T(8,128)(2,1)S(1)} %get-tuple-element.30), channel_id=1, source_target_pairs={{0,3},{1,2},{2,1},{3,0},{4,7},{5,6},{6,5},{7,4},{8,11},{9,10},{10,... | collective-permute-start | bytes 129032 | tf_op jit(solution)/shard_map/ppermute | solution.py:224

commit v5 on v4

--- a/solution.py
+++ b/solution.py
@@ -75,8 +75,11 @@
     normed_self[...] = (normed * g_self[...].reshape(1, -1)).astype(BF16)
 
 
-def self_kernel(normed, w_own, w_other, out_own, out_other, *refs):
-    partial = refs[-1]
+def self_kernel(groups, normed, w_own, w_other, out_own, out_other, *refs):
+    packing, (partial, packed, sems) = refs[:groups], refs[groups:]
+    copies = [pltpu.make_async_copy(packing[i], packed.at[i], sems.at[i]) for i in range(groups)]
+    for copy in copies:
+        copy.start()
     member = position()[1]
     own = normed[...]
     rows = own.shape[0] // ROW_GROUPS
@@ -88,6 +91,8 @@
     width = context.shape[1] // 2
     total = mm(context[:, :width], out_own[...]) + mm(context[:, width:], out_other[...])
     partial[...] = total.astype(BF16)
+    for copy in copies:
+        copy.wait()
 
 
 def query_kernel(groups, x_rows, gain, w_own, w_other, *refs):
@@ -140,19 +145,24 @@
 
 def mlp_kernel(groups, batches, shared, images, listed, *refs):
     count = groups * len(batches)
-    contexts, w_out, refs = refs[:count], refs[count : count + 2 * groups], refs[count + 2 * groups :]
-    after, gain, mlp_own, mlp_other = refs[:4]
-    outs, (kept, partial) = refs[4:-2], refs[-2:]
-    views, width = sum(batches), contexts[0].shape[2] // 2
+    contexts, refs = refs[:count], refs[count:]
+    out_own, out_other, after, gain, mlp_own, mlp_other = refs[:6]
+    outs, partial = refs[6:-1], refs[-1]
+    views = sum(batches)
     group, member = position()
     rows = after.shape[0]
     column = after.shape[1] // (2 * groups)
     residual = after[...]
-    total = jnp.concatenate([residual] * views, axis=0)
-    for step in range(groups):
-        held = jnp.concatenate([block[...].reshape(-1, 2 * width) for block in contexts[step::groups]], axis=0)
-        total = total + mm(held[:, :width], w_out[2 * step][...])
-        total = total + mm(held[:, width:], w_out[2 * step + 1][...])
+    held = jnp.concatenate(
+        [
+            jnp.concatenate([contexts[groups * batch + step][view] for step in range(groups)], axis=1)
+            for batch in range(len(batches))
+            for view in range(batches[batch])
+        ],
+        axis=0,
+    )
+    weight = jnp.concatenate([block[step] for step in range(groups) for block in (out_own, out_other)], axis=0)
+    total = jnp.concatenate([residual] * views, axis=0) + mm(held, weight)
     if images:
         share = view_counts(images, listed)
     else:
@@ -160,7 +170,6 @@
     keep = jnp.zeros_like(residual)
     for view in range(views):
         keep = keep + share[view] * total[view * rows : (view + 1) * rows]
-    kept[...] = keep.T
     normed = (standardize(total) * gain[...].reshape(1, -1)).astype(BF16)
     down = jnp.zeros_like(residual)
     for weights in (mlp_own, mlp_other):
@@ -171,16 +180,14 @@
             added = added + share[view] * hidden[view * rows : (view + 1) * rows]
         w_down = weights[1] if shared else weights[1].T
         down = down + mm(added.astype(BF16), w_down)
-    partial[...] = down.T
+    source = lax.broadcasted_iota(jnp.int32, down.shape, 1) // (2 * column)
+    partial[...] = jnp.where(source == group, down + keep, down).T
     for step in range(groups):
         target = lax.rem(group + step, groups)
         for other in range(2):
             index = target * 2 + (member if other == 0 else 1 - member)
             here = pl.ds(pl.multiple_of(index * column, column), column)
-            piece = partial[here, :]
-            if step == 0:
-                piece = piece + kept[here, :]
-            outs[2 * step + other][...] = piece.astype(outs[2 * step + other].dtype)
+            outs[2 * step + other][...] = partial[here, :].astype(outs[2 * step + other].dtype)
 
 
 def sum_kernel(groups, *refs):
@@ -250,21 +257,21 @@
         blocks += [arrived, swap(arrived)]
     turned = [turn(w_cross_out, step) for step in range(1, groups)]
     self_other, self_out_other, cross_other = swap(w_self_qkv), swap(w_self_out), swap(w_cross_qkv)
-    cross_out_other = swap(w_cross_out)
 
     (mark,) = call(mark_kernel, [shape((8, 128), F32)], [blocks[1]], flops=3 * 10**9)
     (mark,) = call(mark_kernel, [shape((8, 128), F32)], [mark], flops=3 * 10**9)
     x_rows, normed_self, kv = call(
         lambda *refs: memory_kernel(groups, *refs),
         [shape((rows, model), F32), shape((tokens, model), BF16), shape((tokens, 2 * att), BF16)],
-        [*blocks, gain_self, gain_memory, w_cross_qkv, mark, cross_other, cross_out_other],
+        [*blocks, gain_self, gain_memory, w_cross_qkv, mark, cross_other],
         scratch=[pltpu.VMEM((model, tokens), BF16)],
         flops=10**8,
     )
-    (partial,) = call(
-        self_kernel,
-        [shape((rows, model), BF16)],
-        [normed_self, w_self_qkv, self_other, w_self_out, self_out_other, *turned],
+    partial, out_own = call(
+        lambda *refs: self_kernel(groups, *refs),
+        [shape((rows, model), BF16), shape((groups, *w_cross_out.shape), BF16)],
+        [normed_self, w_self_qkv, self_other, w_self_out, self_out_other, w_cross_out, *turned],
+        scratch=[pltpu.SemaphoreType.DMA((groups,))],
         flops=10**8,
     )
 
@@ -291,7 +298,7 @@
     partials = [partial] + [turn(partial, step) for step in range(1, groups)]
     shared = w_up.shape == w_down.shape
     w_down_as_up = w_down if shared else w_down.T
-    after, queries, packed = call(
+    after, queries, mlp_own = call(
         lambda *refs: query_kernel(groups, *refs),
         [shape((rows, model), F32), shape((rows, 2 * att), BF16), shape((2, *w_up.shape), BF16)],
         [x_rows, gain_cross, w_cross_qkv, cross_other, *partials, w_up, w_down_as_up],
@@ -299,7 +306,6 @@
         flops=10**8,
     )
     kv_other = [swap(value) for value in kv_own]
-    passing = [packed, *turned]
     batches = [views - views // 3, views // 3] if views >= 3 else [views]
     contexts, done = [], 0
     for index, batch in enumerate(batches):
@@ -307,7 +313,8 @@
         out_shape = [shape((batch, rows, 2 * att), BF16)]
         aliases = {}
         if index == 0:
-            aliases = {len(args) + i: i for i in range(len(passing))}
+            passing = [mlp_own, out_own]
+            aliases = {len(args) + i: i for i in range(2)}
             args += passing
             out_shape = [shape(value.shape, BF16) for value in passing] + out_shape
         *passed, context = call(
@@ -318,19 +325,15 @@
             aliases=aliases,
         )
         if index == 0:
-            packed, turned = passed[0], passed[1:]
+            mlp_own, out_own = passed
         contexts.append([context] + [turn(context, step) for step in range(1, groups)])
         done += batch
-    packed_other = swap(packed)
-    cross_out = [w_cross_out, cross_out_other]
-    for value in turned:
-        cross_out += [value, swap(value)]
     contexts = [context for batch in contexts for context in batch]
     pieces = call(
         lambda *refs: mlp_kernel(groups, batches, shared, images if static else 0, *refs),
         [shape((column, rows), F32)] * 2 + [shape((column, rows), BF16)] * (2 * groups - 2),
-        [listed, *contexts, *cross_out, after, gain_mlp, packed, packed_other],
-        scratch=[pltpu.VMEM((model, rows), F32)] * 2,
+        [listed, *contexts, out_own, swap(out_own), after, gain_mlp, mlp_own, swap(mlp_own)],
+        scratch=[pltpu.VMEM((model, rows), F32)],
         smem=1,
         flops=3 * 10**9,
     )

time: 41.9 us -> 41 us (0.979)
  waiting for transfers between devices: 16 us -> 15.2 us
    ppermute x7, waiting for transfers between devices: 10.2 us -> 9.71 us  [turn(): lax.ppermute(value, 'head', [(i, (i // 2 + step) % groups * 2 + (i % 2 ^...]
    ppermute x12 -> x11, starting transfers between devices: 2.56 us -> 2.35 us  [swap(): return lax.ppermute(value, 'head', [(i, i ^ 1) for i in range(head)])]
    ppermute x12 -> x11, waiting for transfers between devices: 1.54 us -> 1.49 us  [swap(): return lax.ppermute(value, 'head', [(i, i ^ 1) for i in range(head)])]
  transfers between devices with their start and end apart: 22 -> 21, of which waited for: 8 -> 8; matrix products, arithmetic and copies ran while one was open for 0% -> 0% of each run, Pallas kernels for 9% -> 10%
where the time goes in v5:
time: 41 us; the launch traced here: 40.6 us
  starting transfers between devices  16 us (39%)
  waiting for transfers between devices  15.2 us (37%)
  Pallas kernels  9.07 us (22%)
    ppermute x7, waiting for transfers between devices, turn(): lax.ppermute(value, 'head', [(i, (i // 2 + step) % groups * 2 + (i % 2 ^...  9.71 us
    ppermute x7, starting transfers between devices, turn(): lax.ppermute(value, 'head', [(i, (i // 2 + step) % groups * 2 + (i % 2 ^...  9.12 us
    pallas_call x9, Pallas kernels, call(): pl.pallas_call(kernel, out_shape=out_shape, in_specs=[SMEM] * smem + [VME...  9.07 us
    ppermute x3, starting transfers between devices, body(): lax.ppermute(kv, 'pair', [(other_image(i, step, images), i) for i in rang...  4.52 us
    ppermute x3, waiting for transfers between devices, body(): lax.ppermute(kv, 'pair', [(other_image(i, step, images), i) for i in rang...  4 us
    ppermute x11, starting transfers between devices, swap(): return lax.ppermute(value, 'head', [(i, i ^ 1) for i in range(head)])  2.35 us
    ppermute x11, waiting for transfers between devices, swap(): return lax.ppermute(value, 'head', [(i, i ^ 1) for i in range(head)])  1.49 us
  transfers between devices with their start and end apart: 21, of which 8 were waited for; matrix products, arithmetic and copies ran while one was open for 0% of the time, Pallas kernels for 10%

profile of v5, /device:TPU:0, one launch (start us, length us, event | category | flops | bytes accessed | tf_op | source)
XLA Modules:
  0.0 40.6 jit_solution(5200683321870290964)
XLA Ops:
  0.0 0.5 %collective-permute-start = (bf16[192,224]{1,0:T(8,128)(2,1)}, bf16[192,224]{1,0:T(8,128)(2,1)S(1)}, u32[]{:S(2)}, u32[]{:S(2)}) collective-permute-start(bf16[192,224]{1,0:T(8,128)(2,1)} %bitcast.7), channel_id=1, source_target_pairs={{0,1},{1,0},{2,3},{3,2},{4,5},{5,4},{6,7},{7,6},{8,9},{9,8},{10,11... | collective-permute-start | bytes 258056 | tf_op jit(solution)/shard_map/ppermute | solution.py:228
  0.5 2.5 %collective-permute-start.1 = (bf16[192,224]{1,0:T(8,128)(2,1)}, bf16[192,224]{1,0:T(8,128)(2,1)S(1)}, u32[]{:S(2)}, u32[]{:S(2)}) collective-permute-start(bf16[192,224]{1,0:T(8,128)(2,1)} %bitcast.8), channel_id=1, source_target_pairs={{0,2},{1,3},{2,0},{3,1},{4,6},{5,7},{6,4},{7,5},{8,10},{9,11},{10,... | collective-permute-start | bytes 258056 | tf_op jit(solution)/shard_map/ppermute | solution.py:231
  2.9 0.2 collective-permute-start.3
  3.2 0.3 collective-permute-start.4
  3.5 0.2 collective-permute-start.5
  3.7 0.0 collective-permute-done.block.refs_1_
  3.7 0.8 %collective-permute-start.6 = (bf16[128,768]{1,0:T(8,128)(2,1)}, bf16[128,768]{1,0:T(8,128)(2,1)S(1)}, u32[]{:S(2)}, u32[]{:S(2)}) collective-permute-start(bf16[128,768]{1,0:T(8,128)(2,1)} %refs_5_.3), channel_id=1, source_target_pairs={{0,2},{1,3},{2,0},{3,1},{4,6},{5,7},{6,4},{7,5},{8,10},{9,11},{10,... | collective-permute-start | bytes 589832 | tf_op jit(solution)/shard_map/ppermute | solution.py:231
  4.5 2.2 %collective-permute-done.1.refs_2_ = bf16[192,224]{1,0:T(8,128)(2,1)S(1)} collective-permute-done((bf16[192,224]{1,0:T(8,128)(2,1)}, bf16[192,224]{1,0:T(8,128)(2,1)S(1)}, u32[]{:S(2)}, u32[]{:S(2)}) %collective-permute-start.1) | collective-permute-done | bytes 86048 | tf_op jit(solution)/shard_map/ppermute | solution.py:231
  6.6 0.0 collective-permute-start.2
  6.6 0.0 copy-start.6
  6.6 0.0 copy-start.7
  6.7 0.0 copy-start.8
  6.7 0.0 copy-start.3
  6.7 0.0 copy-start.4
  6.7 0.0 copy-start.5
  6.7 0.0 copy-start.1
  6.7 0.0 copy-start.2
  6.7 0.0 copy-start.9
  6.7 1.2 %collective-permute-done.2.refs_3_ = bf16[192,224]{1,0:T(8,128)(2,1)S(1)} collective-permute-done((bf16[192,224]{1,0:T(8,128)(2,1)S(1)}, bf16[192,224]{1,0:T(8,128)(2,1)S(1)}, u32[]{:S(2)}, u32[]{:S(2)}) %collective-permute-start.2) | collective-permute-done | bytes 86048 | tf_op jit(solution)/shard_map/ppermute | solution.py:228
  7.9 0.0 collective-permute-done.3.refs_8_.refs_3_
  7.9 0.0 copy-done
  8.0 0.7 %shard_map.120 = (f32[112,768]{1,0:T(8,128)S(1)}, bf16[224,768]{1,0:T(8,128)(2,1)S(1)}, bf16[224,256]{1,0:T(8,128)(2,1)S(1)}) custom-call(bf16[192,224]{1,0:T(8,128)(2,1)S(1)} %bitcast.9, bf16[192,224]{1,0:T(8,128)(2,1)S(1)} %collective-permute-done.block.refs_1_, bf16[192,224]{1,0:T(8,128)(2,1)S(1)} %collective-permute-done.1.refs_2_, ...), custom_call_target="tpu_custom_call" | custom-call | flops 100000000 | tf_op jit(solution)/shard_map/pallas_call | solution.py:241
  8.7 2.9 %collective-permute-start.8 = (bf16[224,256]{1,0:T(8,128)(2,1)S(1)}, bf16[224,256]{1,0:T(8,128)(2,1)S(1)}, u32[]{:S(2)}, u32[]{:S(2)}) collective-permute-start(bf16[224,256]{1,0:T(8,128)(2,1)S(1)} %get-tuple-element.24), channel_id=1, source_target_pairs={{8,0},{12,4},{0,8},{4,12},{9,1},{13,5},{1,9},{5,13},{10,2},{14,6},... | collective-permute-start | bytes 344072 | tf_op jit(solution)/shard_map/ppermute | solution.py:283
  11.6 1.4 %collective-permute-start.9 = (bf16[224,256]{1,0:T(8,128)(2,1)S(1)}, bf16[224,256]{1,0:T(8,128)(2,1)S(1)}, u32[]{:S(2)}, u32[]{:S(2)}) collective-permute-start(bf16[224,256]{1,0:T(8,128)(2,1)S(1)} %get-tuple-element.24), channel_id=1, source_target_pairs={{12,0},{8,4},{4,8},{0,12},{13,1},{9,5},{5,9},{1,13},{14,2},{10,6},... | collective-permute-start | bytes 344072 | tf_op jit(solution)/shard_map/ppermute | solution.py:283
  13.0 0.0 collective-permute-done.5.refs_4_
  13.0 0.2 collective-permute-start.10
  13.2 0.0 collective-permute-done.6.refs_6_
  13.2 0.0 collective-permute-done.4.refs_2_
  13.2 0.0 copy-done.4
  13.2 0.0 copy-done.5
  13.2 1.8 %shard_map.121 = (bf16[112,768]{1,0:T(8,128)(2,1)S(1)}, bf16[2,128,768]{2,1,0:T(8,128)(2,1)S(1)}) custom-call(bf16[224,768]{1,0:T(8,128)(2,1)S(1)} %get-tuple-element.21.refs_0_, bf16[3,768,128]{2,1,0:T(8,128)(2,1)S(1)} %copy-done.3, bf16[3,768,128]{2,1,0:T(8,128)(2,1)S(1)} %collective-permute-done.4.refs_2_, bf16[128,768]{1,0:T(8,128)(2,1)S(1)} %copy-done.4, ...), custom_call_target="tpu_custom_call" | custom-call | flops 100000000 | tf_op jit(solution)/shard_map/pallas_call | solution.py:241
  15.1 1.9 %collective-permute-start.7 = (bf16[112,768]{1,0:T(8,128)(2,1)S(1)}, bf16[112,768]{1,0:T(8,128)(2,1)S(1)}, u32[]{:S(2)}, u32[]{:S(2)}) collective-permute-start(bf16[112,768]{1,0:T(8,128)(2,1)S(1)} %get-tuple-element.22.refs_4_), channel_id=1, source_target_pairs={{0,2},{1,3},{2,0},{3,1},{4,6},{5,7},{6,4},{7,5},{8,10},{9,11},{10,... | collective-permute-start | bytes 516104 | tf_op jit(solution)/shard_map/ppermute | solution.py:231
  17.0 3.6 %collective-permute-done.8.refs_1_ = bf16[224,256]{1,0:T(8,128)(2,1)S(1)} collective-permute-done((bf16[224,256]{1,0:T(8,128)(2,1)S(1)}, bf16[224,256]{1,0:T(8,128)(2,1)S(1)}, u32[]{:S(2)}, u32[]{:S(2)}) %collective-permute-start.8) | collective-permute-done | bytes 114720 | tf_op jit(solution)/shard_map/ppermute | solution.py:283
  20.6 0.0 collective-permute-start.11
  20.6 0.0 collective-permute-done.9.refs_2_
  20.6 0.5 %collective-permute-start.12 = (bf16[224,256]{1,0:T(8,128)(2,1)S(1)}, bf16[224,256]{1,0:T(8,128)(2,1)S(1)}, u32[]{:S(2)}, u32[]{:S(2)}) collective-permute-start(bf16[224,256]{1,0:T(8,128)(2,1)S(1)} %collective-permute-done.9.refs_2_), channel_id=1, source_target_pairs={{0,1},{1,0},{2,3},{3,2},{4,5},{5,4},{6,7},{7,6},{8,9},{9,8},{10,11... | collective-permute-start | bytes 344072 | tf_op jit(solution)/shard_map/ppermute | solution.py:228
  21.1 0.4 %collective-permute-done.10.refs_3_ = bf16[224,256]{1,0:T(8,128)(2,1)S(1)} collective-permute-done((bf16[224,256]{1,0:T(8,128)(2,1)S(1)}, bf16[224,256]{1,0:T(8,128)(2,1)S(1)}, u32[]{:S(2)}, u32[]{:S(2)}) %collective-permute-start.10) | collective-permute-done | bytes 114720 | tf_op jit(solution)/shard_map/ppermute | solution.py:283
  21.5 0.0 collective-permute-start.13
  21.5 0.0 collective-permute-done.7.refs_5_
  21.5 0.0 copy-done.1
  21.5 0.9 %shard_map.122 = (f32[112,768]{1,0:T(8,128)S(1)}, bf16[112,256]{1,0:T(8,128)(2,1)S(1)}, bf16[2,768,768]{2,1,0:T(8,128)(2,1)S(1)}) custom-call(f32[112,768]{1,0:T(8,128)S(1)} %get-tuple-element.20.refs_0_, f32[768]{0:T(1024)S(1)} %copy-done.9, bf16[3,768,128]{2,1,0:T(8,128)(2,1)S(1)} %copy-done, ...), custom_call_target="tpu_custom_call" | custom-call | flops 100000000 | tf_op jit(solution)/shard_map/pallas_call | solution.py:241
  22.5 0.0 copy-start.10
  22.5 0.0 copy-start.11
  22.5 0.0 collective-permute-done.11.refs_4_
  22.5 0.0 collective-permute-done.12.refs_5_
  22.5 0.3 collective-permute-done.13.refs_6_
  22.8 1.1 %shard_map.123 = (bf16[2,768,768]{2,1,0:T(8,128)(2,1)S(1)}, bf16[2,128,768]{2,1,0:T(8,128)(2,1)S(1)}, bf16[2,112,256]{2,1,0:T(8,128)(2,1)S(1)}) custom-call(bf16[112,256]{1,0:T(8,128)(2,1)S(1)} %get-tuple-element.23.refs_0_, bf16[224,256]{1,0:T(8,128)(2,1)S(1)} %collective-permute-done.8.refs_1_, ...), custom_call_target="tpu_custom_call", output_to_operand_aliasing={{0}: (7, {}), {1}: (8, {})} | custom-call | flops 100000000 | tf_op jit(solution)/shard_map/pallas_call | solution.py:241
  23.9 0.3 collective-permute-start.17
  24.2 0.3 collective-permute-start.16
  24.5 1.9 %collective-permute-start.14 = (bf16[2,112,256]{2,1,0:T(8,128)(2,1)S(1)}, bf16[2,112,256]{2,1,0:T(8,128)(2,1)S(1)}, u32[]{:S(2)}, u32[]{:S(2)}) collective-permute-start(bf16[2,112,256]{2,1,0:T(8,128)(2,1)S(1)} %get-tuple-element.27.refs_1_), channel_id=1, source_target_pairs={{0,2},{1,3},{2,0},{3,1},{4,6},{5,7},{6,4},{7,5},{8,10},{9,11},{10,... | collective-permute-start | bytes 344072 | tf_op jit(solution)/shard_map/ppermute | solution.py:231
  26.4 0.7 %shard_map.124.refs_3_ = bf16[1,112,256]{2,1,0:T(8,128)(2,1)S(1)} custom-call(bf16[112,256]{1,0:T(8,128)(2,1)S(1)} %get-tuple-element.23.refs_0_, bf16[224,256]{1,0:T(8,128)(2,1)S(1)} %collective-permute-done.8.refs_1_, bf16[224,256]{1,0:T(8,128)(2,1)S(1)} %collective-permute-done.9.refs_2_, bf16[224,256]{1,0:T(8,128)(2,1)S(1)} %collective-permute-done.10.refs_3_, ...), custom_call_target="tpu_custom_call" | custom-call | flops 100000000 | tf_op jit(solution)/shard_map/pallas_call | solution.py:241
  27.1 0.2 collective-permute-start.15
  27.3 4.1 %collective-permute-done.15.refs_4_ = bf16[1,112,256]{2,1,0:T(8,128)(2,1)S(1)} collective-permute-done((bf16[1,112,256]{2,1,0:T(8,128)(2,1)S(1)}, bf16[1,112,256]{2,1,0:T(8,128)(2,1)S(1)}, u32[]{:S(2)}, u32[]{:S(2)}) %collective-permute-start.15) | collective-permute-done | bytes 57376 | tf_op jit(solution)/shard_map/ppermute | solution.py:231
  31.3 0.0 collective-permute-done.14.refs_2_
  31.3 0.0 collective-permute-done.16.refs_6_
  31.3 0.0 collective-permute-done.17.refs_10_
  31.4 3.0 %shard_map.125 = (f32[192,112]{1,0:T(8,128)S(1)}, f32[192,112]{1,0:T(8,128)S(1)}, bf16[192,112]{1,0:T(8,128)(2,1)S(1)}, bf16[192,112]{1,0:T(8,128)(2,1)S(1)}) custom-call(s32[2,4]{1,0:T(2,128)S(1)} %bitcast.10, bf16[2,112,256]{2,1,0:T(8,128)(2,1)S(1)} %get-tuple-element.27.refs_1_, bf16[2,112,256]{2,1,0:T(8,128)(2,1)S(1)} %collective-permute-done.14.refs_2_, ...), custom_call_target="tpu_custom_call" | custom-call | flops 3000000000 | tf_op jit(solution)/shard_map/pallas_call | solution.py:241
  34.4 0.1 collective-permute-start.18
  34.5 1.6 %collective-permute-start.19 = (bf16[192,112]{1,0:T(8,128)(2,1)S(1)}, bf16[192,112]{1,0:T(8,128)(2,1)S(1)}, u32[]{:S(2)}, u32[]{:S(2)}) collective-permute-start(bf16[192,112]{1,0:T(8,128)(2,1)S(1)} %get-tuple-element.33), channel_id=1, source_target_pairs={{0,2},{1,3},{2,0},{3,1},{4,6},{5,7},{6,4},{7,5},{8,10},{9,11},{10,... | collective-permute-start | bytes 129032 | tf_op jit(solution)/shard_map/ppermute | solution.py:231
  36.1 0.2 collective-permute-start.20
  36.3 2.3 %collective-permute-done.19.refs_2_ = bf16[192,112]{1,0:T(8,128)(2,1)S(1)} collective-permute-done((bf16[192,112]{1,0:T(8,128)(2,1)S(1)}, bf16[192,112]{1,0:T(8,128)(2,1)S(1)}, u32[]{:S(2)}, u32[]{:S(2)}) %collective-permute-start.19) | collective-permute-done | bytes 43040 | tf_op jit(solution)/shard_map/ppermute | solution.py:231
  38.6 1.2 %collective-permute-done.20.refs_3_ = bf16[192,112]{1,0:T(8,128)(2,1)S(1)} collective-permute-done((bf16[192,112]{1,0:T(8,128)(2,1)S(1)}, bf16[192,112]{1,0:T(8,128)(2,1)S(1)}, u32[]{:S(2)}, u32[]{:S(2)}) %collective-permute-start.20) | collective-permute-done | bytes 43040 | tf_op jit(solution)/shard_map/ppermute | solution.py:231
  39.8 0.0 collective-permute-done.18.refs_1_
  39.8 0.8 %shard_map.126 = f32[192,224]{1,0:T(8,128)} custom-call(f32[192,112]{1,0:T(8,128)S(1)} %get-tuple-element.31.refs_0_, f32[192,112]{1,0:T(8,128)S(1)} %collective-permute-done.18.refs_1_, bf16[192,112]{1,0:T(8,128)(2,1)S(1)} %collective-permute-done.19.refs_2_, bf16[192,112]{1,0:T(8,128)(2,1)S(1)} %collective-permute-done.20.refs_3_), custom_call_target="tpu_custom_call" | custom-call | tf_op jit(solution)/shard_map/pallas_call | solution.py:241
  (11 shorter events, 0.0 us)
Async XLA Ops:
  0.0 3.7 %collective-permute-start = (bf16[192,224]{1,0:T(8,128)(2,1)}, bf16[192,224]{1,0:T(8,128)(2,1)S(1)}, u32[]{:S(2)}, u32[]{:S(2)}) collective-permute-start(bf16[192,224]{1,0:T(8,128)(2,1)} %bitcast.7), channel_id=1, source_target_pairs={{0,1},{1,0},{2,3},{3,2},{4,5},{5,4},{6,7},{7,6},{8,9},{9,8},{10,11... | collective-permute-start | bytes 258056 | tf_op jit(solution)/shard_map/ppermute | solution.py:228
  0.5 6.2 %collective-permute-start.1 = (bf16[192,224]{1,0:T(8,128)(2,1)}, bf16[192,224]{1,0:T(8,128)(2,1)S(1)}, u32[]{:S(2)}, u32[]{:S(2)}) collective-permute-start(bf16[192,224]{1,0:T(8,128)(2,1)} %bitcast.8), channel_id=1, source_target_pairs={{0,2},{1,3},{2,0},{3,1},{4,6},{5,7},{6,4},{7,5},{8,10},{9,11},{10,... | collective-permute-start | bytes 258056 | tf_op jit(solution)/shard_map/ppermute | solution.py:231
  2.9 5.0 %collective-permute-start.3 = (bf16[3,768,128]{2,1,0:T(8,128)(2,1)}, bf16[3,768,128]{2,1,0:T(8,128)(2,1)S(1)}, u32[]{:S(2)}, u32[]{:S(2)}) collective-permute-start(bf16[3,768,128]{2,1,0:T(8,128)(2,1)} %refs_2_.1), channel_id=1, source_target_pairs={{0,1},{1,0},{2,3},{3,2},{4,5},{5,4},{6,7},{7,6},{8,9},{9,8},{10,11... | collective-permute-start | bytes 1769480 | tf_op jit(solution)/shard_map/ppermute | solution.py:228
  3.2 10.0 %collective-permute-start.4 = (bf16[3,768,128]{2,1,0:T(8,128)(2,1)}, bf16[3,768,128]{2,1,0:T(8,128)(2,1)S(1)}, u32[]{:S(2)}, u32[]{:S(2)}) collective-permute-start(bf16[3,768,128]{2,1,0:T(8,128)(2,1)} %refs_1_.2), channel_id=1, source_target_pairs={{0,1},{1,0},{2,3},{3,2},{4,5},{5,4},{6,7},{7,6},{8,9},{9,8},{10,11... | collective-permute-start | bytes 1769480 | tf_op jit(solution)/shard_map/ppermute | solution.py:228
  3.5 9.5 %collective-permute-start.5 = (bf16[128,768]{1,0:T(8,128)(2,1)}, bf16[128,768]{1,0:T(8,128)(2,1)S(1)}, u32[]{:S(2)}, u32[]{:S(2)}) collective-permute-start(bf16[128,768]{1,0:T(8,128)(2,1)} %refs_3_.1), channel_id=1, source_target_pairs={{0,1},{1,0},{2,3},{3,2},{4,5},{5,4},{6,7},{7,6},{8,9},{9,8},{10,11... | collective-permute-start | bytes 589832 | tf_op jit(solution)/shard_map/ppermute | solution.py:228
  3.7 9.5 %collective-permute-start.6 = (bf16[128,768]{1,0:T(8,128)(2,1)}, bf16[128,768]{1,0:T(8,128)(2,1)S(1)}, u32[]{:S(2)}, u32[]{:S(2)}) collective-permute-start(bf16[128,768]{1,0:T(8,128)(2,1)} %refs_5_.3), channel_id=1, source_target_pairs={{0,2},{1,3},{2,0},{3,1},{4,6},{5,7},{6,4},{7,5},{8,10},{9,11},{10,... | collective-permute-start | bytes 589832 | tf_op jit(solution)/shard_map/ppermute | solution.py:231
  6.6 1.3 %collective-permute-start.2 = (bf16[192,224]{1,0:T(8,128)(2,1)S(1)}, bf16[192,224]{1,0:T(8,128)(2,1)S(1)}, u32[]{:S(2)}, u32[]{:S(2)}) collective-permute-start(bf16[192,224]{1,0:T(8,128)(2,1)S(1)} %collective-permute-done.1.refs_2_), channel_id=1, source_target_pairs={{0,1},{1,0},{2,3},{3,2},{4,5},{5,4},{6,7},{7,6},{8,9},{9,8},{10,11... | collective-permute-start | bytes 258056 | tf_op jit(solution)/shard_map/ppermute | solution.py:228
  6.6 1.3 %copy-start = (bf16[3,768,128]{2,1,0:T(8,128)(2,1)S(1)}, bf16[3,768,128]{2,1,0:T(8,128)(2,1)}, u32[]{:S(2)}) copy-start(bf16[3,768,128]{2,1,0:T(8,128)(2,1)} %refs_2_.1) | copy-start | bytes 1769476
  6.6 1.3 %copy-start.6 = (bf16[1,224,192]{1,2,0:T(8,128)(2,1)S(1)}, bf16[1,224,192]{1,2,0:T(8,128)(2,1)}, u32[]{:S(2)}) copy-start(bf16[1,224,192]{1,2,0:T(8,128)(2,1)} %param.12) | copy-start | bytes 258052
  6.6 1.3 %copy-start.7 = (f32[768]{0:T(1024)S(1)}, f32[768]{0:T(1024)}, u32[]{:S(2)}) copy-start(f32[768]{0:T(1024)} %refs_4_.1) | copy-start | bytes 9220
  6.7 1.3 %copy-start.8 = (f32[768]{0:T(1024)S(1)}, f32[768]{0:T(1024)}, u32[]{:S(2)}) copy-start(f32[768]{0:T(1024)} %refs_5_.2) | copy-start | bytes 9220
  6.7 6.6 %copy-start.3 = (bf16[3,768,128]{2,1,0:T(8,128)(2,1)S(1)}, bf16[3,768,128]{2,1,0:T(8,128)(2,1)}, u32[]{:S(2)}) copy-start(bf16[3,768,128]{2,1,0:T(8,128)(2,1)} %refs_1_.2) | copy-start | bytes 1769476
  6.7 6.6 %copy-start.4 = (bf16[128,768]{1,0:T(8,128)(2,1)S(1)}, bf16[128,768]{1,0:T(8,128)(2,1)}, u32[]{:S(2)}) copy-start(bf16[128,768]{1,0:T(8,128)(2,1)} %refs_3_.1) | copy-start | bytes 589828
  6.7 6.5 %copy-start.5 = (bf16[128,768]{1,0:T(8,128)(2,1)S(1)}, bf16[128,768]{1,0:T(8,128)(2,1)}, u32[]{:S(2)}) copy-start(bf16[128,768]{1,0:T(8,128)(2,1)} %refs_5_.3) | copy-start | bytes 589828
  6.7 14.8 %copy-start.1 = (bf16[768,768]{1,0:T(8,128)(2,1)S(1)}, bf16[768,768]{1,0:T(8,128)(2,1)}, u32[]{:S(2)}) copy-start(bf16[768,768]{1,0:T(8,128)(2,1)} %refs_6_.3) | copy-start | bytes 3538948
  6.7 14.8 %copy-start.2 = (bf16[768,768]{1,0:T(8,128)(2,1)S(1)}, bf16[768,768]{1,0:T(8,128)(2,1)}, u32[]{:S(2)}) copy-start(bf16[768,768]{1,0:T(8,128)(2,1)} %refs_7_.1) | copy-start | bytes 3538948
  6.7 14.8 %copy-start.9 = (f32[768]{0:T(1024)S(1)}, f32[768]{0:T(1024)}, u32[]{:S(2)}) copy-start(f32[768]{0:T(1024)} %refs_1_.3) | copy-start | bytes 9220
  8.7 11.9 %collective-permute-start.8 = (bf16[224,256]{1,0:T(8,128)(2,1)S(1)}, bf16[224,256]{1,0:T(8,128)(2,1)S(1)}, u32[]{:S(2)}, u32[]{:S(2)}) collective-permute-start(bf16[224,256]{1,0:T(8,128)(2,1)S(1)} %get-tuple-element.24), channel_id=1, source_target_pairs={{8,0},{12,4},{0,8},{4,12},{9,1},{13,5},{1,9},{5,13},{10,2},{14,6},... | collective-permute-start | bytes 344072 | tf_op jit(solution)/shard_map/ppermute | solution.py:283
  11.6 8.9 %collective-permute-start.9 = (bf16[224,256]{1,0:T(8,128)(2,1)S(1)}, bf16[224,256]{1,0:T(8,128)(2,1)S(1)}, u32[]{:S(2)}, u32[]{:S(2)}) collective-permute-start(bf16[224,256]{1,0:T(8,128)(2,1)S(1)} %get-tuple-element.24), channel_id=1, source_target_pairs={{12,0},{8,4},{4,8},{0,12},{13,1},{9,5},{5,9},{1,13},{14,2},{10,6},... | collective-permute-start | bytes 344072 | tf_op jit(solution)/shard_map/ppermute | solution.py:283
  13.0 8.5 %collective-permute-start.10 = (bf16[224,256]{1,0:T(8,128)(2,1)S(1)}, bf16[224,256]{1,0:T(8,128)(2,1)S(1)}, u32[]{:S(2)}, u32[]{:S(2)}) collective-permute-start(bf16[224,256]{1,0:T(8,128)(2,1)S(1)} %get-tuple-element.24), channel_id=1, source_target_pairs={{4,0},{0,4},{12,8},{8,12},{5,1},{1,5},{13,9},{9,13},{6,2},{2,6},{1... | collective-permute-start | bytes 344072 | tf_op jit(solution)/shard_map/ppermute | solution.py:283
  15.1 6.4 %collective-permute-start.7 = (bf16[112,768]{1,0:T(8,128)(2,1)S(1)}, bf16[112,768]{1,0:T(8,128)(2,1)S(1)}, u32[]{:S(2)}, u32[]{:S(2)}) collective-permute-start(bf16[112,768]{1,0:T(8,128)(2,1)S(1)} %get-tuple-element.22.refs_4_), channel_id=1, source_target_pairs={{0,2},{1,3},{2,0},{3,1},{4,6},{5,7},{6,4},{7,5},{8,10},{9,11},{10,... | collective-permute-start | bytes 516104 | tf_op jit(solution)/shard_map/ppermute | solution.py:231
  20.6 1.9 %collective-permute-start.11 = (bf16[224,256]{1,0:T(8,128)(2,1)S(1)}, bf16[224,256]{1,0:T(8,128)(2,1)S(1)}, u32[]{:S(2)}, u32[]{:S(2)}) collective-permute-start(bf16[224,256]{1,0:T(8,128)(2,1)S(1)} %collective-permute-done.8.refs_1_), channel_id=1, source_target_pairs={{0,1},{1,0},{2,3},{3,2},{4,5},{5,4},{6,7},{7,6},{8,9},{9,8},{10,11... | collective-permute-start | bytes 344072 | tf_op jit(solution)/shard_map/ppermute | solution.py:228
  20.6 1.9 %collective-permute-start.12 = (bf16[224,256]{1,0:T(8,128)(2,1)S(1)}, bf16[224,256]{1,0:T(8,128)(2,1)S(1)}, u32[]{:S(2)}, u32[]{:S(2)}) collective-permute-start(bf16[224,256]{1,0:T(8,128)(2,1)S(1)} %collective-permute-done.9.refs_2_), channel_id=1, source_target_pairs={{0,1},{1,0},{2,3},{3,2},{4,5},{5,4},{6,7},{7,6},{8,9},{9,8},{10,11... | collective-permute-start | bytes 344072 | tf_op jit(solution)/shard_map/ppermute | solution.py:228
  21.5 1.3 %collective-permute-start.13 = (bf16[224,256]{1,0:T(8,128)(2,1)S(1)}, bf16[224,256]{1,0:T(8,128)(2,1)S(1)}, u32[]{:S(2)}, u32[]{:S(2)}) collective-permute-start(bf16[224,256]{1,0:T(8,128)(2,1)S(1)} %collective-permute-done.10.refs_3_), channel_id=1, source_target_pairs={{0,1},{1,0},{2,3},{3,2},{4,5},{5,4},{6,7},{7,6},{8,9},{9,8},{10,11... | collective-permute-start | bytes 344072 | tf_op jit(solution)/shard_map/ppermute | solution.py:228
  22.5 8.9 %copy-start.10 = (f32[768]{0:T(1024)S(1)}, f32[768]{0:T(1024)}, u32[]{:S(2)}) copy-start(f32[768]{0:T(1024)} %refs_8_.1) | copy-start | bytes 9220
  22.5 8.9 %copy-start.11 = (s32[4,2]{0,1:T(2,128)S(1)}, s32[4,2]{0,1:T(2,128)}, u32[]{:S(2)}) copy-start(s32[4,2]{0,1:T(2,128)} %param.13) | copy-start | bytes 100
  23.9 7.4 %collective-permute-start.17 = (bf16[2,768,768]{2,1,0:T(8,128)(2,1)S(1)}, bf16[2,768,768]{2,1,0:T(8,128)(2,1)S(1)}, u32[]{:S(2)}, u32[]{:S(2)}) collective-permute-start(bf16[2,768,768]{2,1,0:T(8,128)(2,1)S(1)} %get-tuple-element.30.refs_9_), channel_id=1, source_target_pairs={{0,1},{1,0},{2,3},{3,2},{4,5},{5,4},{6,7},{7,6},{8,9},{9,8},{10,11... | collective-permute-start | bytes 7077896 | tf_op jit(solution)/shard_map/ppermute | solution.py:228
  24.2 7.1 %collective-permute-start.16 = (bf16[2,128,768]{2,1,0:T(8,128)(2,1)S(1)}, bf16[2,128,768]{2,1,0:T(8,128)(2,1)S(1)}, u32[]{:S(2)}, u32[]{:S(2)}) collective-permute-start(bf16[2,128,768]{2,1,0:T(8,128)(2,1)S(1)} %get-tuple-element.28.refs_5_), channel_id=1, source_target_pairs={{0,1},{1,0},{2,3},{3,2},{4,5},{5,4},{6,7},{7,6},{8,9},{9,8},{10,11... | collective-permute-start | bytes 1179656 | tf_op jit(solution)/shard_map/ppermute | solution.py:228
  24.5 6.8 %collective-permute-start.14 = (bf16[2,112,256]{2,1,0:T(8,128)(2,1)S(1)}, bf16[2,112,256]{2,1,0:T(8,128)(2,1)S(1)}, u32[]{:S(2)}, u32[]{:S(2)}) collective-permute-start(bf16[2,112,256]{2,1,0:T(8,128)(2,1)S(1)} %get-tuple-element.27.refs_1_), channel_id=1, source_target_pairs={{0,2},{1,3},{2,0},{3,1},{4,6},{5,7},{6,4},{7,5},{8,10},{9,11},{10,... | collective-permute-start | bytes 344072 | tf_op jit(solution)/shard_map/ppermute | solution.py:231
  27.1 4.2 %collective-permute-start.15 = (bf16[1,112,256]{2,1,0:T(8,128)(2,1)S(1)}, bf16[1,112,256]{2,1,0:T(8,128)(2,1)S(1)}, u32[]{:S(2)}, u32[]{:S(2)}) collective-permute-start(bf16[1,112,256]{2,1,0:T(8,128)(2,1)S(1)} %shard_map.124.refs_3_), channel_id=1, source_target_pairs={{0,2},{1,3},{2,0},{3,1},{4,6},{5,7},{6,4},{7,5},{8,10},{9,11},{10,... | collective-permute-start | bytes 172040 | tf_op jit(solution)/shard_map/ppermute | solution.py:231
  34.4 5.4 %collective-permute-start.18 = (f32[192,112]{1,0:T(8,128)S(1)}, f32[192,112]{1,0:T(8,128)S(1)}, u32[]{:S(2)}, u32[]{:S(2)}) collective-permute-start(f32[192,112]{1,0:T(8,128)S(1)} %get-tuple-element.32), channel_id=1, source_target_pairs={{0,1},{1,0},{2,3},{3,2},{4,5},{5,4},{6,7},{7,6},{8,9},{9,8},{10,11... | collective-permute-start | bytes 258056 | tf_op jit(solution)/shard_map/ppermute | solution.py:228
  34.5 4.2 %collective-permute-start.19 = (bf16[192,112]{1,0:T(8,128)(2,1)S(1)}, bf16[192,112]{1,0:T(8,128)(2,1)S(1)}, u32[]{:S(2)}, u32[]{:S(2)}) collective-permute-start(bf16[192,112]{1,0:T(8,128)(2,1)S(1)} %get-tuple-element.33), channel_id=1, source_target_pairs={{0,2},{1,3},{2,0},{3,1},{4,6},{5,7},{6,4},{7,5},{8,10},{9,11},{10,... | collective-permute-start | bytes 129032 | tf_op jit(solution)/shard_map/ppermute | solution.py:231
  36.1 3.7 %collective-permute-start.20 = (bf16[192,112]{1,0:T(8,128)(2,1)S(1)}, bf16[192,112]{1,0:T(8,128)(2,1)S(1)}, u32[]{:S(2)}, u32[]{:S(2)}) collective-permute-start(bf16[192,112]{1,0:T(8,128)(2,1)S(1)} %get-tuple-element.34), channel_id=1, source_target_pairs={{0,3},{1,2},{2,1},{3,0},{4,7},{5,6},{6,5},{7,4},{8,11},{9,10},{10,... | collective-permute-start | bytes 129032 | tf_op jit(solution)/shard_map/ppermute | solution.py:231

commit v6 on v5

--- a/solution.py
+++ b/solution.py
@@ -126,7 +126,7 @@
 
 
 def pair_steps(images):
-    return [*range(2, images), 1]
+    return [2, 1, *range(3, images)]
 
 
 def view_counts(images, pairs):

time: 41 us -> 40.7 us (level)
  no operation moved by 1% of the time
where the time goes in v6:
time: 40.7 us; the launch traced here: 40.4 us
  starting transfers between devices  16.2 us (40%)
  waiting for transfers between devices  14.8 us (36%)
  Pallas kernels  9.06 us (22%)
    ppermute x7, waiting for transfers between devices, turn(): lax.ppermute(value, 'head', [(i, (i // 2 + step) % groups * 2 + (i % 2 ^...  9.66 us
    ppermute x7, starting transfers between devices, turn(): lax.ppermute(value, 'head', [(i, (i // 2 + step) % groups * 2 + (i % 2 ^...  9.33 us
    pallas_call x9, Pallas kernels, call(): pl.pallas_call(kernel, out_shape=out_shape, in_specs=[SMEM] * smem + [VME...  9.06 us
    ppermute x3, starting transfers between devices, body(): lax.ppermute(kv, 'pair', [(other_image(i, step, images), i) for i in rang...  4.51 us
    ppermute x3, waiting for transfers between devices, body(): lax.ppermute(kv, 'pair', [(other_image(i, step, images), i) for i in rang...  3.6 us
    ppermute x11, starting transfers between devices, swap(): return lax.ppermute(value, 'head', [(i, i ^ 1) for i in range(head)])  2.35 us
    ppermute x11, waiting for transfers between devices, swap(): return lax.ppermute(value, 'head', [(i, i ^ 1) for i in range(head)])  1.5 us
  transfers between devices with their start and end apart: 21, of which 8 were waited for; matrix products, arithmetic and copies ran while one was open for 0% of the time, Pallas kernels for 10%

profile of v6, /device:TPU:0, one launch (start us, length us, event | category | flops | bytes accessed | tf_op | source)
XLA Modules:
  0.0 40.4 jit_solution(7873123866938903020)
XLA Ops:
  0.0 0.5 %collective-permute-start = (bf16[192,224]{1,0:T(8,128)(2,1)}, bf16[192,224]{1,0:T(8,128)(2,1)S(1)}, u32[]{:S(2)}, u32[]{:S(2)}) collective-permute-start(bf16[192,224]{1,0:T(8,128)(2,1)} %bitcast.7), channel_id=1, source_target_pairs={{0,1},{1,0},{2,3},{3,2},{4,5},{5,4},{6,7},{7,6},{8,9},{9,8},{10,11... | collective-permute-start | bytes 258056 | tf_op jit(solution)/shard_map/ppermute | solution.py:228
  0.5 2.5 %collective-permute-start.1 = (bf16[192,224]{1,0:T(8,128)(2,1)}, bf16[192,224]{1,0:T(8,128)(2,1)S(1)}, u32[]{:S(2)}, u32[]{:S(2)}) collective-permute-start(bf16[192,224]{1,0:T(8,128)(2,1)} %bitcast.8), channel_id=1, source_target_pairs={{0,2},{1,3},{2,0},{3,1},{4,6},{5,7},{6,4},{7,5},{8,10},{9,11},{10,... | collective-permute-start | bytes 258056 | tf_op jit(solution)/shard_map/ppermute | solution.py:231
  2.9 0.2 collective-permute-start.3
  3.2 0.3 collective-permute-start.4
  3.5 0.2 collective-permute-start.5
  3.7 0.0 collective-permute-done.block.refs_1_
  3.7 0.8 %collective-permute-start.6 = (bf16[128,768]{1,0:T(8,128)(2,1)}, bf16[128,768]{1,0:T(8,128)(2,1)S(1)}, u32[]{:S(2)}, u32[]{:S(2)}) collective-permute-start(bf16[128,768]{1,0:T(8,128)(2,1)} %refs_5_.3), channel_id=1, source_target_pairs={{0,2},{1,3},{2,0},{3,1},{4,6},{5,7},{6,4},{7,5},{8,10},{9,11},{10,... | collective-permute-start | bytes 589832 | tf_op jit(solution)/shard_map/ppermute | solution.py:231
  4.5 2.2 %collective-permute-done.1.refs_2_ = bf16[192,224]{1,0:T(8,128)(2,1)S(1)} collective-permute-done((bf16[192,224]{1,0:T(8,128)(2,1)}, bf16[192,224]{1,0:T(8,128)(2,1)S(1)}, u32[]{:S(2)}, u32[]{:S(2)}) %collective-permute-start.1) | collective-permute-done | bytes 86048 | tf_op jit(solution)/shard_map/ppermute | solution.py:231
  6.6 0.0 collective-permute-start.2
  6.6 0.0 copy-start.6
  6.6 0.0 copy-start.7
  6.7 0.0 copy-start.8
  6.7 0.0 copy-start.3
  6.7 0.0 copy-start.4
  6.7 0.0 copy-start.5
  6.7 0.0 copy-start.1
  6.7 0.0 copy-start.2
  6.7 0.0 copy-start.9
  6.7 1.2 %collective-permute-done.2.refs_3_ = bf16[192,224]{1,0:T(8,128)(2,1)S(1)} collective-permute-done((bf16[192,224]{1,0:T(8,128)(2,1)S(1)}, bf16[192,224]{1,0:T(8,128)(2,1)S(1)}, u32[]{:S(2)}, u32[]{:S(2)}) %collective-permute-start.2) | collective-permute-done | bytes 86048 | tf_op jit(solution)/shard_map/ppermute | solution.py:228
  7.9 0.0 collective-permute-done.3.refs_8_.refs_3_
  7.9 0.0 copy-done
  7.9 0.0 copy-done.6
  7.9 0.0 copy-done.7
  7.9 0.0 copy-done.8
  8.0 0.7 %shard_map.120 = (f32[112,768]{1,0:T(8,128)S(1)}, bf16[224,768]{1,0:T(8,128)(2,1)S(1)}, bf16[224,256]{1,0:T(8,128)(2,1)S(1)}) custom-call(bf16[192,224]{1,0:T(8,128)(2,1)S(1)} %bitcast.9, bf16[192,224]{1,0:T(8,128)(2,1)S(1)} %collective-permute-done.block.refs_1_, bf16[192,224]{1,0:T(8,128)(2,1)S(1)} %collective-permute-done.1.refs_2_, ...), custom_call_target="tpu_custom_call" | custom-call | flops 100000000 | tf_op jit(solution)/shard_map/pallas_call | solution.py:241
  8.7 2.9 %collective-permute-start.8 = (bf16[224,256]{1,0:T(8,128)(2,1)S(1)}, bf16[224,256]{1,0:T(8,128)(2,1)S(1)}, u32[]{:S(2)}, u32[]{:S(2)}) collective-permute-start(bf16[224,256]{1,0:T(8,128)(2,1)S(1)} %get-tuple-element.24), channel_id=1, source_target_pairs={{8,0},{12,4},{0,8},{4,12},{9,1},{13,5},{1,9},{5,13},{10,2},{14,6},... | collective-permute-start | bytes 344072 | tf_op jit(solution)/shard_map/ppermute | solution.py:283
  11.6 1.6 %collective-permute-start.9 = (bf16[224,256]{1,0:T(8,128)(2,1)S(1)}, bf16[224,256]{1,0:T(8,128)(2,1)S(1)}, u32[]{:S(2)}, u32[]{:S(2)}) collective-permute-start(bf16[224,256]{1,0:T(8,128)(2,1)S(1)} %get-tuple-element.24), channel_id=1, source_target_pairs={{4,0},{0,4},{12,8},{8,12},{5,1},{1,5},{13,9},{9,13},{6,2},{2,6},{1... | collective-permute-start | bytes 344072 | tf_op jit(solution)/shard_map/ppermute | solution.py:283
  13.2 0.0 collective-permute-done.5.refs_4_
  13.2 0.0 collective-permute-start.10
  13.2 0.0 collective-permute-done.6.refs_6_
  13.2 0.0 collective-permute-done.4.refs_2_
  13.3 1.8 %shard_map.121 = (bf16[112,768]{1,0:T(8,128)(2,1)S(1)}, bf16[2,128,768]{2,1,0:T(8,128)(2,1)S(1)}) custom-call(bf16[224,768]{1,0:T(8,128)(2,1)S(1)} %get-tuple-element.21.refs_0_, bf16[3,768,128]{2,1,0:T(8,128)(2,1)S(1)} %copy-done.3, bf16[3,768,128]{2,1,0:T(8,128)(2,1)S(1)} %collective-permute-done.4.refs_2_, bf16[128,768]{1,0:T(8,128)(2,1)S(1)} %copy-done.4, ...), custom_call_target="tpu_custom_call" | custom-call | flops 100000000 | tf_op jit(solution)/shard_map/pallas_call | solution.py:241
  15.1 2.1 %collective-permute-start.7 = (bf16[112,768]{1,0:T(8,128)(2,1)S(1)}, bf16[112,768]{1,0:T(8,128)(2,1)S(1)}, u32[]{:S(2)}, u32[]{:S(2)}) collective-permute-start(bf16[112,768]{1,0:T(8,128)(2,1)S(1)} %get-tuple-element.22.refs_4_), channel_id=1, source_target_pairs={{0,2},{1,3},{2,0},{3,1},{4,6},{5,7},{6,4},{7,5},{8,10},{9,11},{10,... | collective-permute-start | bytes 516104 | tf_op jit(solution)/shard_map/ppermute | solution.py:231
  17.2 0.9 %collective-permute-done.8.refs_1_ = bf16[224,256]{1,0:T(8,128)(2,1)S(1)} collective-permute-done((bf16[224,256]{1,0:T(8,128)(2,1)S(1)}, bf16[224,256]{1,0:T(8,128)(2,1)S(1)}, u32[]{:S(2)}, u32[]{:S(2)}) %collective-permute-start.8) | collective-permute-done | bytes 114720 | tf_op jit(solution)/shard_map/ppermute | solution.py:283
  18.1 0.0 collective-permute-start.11
  18.1 0.0 collective-permute-done.9.refs_2_
  18.1 0.5 %collective-permute-start.12 = (bf16[224,256]{1,0:T(8,128)(2,1)S(1)}, bf16[224,256]{1,0:T(8,128)(2,1)S(1)}, u32[]{:S(2)}, u32[]{:S(2)}) collective-permute-start(bf16[224,256]{1,0:T(8,128)(2,1)S(1)} %collective-permute-done.9.refs_2_), channel_id=1, source_target_pairs={{0,1},{1,0},{2,3},{3,2},{4,5},{5,4},{6,7},{7,6},{8,9},{9,8},{10,11... | collective-permute-start | bytes 344072 | tf_op jit(solution)/shard_map/ppermute | solution.py:228
  18.6 2.7 %collective-permute-done.10.refs_3_ = bf16[224,256]{1,0:T(8,128)(2,1)S(1)} collective-permute-done((bf16[224,256]{1,0:T(8,128)(2,1)S(1)}, bf16[224,256]{1,0:T(8,128)(2,1)S(1)}, u32[]{:S(2)}, u32[]{:S(2)}) %collective-permute-start.10) | collective-permute-done | bytes 114720 | tf_op jit(solution)/shard_map/ppermute | solution.py:283
  21.3 0.0 collective-permute-start.13
  21.3 0.0 collective-permute-done.7.refs_5_
  21.4 0.9 %shard_map.122 = (f32[112,768]{1,0:T(8,128)S(1)}, bf16[112,256]{1,0:T(8,128)(2,1)S(1)}, bf16[2,768,768]{2,1,0:T(8,128)(2,1)S(1)}) custom-call(f32[112,768]{1,0:T(8,128)S(1)} %get-tuple-element.20.refs_0_, f32[768]{0:T(1024)S(1)} %copy-done.9, bf16[3,768,128]{2,1,0:T(8,128)(2,1)S(1)} %copy-done, ...), custom_call_target="tpu_custom_call" | custom-call | flops 100000000 | tf_op jit(solution)/shard_map/pallas_call | solution.py:241
  22.3 0.0 copy-start.10
  22.3 0.0 copy-start.11
  22.3 0.0 collective-permute-done.11.refs_4_
  22.3 0.0 collective-permute-done.12.refs_5_
  22.3 0.3 collective-permute-done.13.refs_6_
  22.6 1.1 %shard_map.123 = (bf16[2,768,768]{2,1,0:T(8,128)(2,1)S(1)}, bf16[2,128,768]{2,1,0:T(8,128)(2,1)S(1)}, bf16[2,112,256]{2,1,0:T(8,128)(2,1)S(1)}) custom-call(bf16[112,256]{1,0:T(8,128)(2,1)S(1)} %get-tuple-element.23.refs_0_, bf16[224,256]{1,0:T(8,128)(2,1)S(1)} %collective-permute-done.8.refs_1_, ...), custom_call_target="tpu_custom_call", output_to_operand_aliasing={{0}: (7, {}), {1}: (8, {})} | custom-call | flops 100000000 | tf_op jit(solution)/shard_map/pallas_call | solution.py:241
  23.7 0.3 collective-permute-start.17
  24.0 0.3 collective-permute-start.16
  24.3 1.9 %collective-permute-start.14 = (bf16[2,112,256]{2,1,0:T(8,128)(2,1)S(1)}, bf16[2,112,256]{2,1,0:T(8,128)(2,1)S(1)}, u32[]{:S(2)}, u32[]{:S(2)}) collective-permute-start(bf16[2,112,256]{2,1,0:T(8,128)(2,1)S(1)} %get-tuple-element.27.refs_1_), channel_id=1, source_target_pairs={{0,2},{1,3},{2,0},{3,1},{4,6},{5,7},{6,4},{7,5},{8,10},{9,11},{10,... | collective-permute-start | bytes 344072 | tf_op jit(solution)/shard_map/ppermute | solution.py:231
  26.2 0.7 %shard_map.124.refs_3_ = bf16[1,112,256]{2,1,0:T(8,128)(2,1)S(1)} custom-call(bf16[112,256]{1,0:T(8,128)(2,1)S(1)} %get-tuple-element.23.refs_0_, bf16[224,256]{1,0:T(8,128)(2,1)S(1)} %collective-permute-done.8.refs_1_, bf16[224,256]{1,0:T(8,128)(2,1)S(1)} %collective-permute-done.9.refs_2_, bf16[224,256]{1,0:T(8,128)(2,1)S(1)} %collective-permute-done.10.refs_3_, ...), custom_call_target="tpu_custom_call" | custom-call | flops 100000000 | tf_op jit(solution)/shard_map/pallas_call | solution.py:241
  26.8 0.2 collective-permute-start.15
  27.1 4.0 %collective-permute-done.15.refs_4_ = bf16[1,112,256]{2,1,0:T(8,128)(2,1)S(1)} collective-permute-done((bf16[1,112,256]{2,1,0:T(8,128)(2,1)S(1)}, bf16[1,112,256]{2,1,0:T(8,128)(2,1)S(1)}, u32[]{:S(2)}, u32[]{:S(2)}) %collective-permute-start.15) | collective-permute-done | bytes 57376 | tf_op jit(solution)/shard_map/ppermute | solution.py:231
  31.1 0.0 collective-permute-done.14.refs_2_
  31.1 0.0 collective-permute-done.16.refs_6_
  31.1 0.0 collective-permute-done.17.refs_10_
  31.1 3.0 %shard_map.125 = (f32[192,112]{1,0:T(8,128)S(1)}, f32[192,112]{1,0:T(8,128)S(1)}, bf16[192,112]{1,0:T(8,128)(2,1)S(1)}, bf16[192,112]{1,0:T(8,128)(2,1)S(1)}) custom-call(s32[2,4]{1,0:T(2,128)S(1)} %bitcast.10, bf16[2,112,256]{2,1,0:T(8,128)(2,1)S(1)} %get-tuple-element.27.refs_1_, bf16[2,112,256]{2,1,0:T(8,128)(2,1)S(1)} %collective-permute-done.14.refs_2_, ...), custom_call_target="tpu_custom_call" | custom-call | flops 3000000000 | tf_op jit(solution)/shard_map/pallas_call | solution.py:241
  34.2 0.1 collective-permute-start.18
  34.2 1.6 %collective-permute-start.19 = (bf16[192,112]{1,0:T(8,128)(2,1)S(1)}, bf16[192,112]{1,0:T(8,128)(2,1)S(1)}, u32[]{:S(2)}, u32[]{:S(2)}) collective-permute-start(bf16[192,112]{1,0:T(8,128)(2,1)S(1)} %get-tuple-element.33), channel_id=1, source_target_pairs={{0,2},{1,3},{2,0},{3,1},{4,6},{5,7},{6,4},{7,5},{8,10},{9,11},{10,... | collective-permute-start | bytes 129032 | tf_op jit(solution)/shard_map/ppermute | solution.py:231
  35.9 0.2 collective-permute-start.20
  36.1 2.3 %collective-permute-done.19.refs_2_ = bf16[192,112]{1,0:T(8,128)(2,1)S(1)} collective-permute-done((bf16[192,112]{1,0:T(8,128)(2,1)S(1)}, bf16[192,112]{1,0:T(8,128)(2,1)S(1)}, u32[]{:S(2)}, u32[]{:S(2)}) %collective-permute-start.19) | collective-permute-done | bytes 43040 | tf_op jit(solution)/shard_map/ppermute | solution.py:231
  38.4 1.2 %collective-permute-done.20.refs_3_ = bf16[192,112]{1,0:T(8,128)(2,1)S(1)} collective-permute-done((bf16[192,112]{1,0:T(8,128)(2,1)S(1)}, bf16[192,112]{1,0:T(8,128)(2,1)S(1)}, u32[]{:S(2)}, u32[]{:S(2)}) %collective-permute-start.20) | collective-permute-done | bytes 43040 | tf_op jit(solution)/shard_map/ppermute | solution.py:231
  39.6 0.0 collective-permute-done.18.refs_1_
  39.6 0.8 %shard_map.126 = f32[192,224]{1,0:T(8,128)} custom-call(f32[192,112]{1,0:T(8,128)S(1)} %get-tuple-element.31.refs_0_, f32[192,112]{1,0:T(8,128)S(1)} %collective-permute-done.18.refs_1_, bf16[192,112]{1,0:T(8,128)(2,1)S(1)} %collective-permute-done.19.refs_2_, bf16[192,112]{1,0:T(8,128)(2,1)S(1)} %collective-permute-done.20.refs_3_), custom_call_target="tpu_custom_call" | custom-call | tf_op jit(solution)/shard_map/pallas_call | solution.py:241
  (11 shorter events, 0.0 us)
Async XLA Ops:
  0.0 3.7 %collective-permute-start = (bf16[192,224]{1,0:T(8,128)(2,1)}, bf16[192,224]{1,0:T(8,128)(2,1)S(1)}, u32[]{:S(2)}, u32[]{:S(2)}) collective-permute-start(bf16[192,224]{1,0:T(8,128)(2,1)} %bitcast.7), channel_id=1, source_target_pairs={{0,1},{1,0},{2,3},{3,2},{4,5},{5,4},{6,7},{7,6},{8,9},{9,8},{10,11... | collective-permute-start | bytes 258056 | tf_op jit(solution)/shard_map/ppermute | solution.py:228
  0.5 6.2 %collective-permute-start.1 = (bf16[192,224]{1,0:T(8,128)(2,1)}, bf16[192,224]{1,0:T(8,128)(2,1)S(1)}, u32[]{:S(2)}, u32[]{:S(2)}) collective-permute-start(bf16[192,224]{1,0:T(8,128)(2,1)} %bitcast.8), channel_id=1, source_target_pairs={{0,2},{1,3},{2,0},{3,1},{4,6},{5,7},{6,4},{7,5},{8,10},{9,11},{10,... | collective-permute-start | bytes 258056 | tf_op jit(solution)/shard_map/ppermute | solution.py:231
  2.9 5.0 %collective-permute-start.3 = (bf16[3,768,128]{2,1,0:T(8,128)(2,1)}, bf16[3,768,128]{2,1,0:T(8,128)(2,1)S(1)}, u32[]{:S(2)}, u32[]{:S(2)}) collective-permute-start(bf16[3,768,128]{2,1,0:T(8,128)(2,1)} %refs_2_.1), channel_id=1, source_target_pairs={{0,1},{1,0},{2,3},{3,2},{4,5},{5,4},{6,7},{7,6},{8,9},{9,8},{10,11... | collective-permute-start | bytes 1769480 | tf_op jit(solution)/shard_map/ppermute | solution.py:228
  3.2 10.1 %collective-permute-start.4 = (bf16[3,768,128]{2,1,0:T(8,128)(2,1)}, bf16[3,768,128]{2,1,0:T(8,128)(2,1)S(1)}, u32[]{:S(2)}, u32[]{:S(2)}) collective-permute-start(bf16[3,768,128]{2,1,0:T(8,128)(2,1)} %refs_1_.2), channel_id=1, source_target_pairs={{0,1},{1,0},{2,3},{3,2},{4,5},{5,4},{6,7},{7,6},{8,9},{9,8},{10,11... | collective-permute-start | bytes 1769480 | tf_op jit(solution)/shard_map/ppermute | solution.py:228
  3.5 9.8 %collective-permute-start.5 = (bf16[128,768]{1,0:T(8,128)(2,1)}, bf16[128,768]{1,0:T(8,128)(2,1)S(1)}, u32[]{:S(2)}, u32[]{:S(2)}) collective-permute-start(bf16[128,768]{1,0:T(8,128)(2,1)} %refs_3_.1), channel_id=1, source_target_pairs={{0,1},{1,0},{2,3},{3,2},{4,5},{5,4},{6,7},{7,6},{8,9},{9,8},{10,11... | collective-permute-start | bytes 589832 | tf_op jit(solution)/shard_map/ppermute | solution.py:228
  3.7 9.5 %collective-permute-start.6 = (bf16[128,768]{1,0:T(8,128)(2,1)}, bf16[128,768]{1,0:T(8,128)(2,1)S(1)}, u32[]{:S(2)}, u32[]{:S(2)}) collective-permute-start(bf16[128,768]{1,0:T(8,128)(2,1)} %refs_5_.3), channel_id=1, source_target_pairs={{0,2},{1,3},{2,0},{3,1},{4,6},{5,7},{6,4},{7,5},{8,10},{9,11},{10,... | collective-permute-start | bytes 589832 | tf_op jit(solution)/shard_map/ppermute | solution.py:231
  6.6 1.3 %collective-permute-start.2 = (bf16[192,224]{1,0:T(8,128)(2,1)S(1)}, bf16[192,224]{1,0:T(8,128)(2,1)S(1)}, u32[]{:S(2)}, u32[]{:S(2)}) collective-permute-start(bf16[192,224]{1,0:T(8,128)(2,1)S(1)} %collective-permute-done.1.refs_2_), channel_id=1, source_target_pairs={{0,1},{1,0},{2,3},{3,2},{4,5},{5,4},{6,7},{7,6},{8,9},{9,8},{10,11... | collective-permute-start | bytes 258056 | tf_op jit(solution)/shard_map/ppermute | solution.py:228
  6.6 1.3 %copy-start = (bf16[3,768,128]{2,1,0:T(8,128)(2,1)S(1)}, bf16[3,768,128]{2,1,0:T(8,128)(2,1)}, u32[]{:S(2)}) copy-start(bf16[3,768,128]{2,1,0:T(8,128)(2,1)} %refs_2_.1) | copy-start | bytes 1769476
  6.6 1.3 %copy-start.6 = (bf16[1,224,192]{1,2,0:T(8,128)(2,1)S(1)}, bf16[1,224,192]{1,2,0:T(8,128)(2,1)}, u32[]{:S(2)}) copy-start(bf16[1,224,192]{1,2,0:T(8,128)(2,1)} %param.12) | copy-start | bytes 258052
  6.6 1.3 %copy-start.7 = (f32[768]{0:T(1024)S(1)}, f32[768]{0:T(1024)}, u32[]{:S(2)}) copy-start(f32[768]{0:T(1024)} %refs_4_.1) | copy-start | bytes 9220
  6.7 1.3 %copy-start.8 = (f32[768]{0:T(1024)S(1)}, f32[768]{0:T(1024)}, u32[]{:S(2)}) copy-start(f32[768]{0:T(1024)} %refs_5_.2) | copy-start | bytes 9220
  6.7 6.6 %copy-start.3 = (bf16[3,768,128]{2,1,0:T(8,128)(2,1)S(1)}, bf16[3,768,128]{2,1,0:T(8,128)(2,1)}, u32[]{:S(2)}) copy-start(bf16[3,768,128]{2,1,0:T(8,128)(2,1)} %refs_1_.2) | copy-start | bytes 1769476
  6.7 6.6 %copy-start.4 = (bf16[128,768]{1,0:T(8,128)(2,1)S(1)}, bf16[128,768]{1,0:T(8,128)(2,1)}, u32[]{:S(2)}) copy-start(bf16[128,768]{1,0:T(8,128)(2,1)} %refs_3_.1) | copy-start | bytes 589828
  6.7 6.6 %copy-start.5 = (bf16[128,768]{1,0:T(8,128)(2,1)S(1)}, bf16[128,768]{1,0:T(8,128)(2,1)}, u32[]{:S(2)}) copy-start(bf16[128,768]{1,0:T(8,128)(2,1)} %refs_5_.3) | copy-start | bytes 589828
  6.7 14.6 %copy-start.1 = (bf16[768,768]{1,0:T(8,128)(2,1)S(1)}, bf16[768,768]{1,0:T(8,128)(2,1)}, u32[]{:S(2)}) copy-start(bf16[768,768]{1,0:T(8,128)(2,1)} %refs_6_.3) | copy-start | bytes 3538948
  6.7 14.6 %copy-start.2 = (bf16[768,768]{1,0:T(8,128)(2,1)S(1)}, bf16[768,768]{1,0:T(8,128)(2,1)}, u32[]{:S(2)}) copy-start(bf16[768,768]{1,0:T(8,128)(2,1)} %refs_7_.1) | copy-start | bytes 3538948
  6.7 14.6 %copy-start.9 = (f32[768]{0:T(1024)S(1)}, f32[768]{0:T(1024)}, u32[]{:S(2)}) copy-start(f32[768]{0:T(1024)} %refs_1_.3) | copy-start | bytes 9220
  8.7 9.4 %collective-permute-start.8 = (bf16[224,256]{1,0:T(8,128)(2,1)S(1)}, bf16[224,256]{1,0:T(8,128)(2,1)S(1)}, u32[]{:S(2)}, u32[]{:S(2)}) collective-permute-start(bf16[224,256]{1,0:T(8,128)(2,1)S(1)} %get-tuple-element.24), channel_id=1, source_target_pairs={{8,0},{12,4},{0,8},{4,12},{9,1},{13,5},{1,9},{5,13},{10,2},{14,6},... | collective-permute-start | bytes 344072 | tf_op jit(solution)/shard_map/ppermute | solution.py:283
  11.6 6.4 %collective-permute-start.9 = (bf16[224,256]{1,0:T(8,128)(2,1)S(1)}, bf16[224,256]{1,0:T(8,128)(2,1)S(1)}, u32[]{:S(2)}, u32[]{:S(2)}) collective-permute-start(bf16[224,256]{1,0:T(8,128)(2,1)S(1)} %get-tuple-element.24), channel_id=1, source_target_pairs={{4,0},{0,4},{12,8},{8,12},{5,1},{1,5},{13,9},{9,13},{6,2},{2,6},{1... | collective-permute-start | bytes 344072 | tf_op jit(solution)/shard_map/ppermute | solution.py:283
  13.2 8.1 %collective-permute-start.10 = (bf16[224,256]{1,0:T(8,128)(2,1)S(1)}, bf16[224,256]{1,0:T(8,128)(2,1)S(1)}, u32[]{:S(2)}, u32[]{:S(2)}) collective-permute-start(bf16[224,256]{1,0:T(8,128)(2,1)S(1)} %get-tuple-element.24), channel_id=1, source_target_pairs={{12,0},{8,4},{4,8},{0,12},{13,1},{9,5},{5,9},{1,13},{14,2},{10,6},... | collective-permute-start | bytes 344072 | tf_op jit(solution)/shard_map/ppermute | solution.py:283
  15.1 6.2 %collective-permute-start.7 = (bf16[112,768]{1,0:T(8,128)(2,1)S(1)}, bf16[112,768]{1,0:T(8,128)(2,1)S(1)}, u32[]{:S(2)}, u32[]{:S(2)}) collective-permute-start(bf16[112,768]{1,0:T(8,128)(2,1)S(1)} %get-tuple-element.22.refs_4_), channel_id=1, source_target_pairs={{0,2},{1,3},{2,0},{3,1},{4,6},{5,7},{6,4},{7,5},{8,10},{9,11},{10,... | collective-permute-start | bytes 516104 | tf_op jit(solution)/shard_map/ppermute | solution.py:231
  18.1 4.3 %collective-permute-start.11 = (bf16[224,256]{1,0:T(8,128)(2,1)S(1)}, bf16[224,256]{1,0:T(8,128)(2,1)S(1)}, u32[]{:S(2)}, u32[]{:S(2)}) collective-permute-start(bf16[224,256]{1,0:T(8,128)(2,1)S(1)} %collective-permute-done.8.refs_1_), channel_id=1, source_target_pairs={{0,1},{1,0},{2,3},{3,2},{4,5},{5,4},{6,7},{7,6},{8,9},{9,8},{10,11... | collective-permute-start | bytes 344072 | tf_op jit(solution)/shard_map/ppermute | solution.py:228
  18.1 4.3 %collective-permute-start.12 = (bf16[224,256]{1,0:T(8,128)(2,1)S(1)}, bf16[224,256]{1,0:T(8,128)(2,1)S(1)}, u32[]{:S(2)}, u32[]{:S(2)}) collective-permute-start(bf16[224,256]{1,0:T(8,128)(2,1)S(1)} %collective-permute-done.9.refs_2_), channel_id=1, source_target_pairs={{0,1},{1,0},{2,3},{3,2},{4,5},{5,4},{6,7},{7,6},{8,9},{9,8},{10,11... | collective-permute-start | bytes 344072 | tf_op jit(solution)/shard_map/ppermute | solution.py:228
  21.3 1.3 %collective-permute-start.13 = (bf16[224,256]{1,0:T(8,128)(2,1)S(1)}, bf16[224,256]{1,0:T(8,128)(2,1)S(1)}, u32[]{:S(2)}, u32[]{:S(2)}) collective-permute-start(bf16[224,256]{1,0:T(8,128)(2,1)S(1)} %collective-permute-done.10.refs_3_), channel_id=1, source_target_pairs={{0,1},{1,0},{2,3},{3,2},{4,5},{5,4},{6,7},{7,6},{8,9},{9,8},{10,11... | collective-permute-start | bytes 344072 | tf_op jit(solution)/shard_map/ppermute | solution.py:228
  22.3 8.8 %copy-start.10 = (f32[768]{0:T(1024)S(1)}, f32[768]{0:T(1024)}, u32[]{:S(2)}) copy-start(f32[768]{0:T(1024)} %refs_8_.1) | copy-start | bytes 9220
  22.3 8.8 %copy-start.11 = (s32[4,2]{0,1:T(2,128)S(1)}, s32[4,2]{0,1:T(2,128)}, u32[]{:S(2)}) copy-start(s32[4,2]{0,1:T(2,128)} %param.13) | copy-start | bytes 100
  23.7 7.3 %collective-permute-start.17 = (bf16[2,768,768]{2,1,0:T(8,128)(2,1)S(1)}, bf16[2,768,768]{2,1,0:T(8,128)(2,1)S(1)}, u32[]{:S(2)}, u32[]{:S(2)}) collective-permute-start(bf16[2,768,768]{2,1,0:T(8,128)(2,1)S(1)} %get-tuple-element.30.refs_9_), channel_id=1, source_target_pairs={{0,1},{1,0},{2,3},{3,2},{4,5},{5,4},{6,7},{7,6},{8,9},{9,8},{10,11... | collective-permute-start | bytes 7077896 | tf_op jit(solution)/shard_map/ppermute | solution.py:228
  24.0 7.1 %collective-permute-start.16 = (bf16[2,128,768]{2,1,0:T(8,128)(2,1)S(1)}, bf16[2,128,768]{2,1,0:T(8,128)(2,1)S(1)}, u32[]{:S(2)}, u32[]{:S(2)}) collective-permute-start(bf16[2,128,768]{2,1,0:T(8,128)(2,1)S(1)} %get-tuple-element.28.refs_5_), channel_id=1, source_target_pairs={{0,1},{1,0},{2,3},{3,2},{4,5},{5,4},{6,7},{7,6},{8,9},{9,8},{10,11... | collective-permute-start | bytes 1179656 | tf_op jit(solution)/shard_map/ppermute | solution.py:228
  24.3 6.8 %collective-permute-start.14 = (bf16[2,112,256]{2,1,0:T(8,128)(2,1)S(1)}, bf16[2,112,256]{2,1,0:T(8,128)(2,1)S(1)}, u32[]{:S(2)}, u32[]{:S(2)}) collective-permute-start(bf16[2,112,256]{2,1,0:T(8,128)(2,1)S(1)} %get-tuple-element.27.refs_1_), channel_id=1, source_target_pairs={{0,2},{1,3},{2,0},{3,1},{4,6},{5,7},{6,4},{7,5},{8,10},{9,11},{10,... | collective-permute-start | bytes 344072 | tf_op jit(solution)/shard_map/ppermute | solution.py:231
  26.8 4.2 %collective-permute-start.15 = (bf16[1,112,256]{2,1,0:T(8,128)(2,1)S(1)}, bf16[1,112,256]{2,1,0:T(8,128)(2,1)S(1)}, u32[]{:S(2)}, u32[]{:S(2)}) collective-permute-start(bf16[1,112,256]{2,1,0:T(8,128)(2,1)S(1)} %shard_map.124.refs_3_), channel_id=1, source_target_pairs={{0,2},{1,3},{2,0},{3,1},{4,6},{5,7},{6,4},{7,5},{8,10},{9,11},{10,... | collective-permute-start | bytes 172040 | tf_op jit(solution)/shard_map/ppermute | solution.py:231
  34.2 5.4 %collective-permute-start.18 = (f32[192,112]{1,0:T(8,128)S(1)}, f32[192,112]{1,0:T(8,128)S(1)}, u32[]{:S(2)}, u32[]{:S(2)}) collective-permute-start(f32[192,112]{1,0:T(8,128)S(1)} %get-tuple-element.32), channel_id=1, source_target_pairs={{0,1},{1,0},{2,3},{3,2},{4,5},{5,4},{6,7},{7,6},{8,9},{9,8},{10,11... | collective-permute-start | bytes 258056 | tf_op jit(solution)/shard_map/ppermute | solution.py:228
  34.2 4.2 %collective-permute-start.19 = (bf16[192,112]{1,0:T(8,128)(2,1)S(1)}, bf16[192,112]{1,0:T(8,128)(2,1)S(1)}, u32[]{:S(2)}, u32[]{:S(2)}) collective-permute-start(bf16[192,112]{1,0:T(8,128)(2,1)S(1)} %get-tuple-element.33), channel_id=1, source_target_pairs={{0,2},{1,3},{2,0},{3,1},{4,6},{5,7},{6,4},{7,5},{8,10},{9,11},{10,... | collective-permute-start | bytes 129032 | tf_op jit(solution)/shard_map/ppermute | solution.py:231
  35.9 3.7 %collective-permute-start.20 = (bf16[192,112]{1,0:T(8,128)(2,1)S(1)}, bf16[192,112]{1,0:T(8,128)(2,1)S(1)}, u32[]{:S(2)}, u32[]{:S(2)}) collective-permute-start(bf16[192,112]{1,0:T(8,128)(2,1)S(1)} %get-tuple-element.34), channel_id=1, source_target_pairs={{0,3},{1,2},{2,1},{3,0},{4,7},{5,6},{6,5},{7,4},{8,11},{9,10},{10,... | collective-permute-start | bytes 129032 | tf_op jit(solution)/shard_map/ppermute | solution.py:231

commit v7 on v6

--- a/solution.py
+++ b/solution.py
@@ -37,12 +37,12 @@
     scores = lax.dot_general(stacked, k, (((1,), (1,)), ((), ())), preferred_element_type=F32)
     top = jnp.max(scores, axis=-1, keepdims=True)
     weights = jnp.exp((scores - top) * SCALE)
-    total = jnp.sum(weights, axis=-1, keepdims=True)
-    weights = (weights * (1.0 / total)).astype(BF16)
-    mixed = mm(weights, v)
+    inverse = 1.0 / jnp.sum(weights, axis=-1, keepdims=True)
+    mixed = mm(weights.astype(BF16), v)
     context = jnp.zeros((rows, width), F32)
     for i in range(heads):
-        context = context + jnp.where(lane_head == i, mixed[i * rows : (i + 1) * rows], 0.0)
+        here = slice(i * rows, (i + 1) * rows)
+        context = jnp.where(lane_head == i, mixed[here] * inverse[here], context)
     return context
 
 
@@ -52,7 +52,7 @@
 
 
 def mark_kernel(block, out):
-    out[...] = block[:8, :128].astype(out.dtype)
+    out[...] = block[:16, :128].astype(out.dtype)
 
 
 def memory_kernel(groups, *refs):
@@ -126,7 +126,7 @@
 
 
 def pair_steps(images):
-    return [2, 1, *range(3, images)]
+    return sorted(range(1, images), key=lambda step: (step != 2, step))
 
 
 def view_counts(images, pairs):
@@ -153,16 +153,19 @@
     rows = after.shape[0]
     column = after.shape[1] // (2 * groups)
     residual = after[...]
-    held = jnp.concatenate(
-        [
-            jnp.concatenate([contexts[groups * batch + step][view] for step in range(groups)], axis=1)
-            for batch in range(len(batches))
-            for view in range(batches[batch])
-        ],
-        axis=0,
-    )
-    weight = jnp.concatenate([block[step] for step in range(groups) for block in (out_own, out_other)], axis=0)
-    total = jnp.concatenate([residual] * views, axis=0) + mm(held, weight)
+    att = out_own.shape[1]
+    total = jnp.concatenate([residual] * views, axis=0)
+    for other, weight in enumerate((out_own, out_other)):
+        lanes = slice(other * att, (other + 1) * att)
+        held = jnp.concatenate(
+            [
+                jnp.concatenate([contexts[groups * batch + step][view, :, lanes] for step in range(groups)], axis=1)
+                for batch in range(len(batches))
+                for view in range(batches[batch])
+            ],
+            axis=0,
+        )
+        total = total + mm(held, weight[...].reshape(groups * att, -1))
     if images:
         share = view_counts(images, listed)
     else:
@@ -258,8 +261,8 @@
     turned = [turn(w_cross_out, step) for step in range(1, groups)]
     self_other, self_out_other, cross_other = swap(w_self_qkv), swap(w_self_out), swap(w_cross_qkv)
 
-    (mark,) = call(mark_kernel, [shape((8, 128), F32)], [blocks[1]], flops=3 * 10**9)
-    (mark,) = call(mark_kernel, [shape((8, 128), F32)], [mark], flops=3 * 10**9)
+    (mark,) = call(mark_kernel, [shape((16, 128), F32)], [blocks[1]], flops=3 * 10**9)
+    (mark,) = call(mark_kernel, [shape((16, 128), F32)], [mark], flops=3 * 10**9)
     x_rows, normed_self, kv = call(
         lambda *refs: memory_kernel(groups, *refs),
         [shape((rows, model), F32), shape((tokens, model), BF16), shape((tokens, 2 * att), BF16)],

time: 40.7 us -> 40.4 us (level)
  Pallas kernels: 9.06 us -> 8.5 us
    pallas_call x9, Pallas kernels: 9.06 us -> 8.5 us  [call(): pl.pallas_call(kernel, out_shape=out_shape, in_specs=[SMEM] * smem + [VME...]
where the time goes in v7:
time: 40.4 us; the launch traced here: 40.1 us
  starting transfers between devices  16.2 us (40%)
  waiting for transfers between devices  15 us (37%)
  Pallas kernels  8.5 us (21%)
    ppermute x7, waiting for transfers between devices, turn(): lax.ppermute(value, 'head', [(i, (i // 2 + step) % groups * 2 + (i % 2 ^...  9.79 us
    ppermute x7, starting transfers between devices, turn(): lax.ppermute(value, 'head', [(i, (i // 2 + step) % groups * 2 + (i % 2 ^...  9.34 us
    pallas_call x9, Pallas kernels, call(): pl.pallas_call(kernel, out_shape=out_shape, in_specs=[SMEM] * smem + [VME...  8.5 us
    ppermute x3, starting transfers between devices, body(): lax.ppermute(kv, 'pair', [(other_image(i, step, images), i) for i in rang...  4.51 us
    ppermute x3, waiting for transfers between devices, body(): lax.ppermute(kv, 'pair', [(other_image(i, step, images), i) for i in rang...  3.75 us
    ppermute x11, starting transfers between devices, swap(): return lax.ppermute(value, 'head', [(i, i ^ 1) for i in range(head)])  2.35 us
    ppermute x11, waiting for transfers between devices, swap(): return lax.ppermute(value, 'head', [(i, i ^ 1) for i in range(head)])  1.5 us
  transfers between devices with their start and end apart: 21, of which 8 were waited for; matrix products, arithmetic and copies ran while one was open for 0% of the time, Pallas kernels for 10%

profile of v7, /device:TPU:0, one launch (start us, length us, event | category | flops | bytes accessed | tf_op | source)
XLA Modules:
  0.0 40.1 jit_solution(6655402195298011586)
XLA Ops:
  0.0 0.5 %collective-permute-start = (bf16[192,224]{1,0:T(8,128)(2,1)}, bf16[192,224]{1,0:T(8,128)(2,1)S(1)}, u32[]{:S(2)}, u32[]{:S(2)}) collective-permute-start(bf16[192,224]{1,0:T(8,128)(2,1)} %bitcast.7), channel_id=1, source_target_pairs={{0,1},{1,0},{2,3},{3,2},{4,5},{5,4},{6,7},{7,6},{8,9},{9,8},{10,11... | collective-permute-start | bytes 258056 | tf_op jit(solution)/shard_map/ppermute | solution.py:231
  0.5 2.5 %collective-permute-start.1 = (bf16[192,224]{1,0:T(8,128)(2,1)}, bf16[192,224]{1,0:T(8,128)(2,1)S(1)}, u32[]{:S(2)}, u32[]{:S(2)}) collective-permute-start(bf16[192,224]{1,0:T(8,128)(2,1)} %bitcast.8), channel_id=1, source_target_pairs={{0,2},{1,3},{2,0},{3,1},{4,6},{5,7},{6,4},{7,5},{8,10},{9,11},{10,... | collective-permute-start | bytes 258056 | tf_op jit(solution)/shard_map/ppermute | solution.py:234
  2.9 0.2 collective-permute-start.3
  3.2 0.3 collective-permute-start.4
  3.5 0.2 collective-permute-start.5
  3.7 0.0 collective-permute-done.block.refs_1_
  3.7 0.8 %collective-permute-start.6 = (bf16[128,768]{1,0:T(8,128)(2,1)}, bf16[128,768]{1,0:T(8,128)(2,1)S(1)}, u32[]{:S(2)}, u32[]{:S(2)}) collective-permute-start(bf16[128,768]{1,0:T(8,128)(2,1)} %refs_5_.3), channel_id=1, source_target_pairs={{0,2},{1,3},{2,0},{3,1},{4,6},{5,7},{6,4},{7,5},{8,10},{9,11},{10,... | collective-permute-start | bytes 589832 | tf_op jit(solution)/shard_map/ppermute | solution.py:234
  4.5 2.2 %collective-permute-done.1.refs_2_ = bf16[192,224]{1,0:T(8,128)(2,1)S(1)} collective-permute-done((bf16[192,224]{1,0:T(8,128)(2,1)}, bf16[192,224]{1,0:T(8,128)(2,1)S(1)}, u32[]{:S(2)}, u32[]{:S(2)}) %collective-permute-start.1) | collective-permute-done | bytes 86048 | tf_op jit(solution)/shard_map/ppermute | solution.py:234
  6.6 0.0 collective-permute-start.2
  6.6 0.0 copy-start.6
  6.6 0.0 copy-start.7
  6.7 0.0 copy-start.8
  6.7 0.0 copy-start.3
  6.7 0.0 copy-start.4
  6.7 0.0 copy-start.5
  6.7 0.0 copy-start.1
  6.7 0.0 copy-start.2
  6.7 0.0 copy-start.9
  6.7 1.2 %collective-permute-done.2.refs_3_ = bf16[192,224]{1,0:T(8,128)(2,1)S(1)} collective-permute-done((bf16[192,224]{1,0:T(8,128)(2,1)S(1)}, bf16[192,224]{1,0:T(8,128)(2,1)S(1)}, u32[]{:S(2)}, u32[]{:S(2)}) %collective-permute-start.2) | collective-permute-done | bytes 86048 | tf_op jit(solution)/shard_map/ppermute | solution.py:231
  7.9 0.0 collective-permute-done.3.refs_8_.refs_3_
  7.9 0.0 copy-done
  7.9 0.0 copy-done.7
  7.9 0.0 copy-done.8
  8.0 0.7 %shard_map.120 = (f32[112,768]{1,0:T(8,128)S(1)}, bf16[224,768]{1,0:T(8,128)(2,1)S(1)}, bf16[224,256]{1,0:T(8,128)(2,1)S(1)}) custom-call(bf16[192,224]{1,0:T(8,128)(2,1)S(1)} %bitcast.9, bf16[192,224]{1,0:T(8,128)(2,1)S(1)} %collective-permute-done.block.refs_1_, bf16[192,224]{1,0:T(8,128)(2,1)S(1)} %collective-permute-done.1.refs_2_, ...), custom_call_target="tpu_custom_call" | custom-call | flops 100000000 | tf_op jit(solution)/shard_map/pallas_call | solution.py:244
  8.7 2.9 %collective-permute-start.8 = (bf16[224,256]{1,0:T(8,128)(2,1)S(1)}, bf16[224,256]{1,0:T(8,128)(2,1)S(1)}, u32[]{:S(2)}, u32[]{:S(2)}) collective-permute-start(bf16[224,256]{1,0:T(8,128)(2,1)S(1)} %get-tuple-element.24), channel_id=1, source_target_pairs={{8,0},{12,4},{0,8},{4,12},{9,1},{13,5},{1,9},{5,13},{10,2},{14,6},... | collective-permute-start | bytes 344072 | tf_op jit(solution)/shard_map/ppermute | solution.py:286
  11.6 1.6 %collective-permute-start.9 = (bf16[224,256]{1,0:T(8,128)(2,1)S(1)}, bf16[224,256]{1,0:T(8,128)(2,1)S(1)}, u32[]{:S(2)}, u32[]{:S(2)}) collective-permute-start(bf16[224,256]{1,0:T(8,128)(2,1)S(1)} %get-tuple-element.24), channel_id=1, source_target_pairs={{4,0},{0,4},{12,8},{8,12},{5,1},{1,5},{13,9},{9,13},{6,2},{2,6},{1... | collective-permute-start | bytes 344072 | tf_op jit(solution)/shard_map/ppermute | solution.py:286
  13.2 0.0 collective-permute-done.5.refs_4_
  13.2 0.0 collective-permute-start.10
  13.2 0.0 collective-permute-done.6.refs_6_
  13.2 0.0 collective-permute-done.4.refs_2_
  13.3 1.7 %shard_map.121 = (bf16[112,768]{1,0:T(8,128)(2,1)S(1)}, bf16[2,128,768]{2,1,0:T(8,128)(2,1)S(1)}) custom-call(bf16[224,768]{1,0:T(8,128)(2,1)S(1)} %get-tuple-element.21.refs_0_, bf16[3,768,128]{2,1,0:T(8,128)(2,1)S(1)} %copy-done.3, bf16[3,768,128]{2,1,0:T(8,128)(2,1)S(1)} %collective-permute-done.4.refs_2_, bf16[128,768]{1,0:T(8,128)(2,1)S(1)} %copy-done.4, ...), custom_call_target="tpu_custom_call" | custom-call | flops 100000000 | tf_op jit(solution)/shard_map/pallas_call | solution.py:244
  14.9 2.1 %collective-permute-start.7 = (bf16[112,768]{1,0:T(8,128)(2,1)S(1)}, bf16[112,768]{1,0:T(8,128)(2,1)S(1)}, u32[]{:S(2)}, u32[]{:S(2)}) collective-permute-start(bf16[112,768]{1,0:T(8,128)(2,1)S(1)} %get-tuple-element.22.refs_4_), channel_id=1, source_target_pairs={{0,2},{1,3},{2,0},{3,1},{4,6},{5,7},{6,4},{7,5},{8,10},{9,11},{10,... | collective-permute-start | bytes 516104 | tf_op jit(solution)/shard_map/ppermute | solution.py:234
  17.1 1.0 %collective-permute-done.8.refs_1_ = bf16[224,256]{1,0:T(8,128)(2,1)S(1)} collective-permute-done((bf16[224,256]{1,0:T(8,128)(2,1)S(1)}, bf16[224,256]{1,0:T(8,128)(2,1)S(1)}, u32[]{:S(2)}, u32[]{:S(2)}) %collective-permute-start.8) | collective-permute-done | bytes 114720 | tf_op jit(solution)/shard_map/ppermute | solution.py:286
  18.1 0.0 collective-permute-start.11
  18.1 0.0 collective-permute-done.9.refs_2_
  18.1 0.5 %collective-permute-start.12 = (bf16[224,256]{1,0:T(8,128)(2,1)S(1)}, bf16[224,256]{1,0:T(8,128)(2,1)S(1)}, u32[]{:S(2)}, u32[]{:S(2)}) collective-permute-start(bf16[224,256]{1,0:T(8,128)(2,1)S(1)} %collective-permute-done.9.refs_2_), channel_id=1, source_target_pairs={{0,1},{1,0},{2,3},{3,2},{4,5},{5,4},{6,7},{7,6},{8,9},{9,8},{10,11... | collective-permute-start | bytes 344072 | tf_op jit(solution)/shard_map/ppermute | solution.py:231
  18.6 2.7 %collective-permute-done.10.refs_3_ = bf16[224,256]{1,0:T(8,128)(2,1)S(1)} collective-permute-done((bf16[224,256]{1,0:T(8,128)(2,1)S(1)}, bf16[224,256]{1,0:T(8,128)(2,1)S(1)}, u32[]{:S(2)}, u32[]{:S(2)}) %collective-permute-start.10) | collective-permute-done | bytes 114720 | tf_op jit(solution)/shard_map/ppermute | solution.py:286
  21.3 0.0 collective-permute-start.13
  21.3 0.0 collective-permute-done.7.refs_5_
  21.3 0.0 copy-done.1
  21.3 0.9 %shard_map.122 = (f32[112,768]{1,0:T(8,128)S(1)}, bf16[112,256]{1,0:T(8,128)(2,1)S(1)}, bf16[2,768,768]{2,1,0:T(8,128)(2,1)S(1)}) custom-call(f32[112,768]{1,0:T(8,128)S(1)} %get-tuple-element.20.refs_0_, f32[768]{0:T(1024)S(1)} %copy-done.9, bf16[3,768,128]{2,1,0:T(8,128)(2,1)S(1)} %copy-done, ...), custom_call_target="tpu_custom_call" | custom-call | flops 100000000 | tf_op jit(solution)/shard_map/pallas_call | solution.py:244
  22.3 0.0 copy-start.10
  22.3 0.0 copy-start.11
  22.3 0.0 collective-permute-done.11.refs_4_
  22.3 0.0 collective-permute-done.12.refs_5_
  22.3 0.3 collective-permute-done.13.refs_6_
  22.6 0.8 %shard_map.123 = (bf16[2,768,768]{2,1,0:T(8,128)(2,1)S(1)}, bf16[2,128,768]{2,1,0:T(8,128)(2,1)S(1)}, bf16[2,112,256]{2,1,0:T(8,128)(2,1)S(1)}) custom-call(bf16[112,256]{1,0:T(8,128)(2,1)S(1)} %get-tuple-element.23.refs_0_, bf16[224,256]{1,0:T(8,128)(2,1)S(1)} %collective-permute-done.8.refs_1_, ...), custom_call_target="tpu_custom_call", output_to_operand_aliasing={{0}: (7, {}), {1}: (8, {})} | custom-call | flops 100000000 | tf_op jit(solution)/shard_map/pallas_call | solution.py:244
  23.5 0.3 collective-permute-start.17
  23.8 0.3 collective-permute-start.16
  24.1 1.8 %collective-permute-start.14 = (bf16[2,112,256]{2,1,0:T(8,128)(2,1)S(1)}, bf16[2,112,256]{2,1,0:T(8,128)(2,1)S(1)}, u32[]{:S(2)}, u32[]{:S(2)}) collective-permute-start(bf16[2,112,256]{2,1,0:T(8,128)(2,1)S(1)} %get-tuple-element.27.refs_1_), channel_id=1, source_target_pairs={{0,2},{1,3},{2,0},{3,1},{4,6},{5,7},{6,4},{7,5},{8,10},{9,11},{10,... | collective-permute-start | bytes 344072 | tf_op jit(solution)/shard_map/ppermute | solution.py:234
  25.9 0.5 %shard_map.124.refs_3_ = bf16[1,112,256]{2,1,0:T(8,128)(2,1)S(1)} custom-call(bf16[112,256]{1,0:T(8,128)(2,1)S(1)} %get-tuple-element.23.refs_0_, bf16[224,256]{1,0:T(8,128)(2,1)S(1)} %collective-permute-done.8.refs_1_, bf16[224,256]{1,0:T(8,128)(2,1)S(1)} %collective-permute-done.9.refs_2_, bf16[224,256]{1,0:T(8,128)(2,1)S(1)} %collective-permute-done.10.refs_3_, ...), custom_call_target="tpu_custom_call" | custom-call | flops 100000000 | tf_op jit(solution)/shard_map/pallas_call | solution.py:244
  26.4 0.2 collective-permute-start.15
  26.7 4.0 %collective-permute-done.15.refs_4_ = bf16[1,112,256]{2,1,0:T(8,128)(2,1)S(1)} collective-permute-done((bf16[1,112,256]{2,1,0:T(8,128)(2,1)S(1)}, bf16[1,112,256]{2,1,0:T(8,128)(2,1)S(1)}, u32[]{:S(2)}, u32[]{:S(2)}) %collective-permute-start.15) | collective-permute-done | bytes 57376 | tf_op jit(solution)/shard_map/ppermute | solution.py:234
  30.7 0.0 collective-permute-done.14.refs_2_
  30.7 0.0 collective-permute-done.16.refs_6_
  30.7 0.0 collective-permute-done.17.refs_10_
  30.7 3.0 %shard_map.125 = (f32[192,112]{1,0:T(8,128)S(1)}, f32[192,112]{1,0:T(8,128)S(1)}, bf16[192,112]{1,0:T(8,128)(2,1)S(1)}, bf16[192,112]{1,0:T(8,128)(2,1)S(1)}) custom-call(s32[2,4]{1,0:T(2,128)S(1)} %bitcast.10, bf16[2,112,256]{2,1,0:T(8,128)(2,1)S(1)} %get-tuple-element.27.refs_1_, bf16[2,112,256]{2,1,0:T(8,128)(2,1)S(1)} %collective-permute-done.14.refs_2_, ...), custom_call_target="tpu_custom_call" | custom-call | flops 3000000000 | tf_op jit(solution)/shard_map/pallas_call | solution.py:244
  33.7 0.1 collective-permute-start.18
  33.8 1.8 %collective-permute-start.19 = (bf16[192,112]{1,0:T(8,128)(2,1)S(1)}, bf16[192,112]{1,0:T(8,128)(2,1)S(1)}, u32[]{:S(2)}, u32[]{:S(2)}) collective-permute-start(bf16[192,112]{1,0:T(8,128)(2,1)S(1)} %get-tuple-element.33), channel_id=1, source_target_pairs={{0,2},{1,3},{2,0},{3,1},{4,6},{5,7},{6,4},{7,5},{8,10},{9,11},{10,... | collective-permute-start | bytes 129032 | tf_op jit(solution)/shard_map/ppermute | solution.py:234
  35.6 0.1 collective-permute-start.20
  35.7 2.3 %collective-permute-done.19.refs_2_ = bf16[192,112]{1,0:T(8,128)(2,1)S(1)} collective-permute-done((bf16[192,112]{1,0:T(8,128)(2,1)S(1)}, bf16[192,112]{1,0:T(8,128)(2,1)S(1)}, u32[]{:S(2)}, u32[]{:S(2)}) %collective-permute-start.19) | collective-permute-done | bytes 43040 | tf_op jit(solution)/shard_map/ppermute | solution.py:234
  38.0 1.3 %collective-permute-done.20.refs_3_ = bf16[192,112]{1,0:T(8,128)(2,1)S(1)} collective-permute-done((bf16[192,112]{1,0:T(8,128)(2,1)S(1)}, bf16[192,112]{1,0:T(8,128)(2,1)S(1)}, u32[]{:S(2)}, u32[]{:S(2)}) %collective-permute-start.20) | collective-permute-done | bytes 43040 | tf_op jit(solution)/shard_map/ppermute | solution.py:234
  39.3 0.0 collective-permute-done.18.refs_1_
  39.3 0.8 %shard_map.126 = f32[192,224]{1,0:T(8,128)} custom-call(f32[192,112]{1,0:T(8,128)S(1)} %get-tuple-element.31.refs_0_, f32[192,112]{1,0:T(8,128)S(1)} %collective-permute-done.18.refs_1_, bf16[192,112]{1,0:T(8,128)(2,1)S(1)} %collective-permute-done.19.refs_2_, bf16[192,112]{1,0:T(8,128)(2,1)S(1)} %collective-permute-done.20.refs_3_), custom_call_target="tpu_custom_call" | custom-call | tf_op jit(solution)/shard_map/pallas_call | solution.py:244
  (11 shorter events, 0.0 us)
Async XLA Ops:
  0.0 3.7 %collective-permute-start = (bf16[192,224]{1,0:T(8,128)(2,1)}, bf16[192,224]{1,0:T(8,128)(2,1)S(1)}, u32[]{:S(2)}, u32[]{:S(2)}) collective-permute-start(bf16[192,224]{1,0:T(8,128)(2,1)} %bitcast.7), channel_id=1, source_target_pairs={{0,1},{1,0},{2,3},{3,2},{4,5},{5,4},{6,7},{7,6},{8,9},{9,8},{10,11... | collective-permute-start | bytes 258056 | tf_op jit(solution)/shard_map/ppermute | solution.py:231
  0.5 6.2 %collective-permute-start.1 = (bf16[192,224]{1,0:T(8,128)(2,1)}, bf16[192,224]{1,0:T(8,128)(2,1)S(1)}, u32[]{:S(2)}, u32[]{:S(2)}) collective-permute-start(bf16[192,224]{1,0:T(8,128)(2,1)} %bitcast.8), channel_id=1, source_target_pairs={{0,2},{1,3},{2,0},{3,1},{4,6},{5,7},{6,4},{7,5},{8,10},{9,11},{10,... | collective-permute-start | bytes 258056 | tf_op jit(solution)/shard_map/ppermute | solution.py:234
  2.9 5.0 %collective-permute-start.3 = (bf16[3,768,128]{2,1,0:T(8,128)(2,1)}, bf16[3,768,128]{2,1,0:T(8,128)(2,1)S(1)}, u32[]{:S(2)}, u32[]{:S(2)}) collective-permute-start(bf16[3,768,128]{2,1,0:T(8,128)(2,1)} %refs_2_.1), channel_id=1, source_target_pairs={{0,1},{1,0},{2,3},{3,2},{4,5},{5,4},{6,7},{7,6},{8,9},{9,8},{10,11... | collective-permute-start | bytes 1769480 | tf_op jit(solution)/shard_map/ppermute | solution.py:231
  3.2 10.0 %collective-permute-start.4 = (bf16[3,768,128]{2,1,0:T(8,128)(2,1)}, bf16[3,768,128]{2,1,0:T(8,128)(2,1)S(1)}, u32[]{:S(2)}, u32[]{:S(2)}) collective-permute-start(bf16[3,768,128]{2,1,0:T(8,128)(2,1)} %refs_1_.2), channel_id=1, source_target_pairs={{0,1},{1,0},{2,3},{3,2},{4,5},{5,4},{6,7},{7,6},{8,9},{9,8},{10,11... | collective-permute-start | bytes 1769480 | tf_op jit(solution)/shard_map/ppermute | solution.py:231
  3.5 9.8 %collective-permute-start.5 = (bf16[128,768]{1,0:T(8,128)(2,1)}, bf16[128,768]{1,0:T(8,128)(2,1)S(1)}, u32[]{:S(2)}, u32[]{:S(2)}) collective-permute-start(bf16[128,768]{1,0:T(8,128)(2,1)} %refs_3_.1), channel_id=1, source_target_pairs={{0,1},{1,0},{2,3},{3,2},{4,5},{5,4},{6,7},{7,6},{8,9},{9,8},{10,11... | collective-permute-start | bytes 589832 | tf_op jit(solution)/shard_map/ppermute | solution.py:231
  3.7 9.5 %collective-permute-start.6 = (bf16[128,768]{1,0:T(8,128)(2,1)}, bf16[128,768]{1,0:T(8,128)(2,1)S(1)}, u32[]{:S(2)}, u32[]{:S(2)}) collective-permute-start(bf16[128,768]{1,0:T(8,128)(2,1)} %refs_5_.3), channel_id=1, source_target_pairs={{0,2},{1,3},{2,0},{3,1},{4,6},{5,7},{6,4},{7,5},{8,10},{9,11},{10,... | collective-permute-start | bytes 589832 | tf_op jit(solution)/shard_map/ppermute | solution.py:234
  6.6 1.3 %collective-permute-start.2 = (bf16[192,224]{1,0:T(8,128)(2,1)S(1)}, bf16[192,224]{1,0:T(8,128)(2,1)S(1)}, u32[]{:S(2)}, u32[]{:S(2)}) collective-permute-start(bf16[192,224]{1,0:T(8,128)(2,1)S(1)} %collective-permute-done.1.refs_2_), channel_id=1, source_target_pairs={{0,1},{1,0},{2,3},{3,2},{4,5},{5,4},{6,7},{7,6},{8,9},{9,8},{10,11... | collective-permute-start | bytes 258056 | tf_op jit(solution)/shard_map/ppermute | solution.py:231
  6.6 1.3 %copy-start = (bf16[3,768,128]{2,1,0:T(8,128)(2,1)S(1)}, bf16[3,768,128]{2,1,0:T(8,128)(2,1)}, u32[]{:S(2)}) copy-start(bf16[3,768,128]{2,1,0:T(8,128)(2,1)} %refs_2_.1) | copy-start | bytes 1769476
  6.6 1.3 %copy-start.6 = (bf16[1,224,192]{1,2,0:T(8,128)(2,1)S(1)}, bf16[1,224,192]{1,2,0:T(8,128)(2,1)}, u32[]{:S(2)}) copy-start(bf16[1,224,192]{1,2,0:T(8,128)(2,1)} %param.12) | copy-start | bytes 258052
  6.6 1.3 %copy-start.7 = (f32[768]{0:T(1024)S(1)}, f32[768]{0:T(1024)}, u32[]{:S(2)}) copy-start(f32[768]{0:T(1024)} %refs_4_.1) | copy-start | bytes 9220
  6.7 1.3 %copy-start.8 = (f32[768]{0:T(1024)S(1)}, f32[768]{0:T(1024)}, u32[]{:S(2)}) copy-start(f32[768]{0:T(1024)} %refs_5_.2) | copy-start | bytes 9220
  6.7 6.6 %copy-start.3 = (bf16[3,768,128]{2,1,0:T(8,128)(2,1)S(1)}, bf16[3,768,128]{2,1,0:T(8,128)(2,1)}, u32[]{:S(2)}) copy-start(bf16[3,768,128]{2,1,0:T(8,128)(2,1)} %refs_1_.2) | copy-start | bytes 1769476
  6.7 6.6 %copy-start.4 = (bf16[128,768]{1,0:T(8,128)(2,1)S(1)}, bf16[128,768]{1,0:T(8,128)(2,1)}, u32[]{:S(2)}) copy-start(bf16[128,768]{1,0:T(8,128)(2,1)} %refs_3_.1) | copy-start | bytes 589828
  6.7 6.6 %copy-start.5 = (bf16[128,768]{1,0:T(8,128)(2,1)S(1)}, bf16[128,768]{1,0:T(8,128)(2,1)}, u32[]{:S(2)}) copy-start(bf16[128,768]{1,0:T(8,128)(2,1)} %refs_5_.3) | copy-start | bytes 589828
  6.7 14.6 %copy-start.1 = (bf16[768,768]{1,0:T(8,128)(2,1)S(1)}, bf16[768,768]{1,0:T(8,128)(2,1)}, u32[]{:S(2)}) copy-start(bf16[768,768]{1,0:T(8,128)(2,1)} %refs_6_.3) | copy-start | bytes 3538948
  6.7 14.6 %copy-start.2 = (bf16[768,768]{1,0:T(8,128)(2,1)S(1)}, bf16[768,768]{1,0:T(8,128)(2,1)}, u32[]{:S(2)}) copy-start(bf16[768,768]{1,0:T(8,128)(2,1)} %refs_7_.1) | copy-start | bytes 3538948
  6.7 14.6 %copy-start.9 = (f32[768]{0:T(1024)S(1)}, f32[768]{0:T(1024)}, u32[]{:S(2)}) copy-start(f32[768]{0:T(1024)} %refs_1_.3) | copy-start | bytes 9220
  8.7 9.4 %collective-permute-start.8 = (bf16[224,256]{1,0:T(8,128)(2,1)S(1)}, bf16[224,256]{1,0:T(8,128)(2,1)S(1)}, u32[]{:S(2)}, u32[]{:S(2)}) collective-permute-start(bf16[224,256]{1,0:T(8,128)(2,1)S(1)} %get-tuple-element.24), channel_id=1, source_target_pairs={{8,0},{12,4},{0,8},{4,12},{9,1},{13,5},{1,9},{5,13},{10,2},{14,6},... | collective-permute-start | bytes 344072 | tf_op jit(solution)/shard_map/ppermute | solution.py:286
  11.6 6.4 %collective-permute-start.9 = (bf16[224,256]{1,0:T(8,128)(2,1)S(1)}, bf16[224,256]{1,0:T(8,128)(2,1)S(1)}, u32[]{:S(2)}, u32[]{:S(2)}) collective-permute-start(bf16[224,256]{1,0:T(8,128)(2,1)S(1)} %get-tuple-element.24), channel_id=1, source_target_pairs={{4,0},{0,4},{12,8},{8,12},{5,1},{1,5},{13,9},{9,13},{6,2},{2,6},{1... | collective-permute-start | bytes 344072 | tf_op jit(solution)/shard_map/ppermute | solution.py:286
  13.2 8.1 %collective-permute-start.10 = (bf16[224,256]{1,0:T(8,128)(2,1)S(1)}, bf16[224,256]{1,0:T(8,128)(2,1)S(1)}, u32[]{:S(2)}, u32[]{:S(2)}) collective-permute-start(bf16[224,256]{1,0:T(8,128)(2,1)S(1)} %get-tuple-element.24), channel_id=1, source_target_pairs={{12,0},{8,4},{4,8},{0,12},{13,1},{9,5},{5,9},{1,13},{14,2},{10,6},... | collective-permute-start | bytes 344072 | tf_op jit(solution)/shard_map/ppermute | solution.py:286
  14.9 6.4 %collective-permute-start.7 = (bf16[112,768]{1,0:T(8,128)(2,1)S(1)}, bf16[112,768]{1,0:T(8,128)(2,1)S(1)}, u32[]{:S(2)}, u32[]{:S(2)}) collective-permute-start(bf16[112,768]{1,0:T(8,128)(2,1)S(1)} %get-tuple-element.22.refs_4_), channel_id=1, source_target_pairs={{0,2},{1,3},{2,0},{3,1},{4,6},{5,7},{6,4},{7,5},{8,10},{9,11},{10,... | collective-permute-start | bytes 516104 | tf_op jit(solution)/shard_map/ppermute | solution.py:234
  18.1 4.3 %collective-permute-start.11 = (bf16[224,256]{1,0:T(8,128)(2,1)S(1)}, bf16[224,256]{1,0:T(8,128)(2,1)S(1)}, u32[]{:S(2)}, u32[]{:S(2)}) collective-permute-start(bf16[224,256]{1,0:T(8,128)(2,1)S(1)} %collective-permute-done.8.refs_1_), channel_id=1, source_target_pairs={{0,1},{1,0},{2,3},{3,2},{4,5},{5,4},{6,7},{7,6},{8,9},{9,8},{10,11... | collective-permute-start | bytes 344072 | tf_op jit(solution)/shard_map/ppermute | solution.py:231
  18.1 4.3 %collective-permute-start.12 = (bf16[224,256]{1,0:T(8,128)(2,1)S(1)}, bf16[224,256]{1,0:T(8,128)(2,1)S(1)}, u32[]{:S(2)}, u32[]{:S(2)}) collective-permute-start(bf16[224,256]{1,0:T(8,128)(2,1)S(1)} %collective-permute-done.9.refs_2_), channel_id=1, source_target_pairs={{0,1},{1,0},{2,3},{3,2},{4,5},{5,4},{6,7},{7,6},{8,9},{9,8},{10,11... | collective-permute-start | bytes 344072 | tf_op jit(solution)/shard_map/ppermute | solution.py:231
  21.3 1.3 %collective-permute-start.13 = (bf16[224,256]{1,0:T(8,128)(2,1)S(1)}, bf16[224,256]{1,0:T(8,128)(2,1)S(1)}, u32[]{:S(2)}, u32[]{:S(2)}) collective-permute-start(bf16[224,256]{1,0:T(8,128)(2,1)S(1)} %collective-permute-done.10.refs_3_), channel_id=1, source_target_pairs={{0,1},{1,0},{2,3},{3,2},{4,5},{5,4},{6,7},{7,6},{8,9},{9,8},{10,11... | collective-permute-start | bytes 344072 | tf_op jit(solution)/shard_map/ppermute | solution.py:231
  22.3 8.4 %copy-start.10 = (f32[768]{0:T(1024)S(1)}, f32[768]{0:T(1024)}, u32[]{:S(2)}) copy-start(f32[768]{0:T(1024)} %refs_8_.1) | copy-start | bytes 9220
  22.3 8.4 %copy-start.11 = (s32[4,2]{0,1:T(2,128)S(1)}, s32[4,2]{0,1:T(2,128)}, u32[]{:S(2)}) copy-start(s32[4,2]{0,1:T(2,128)} %param.13) | copy-start | bytes 100
  23.5 7.2 %collective-permute-start.17 = (bf16[2,768,768]{2,1,0:T(8,128)(2,1)S(1)}, bf16[2,768,768]{2,1,0:T(8,128)(2,1)S(1)}, u32[]{:S(2)}, u32[]{:S(2)}) collective-permute-start(bf16[2,768,768]{2,1,0:T(8,128)(2,1)S(1)} %get-tuple-element.30.refs_9_), channel_id=1, source_target_pairs={{0,1},{1,0},{2,3},{3,2},{4,5},{5,4},{6,7},{7,6},{8,9},{9,8},{10,11... | collective-permute-start | bytes 7077896 | tf_op jit(solution)/shard_map/ppermute | solution.py:231
  23.8 6.9 %collective-permute-start.16 = (bf16[2,128,768]{2,1,0:T(8,128)(2,1)S(1)}, bf16[2,128,768]{2,1,0:T(8,128)(2,1)S(1)}, u32[]{:S(2)}, u32[]{:S(2)}) collective-permute-start(bf16[2,128,768]{2,1,0:T(8,128)(2,1)S(1)} %get-tuple-element.28.refs_5_), channel_id=1, source_target_pairs={{0,1},{1,0},{2,3},{3,2},{4,5},{5,4},{6,7},{7,6},{8,9},{9,8},{10,11... | collective-permute-start | bytes 1179656 | tf_op jit(solution)/shard_map/ppermute | solution.py:231
  24.1 6.6 %collective-permute-start.14 = (bf16[2,112,256]{2,1,0:T(8,128)(2,1)S(1)}, bf16[2,112,256]{2,1,0:T(8,128)(2,1)S(1)}, u32[]{:S(2)}, u32[]{:S(2)}) collective-permute-start(bf16[2,112,256]{2,1,0:T(8,128)(2,1)S(1)} %get-tuple-element.27.refs_1_), channel_id=1, source_target_pairs={{0,2},{1,3},{2,0},{3,1},{4,6},{5,7},{6,4},{7,5},{8,10},{9,11},{10,... | collective-permute-start | bytes 344072 | tf_op jit(solution)/shard_map/ppermute | solution.py:234
  26.4 4.2 %collective-permute-start.15 = (bf16[1,112,256]{2,1,0:T(8,128)(2,1)S(1)}, bf16[1,112,256]{2,1,0:T(8,128)(2,1)S(1)}, u32[]{:S(2)}, u32[]{:S(2)}) collective-permute-start(bf16[1,112,256]{2,1,0:T(8,128)(2,1)S(1)} %shard_map.124.refs_3_), channel_id=1, source_target_pairs={{0,2},{1,3},{2,0},{3,1},{4,6},{5,7},{6,4},{7,5},{8,10},{9,11},{10,... | collective-permute-start | bytes 172040 | tf_op jit(solution)/shard_map/ppermute | solution.py:234
  33.7 5.6 %collective-permute-start.18 = (f32[192,112]{1,0:T(8,128)S(1)}, f32[192,112]{1,0:T(8,128)S(1)}, u32[]{:S(2)}, u32[]{:S(2)}) collective-permute-start(f32[192,112]{1,0:T(8,128)S(1)} %get-tuple-element.32), channel_id=1, source_target_pairs={{0,1},{1,0},{2,3},{3,2},{4,5},{5,4},{6,7},{7,6},{8,9},{9,8},{10,11... | collective-permute-start | bytes 258056 | tf_op jit(solution)/shard_map/ppermute | solution.py:231
  33.8 4.2 %collective-permute-start.19 = (bf16[192,112]{1,0:T(8,128)(2,1)S(1)}, bf16[192,112]{1,0:T(8,128)(2,1)S(1)}, u32[]{:S(2)}, u32[]{:S(2)}) collective-permute-start(bf16[192,112]{1,0:T(8,128)(2,1)S(1)} %get-tuple-element.33), channel_id=1, source_target_pairs={{0,2},{1,3},{2,0},{3,1},{4,6},{5,7},{6,4},{7,5},{8,10},{9,11},{10,... | collective-permute-start | bytes 129032 | tf_op jit(solution)/shard_map/ppermute | solution.py:234
  35.6 3.7 %collective-permute-start.20 = (bf16[192,112]{1,0:T(8,128)(2,1)S(1)}, bf16[192,112]{1,0:T(8,128)(2,1)S(1)}, u32[]{:S(2)}, u32[]{:S(2)}) collective-permute-start(bf16[192,112]{1,0:T(8,128)(2,1)S(1)} %get-tuple-element.34), channel_id=1, source_target_pairs={{0,3},{1,2},{2,1},{3,0},{4,7},{5,6},{6,5},{7,4},{8,11},{9,10},{10,... | collective-permute-start | bytes 129032 | tf_op jit(solution)/shard_map/ppermute | solution.py:234
